TPU v7x, 128 devices: a whole 4x4x4 slice. The times are simulated.
128 devices in a mesh: group: 4 (over z), dev: 32 (over x, y, core).
Axes of the slice: x: 4, y: 4, z: 4, core: 2. Of those that a mesh axis runs over, the one named last changes fastest.
Arguments:
- charges: bfloat16 [524288, 128], P(('group', 'dev')), may hold values from -6 to 6
- panel_coords: bfloat16 [2048, 3, 256], P(('group', 'dev')), may hold values from 0 to 1
- cluster_basis: bfloat16 [2048, 32, 256], P(('group', 'dev')), may hold values from -0.75 to 0.75
- trans_leaf: bfloat16 [2048, 32, 32], P(('group', 'dev')), may hold values from -0.75 to 0.75
- trans_pair: bfloat16 [128, 32, 32], P(('group', 'dev')), may hold values from -0.75 to 0.75
- trans_quad: bfloat16 [128, 32, 32], P(('group', 'dev')), may hold values from -0.5 to 0.5
- skel_points: bfloat16 [128, 3, 32], P(('group', 'dev')), may hold values from 0 to 1
- send_slots: int32 [4096, 1], P(('group', 'dev')), may hold values from 0 to 15
- pair_first: int32 [32768], P(('group', 'dev')), may hold values from 0 to 15
- pair_second: int32 [32768], P(('group', 'dev')), may hold values from 0 to 47
- pair_count: int32 [128], P(('group', 'dev')), may hold values from 64 to 256, as said below
- far_one: int32 [128, 8], P(('group', 'dev')), may hold values from 0 to 127
- far_two: int32 [128, 8], P(('group', 'dev')), may hold values from 0 to 63
- far_three: int32 [128, 8], P(('group', 'dev')), may hold values from 0 to 31
Outputs:
- potential: float32 [524288, 128], P(('group', 'dev'))
Inputs may be any that keep to these rules, and one draw needn't show every extreme that they name: `send_slots`: row s * 32 + h holds local cluster indices of owner s sent to member h of its team; every slot is used. `pair_count`: some owner has all 256 pairs live.
All inputs are finite; a program needn't handle non-finite values.
Results may differ from a plain program's by a relative error of at most 0.0051.
Values may be sent and summed in bfloat16 or wider, within the bound.
A program may use at most 128 MiB of HBM per device.

v0:
```python
import jax
import jax.numpy as jnp
from jax import lax
from jax.sharding import PartitionSpec as P

KCOEF = 0.005
DELTA = 0.02
HIGH = lax.Precision.HIGHEST


def partner(shard, axis, stride):
    return lax.ppermute(shard, axis, [(i, i ^ 1 << stride) for i in range(lax.axis_size(axis))])


def coulomb(left, right):
    total = DELTA * DELTA
    for axis_id in range(3):
        source = left[..., axis_id, :].astype(jnp.float32)
        target = right[..., axis_id, :].astype(jnp.float32)
        gap = source[..., :, None] - target[..., None, :]
        total = total + gap * gap
    return KCOEF / jnp.sqrt(total)


def climb(pair_part, quad_part):
    other_pair, other_quad = partner((pair_part, quad_part), "dev", 0)
    quad_half = quad_part + other_quad
    other_half = partner(quad_half, "dev", 1)
    return (pair_part + other_pair, quad_half + other_half)


def spread(first_item, second_item, third_item, fourth_item):
    return (
        lax.all_gather(first_item, ("group", "dev"), axis=0, tiled=True),
        lax.all_gather(second_item, ("group", "dev"), axis=0, tiled=True),
        lax.all_gather(third_item, ("group", "dev"), axis=0, tiled=True),
        lax.all_gather(fourth_item, ("group", "dev"), axis=0, tiled=True),
    )


def level_far(own_points, all_points, skeleton, far_ids):
    tiles = coulomb(own_points[None], jnp.take(all_points, far_ids, axis=0))
    sources = jnp.take(skeleton, far_ids, axis=0).astype(jnp.float32)
    return jnp.einsum("fab,fbr->ar", tiles, sources, precision=HIGH)


def shards(
    charges,
    panel_coords,
    cluster_basis,
    trans_leaf,
    trans_pair,
    trans_quad,
    skel_points,
    send_slots,
    pair_first,
    pair_second,
    pair_count,
    far_one,
    far_two,
    far_three,
):
    clusters = panel_coords.shape[0]
    width = panel_coords.shape[2]
    conductors = charges.shape[1]
    peers = lax.axis_size("dev")
    capacity = send_slots.shape[1]
    blocks = charges.reshape(clusters, width, conductors)
    flat_slots = send_slots.reshape(-1)
    outgoing = jnp.take(blocks, flat_slots, axis=0).reshape(peers, capacity, width, conductors)
    outgoing_xyz = jnp.take(panel_coords, flat_slots, axis=0).reshape(peers, capacity, 3, width)
    incoming, incoming_xyz = (
        lax.all_to_all(outgoing, "dev", split_axis=0, concat_axis=0, tiled=True),
        lax.all_to_all(outgoing_xyz, "dev", split_axis=0, concat_axis=0, tiled=True),
    )
    table = jnp.concatenate([blocks, incoming.reshape(peers * capacity, width, conductors)], axis=0)
    table_xyz = jnp.concatenate(
        [panel_coords, incoming_xyz.reshape(peers * capacity, 3, width)], axis=0
    )
    entries = table.shape[0]
    count = pair_count[0]
    firsts = pair_first.reshape(-1, 16)
    seconds = pair_second.reshape(-1, 16)
    orders = jnp.arange(pair_first.shape[0], dtype=jnp.int32).reshape(-1, 16)

    def near_step(accum, inputs):
        first, second, index = inputs
        tile = coulomb(
            jnp.take(table_xyz, first, axis=0), jnp.take(table_xyz, second, axis=0)
        ).astype(jnp.bfloat16)
        to_first = jnp.einsum(
            "pij,pjr->pir",
            tile,
            jnp.take(table, second, axis=0),
            preferred_element_type=jnp.float32,
        )
        to_second = jnp.einsum(
            "pij,pir->pjr", tile, jnp.take(table, first, axis=0), preferred_element_type=jnp.float32
        )
        live = (index < count).astype(jnp.float32)
        back = live * (first != second).astype(jnp.float32)
        accum = accum.at[first].add(to_first * live[:, None, None])
        accum = accum.at[second].add(to_second * back[:, None, None])
        return (accum, None)

    start = jnp.zeros((entries, width, conductors), jnp.float32)
    accum, _ = lax.scan(near_step, start, (firsts, seconds, orders))
    sent_back = accum[clusters:].astype(jnp.bfloat16).reshape(peers, capacity, width, conductors)
    returned = lax.all_to_all(sent_back, "dev", split_axis=0, concat_axis=0, tiled=True)
    select = (flat_slots[None, :] == jnp.arange(clusters, dtype=jnp.int32)[:, None]).astype(
        jnp.float32
    )
    gathered_back = returned.reshape(peers * capacity, width * conductors).astype(jnp.float32)
    near = accum[:clusters] + jnp.dot(select, gathered_back, precision=HIGH).reshape(
        clusters, width, conductors
    )
    leaf_skel = jnp.einsum(
        "cak,ckr->car", cluster_basis, blocks, preferred_element_type=jnp.float32
    ).astype(jnp.bfloat16)
    top_skel = jnp.einsum(
        "cab,cbr->ar", trans_leaf, leaf_skel, preferred_element_type=jnp.float32
    ).astype(jnp.bfloat16)[None]
    pair_part = jnp.dot(trans_pair[0], top_skel[0], preferred_element_type=jnp.float32)
    quad_part = jnp.dot(trans_quad[0], top_skel[0], preferred_element_type=jnp.float32)
    pair_sum, quad_sum = climb(pair_part, quad_part)
    all_top, pair_copies, quad_copies, all_points = spread(
        top_skel,
        pair_sum.astype(jnp.bfloat16)[None],
        quad_sum.astype(jnp.bfloat16)[None],
        skel_points,
    )
    pair_all = pair_copies[0::2]
    quad_all = quad_copies[0::4]
    owner = lax.axis_index("group") * peers + lax.axis_index("dev")
    points_one = all_points.astype(jnp.float32)
    points_two = 0.5 * (points_one[0::2] + points_one[1::2])
    points_three = 0.5 * (points_two[0::2] + points_two[1::2])
    far_top = level_far(jnp.take(points_one, owner, axis=0), points_one, all_top, far_one[0])
    far_pair = level_far(jnp.take(points_two, owner // 2, axis=0), points_two, pair_all, far_two[0])
    far_quad = level_far(
        jnp.take(points_three, owner // 4, axis=0), points_three, quad_all, far_three[0]
    )
    pair_down, quad_down = climb(far_pair, far_quad)
    down = far_top + jnp.dot(trans_pair[0].astype(jnp.float32).T, pair_down, precision=HIGH)
    down = down + jnp.dot(trans_quad[0].astype(jnp.float32).T, quad_down, precision=HIGH)
    leaf_down = jnp.einsum(
        "cba,br->car", trans_leaf.astype(jnp.float32), down, precision=HIGH
    ).astype(jnp.bfloat16)
    far_pot = jnp.einsum(
        "cak,car->ckr", cluster_basis, leaf_down, preferred_element_type=jnp.float32
    )
    return (near + far_pot).reshape(clusters * width, conductors)


def solution(mesh):
    placed = (
        P(("group", "dev"), None),
        P(("group", "dev"), None, None),
        P(("group", "dev"), None, None),
        P(("group", "dev"), None, None),
        P(("group", "dev"), None, None),
        P(("group", "dev"), None, None),
        P(("group", "dev"), None, None),
        P(("group", "dev"), None),
        P(("group", "dev")),
        P(("group", "dev")),
        P(("group", "dev")),
        P(("group", "dev"), None),
        P(("group", "dev"), None),
        P(("group", "dev"), None),
    )
    return jax.shard_map(
        shards, mesh=mesh, in_specs=placed, out_specs=P(("group", "dev"), None), check_vma=False
    )
```

profile of v0, /device:TPU:1, one launch (start us, length us, event | category | flops | bytes accessed | tf_op | source)
XLA Modules:
  0.0 709.6 jit_solution(17920991413581112477)
XLA Ops:
  10.2 8.6 %all-to-all-start = ((bf16[32,1,3,256]{3,2,1,0:T(4,128)(2,1)}), bf16[32,1,3,256]{3,2,1,0:T(4,128)(2,1)}, u32[]{:S(2)}, u32[]{:S(2)}) async-start(bf16[32,1,3,256]{3,2,1,0:T(4,128)(2,1)} %copy.26), calls=%async_computation | async-start | bytes 131072 | tf_op jit(solution)/shard_map/all_to_all | solution.py:74
  25.7 37.4 %all_gather.12 = bf16[128,3,32]{2,1,0:T(4,128)(2,1)S(1)} all-gather(bf16[1,3,32]{2,1,0:T(4,128)(2,1)S(1)} %copy-done.31), channel_id=1, replica_groups=mesh['group'=4,'dev'=32] {'group','dev'}, dimensions={0}, use_global_device_ids=true | all-gather | bytes 24768 | tf_op jit(solution)/shard_map/all_gather | solution.py:37
  85.5 12.2 %collective-permute-done.3 = f32[32,128]{1,0:T(8,128)S(1)} collective-permute-done((f32[32,128]{1,0:T(8,128)S(1)}, f32[32,128]{1,0:T(8,128)S(1)}, u32[]{:S(2)}, u32[]{:S(2)}) %collective-permute-start.3) | collective-permute-done | bytes 16416 | tf_op jit(solution)/shard_map/ppermute | solution.py:12
  110.6 547.1 %while.13 = (s32[]{:T(128)}, f32[48,256,128]{2,1,0:T(8,128)}, s32[16,16]{1,0:T(8,128)S(1)}, bf16[48,3,256]{2,1,0:T(4,128)(2,1)S(1)}, s32[16,16]{1,0:T(8,128)S(1)...) while((s32[]{:T(128)}, f32[48,256,128]{2,1,0:T(8,128)}, ...), condition=%wide.region_3.6_spmd, body=%wide.region_0.5_spmd.sunk | while | flops 563136896 | bytes 24176648 | solution.py:107
  122.7 5.1 convolution_multiply_fusion.4
  127.7 5.4 scatter_fusion
  139.2 5.6 scatter_fusion.1
  156.9 5.1 convolution_multiply_fusion.4
  162.0 5.4 scatter_fusion
  173.4 5.5 scatter_fusion.1
  191.1 5.1 convolution_multiply_fusion.4
  196.1 5.5 scatter_fusion
  207.7 5.7 scatter_fusion.1
  230.6 5.4 scatter_fusion
  242.0 5.6 scatter_fusion.1
  259.7 5.1 convolution_multiply_fusion.4
  264.8 5.4 scatter_fusion
  276.2 5.6 scatter_fusion.1
  293.9 5.1 convolution_multiply_fusion.4
  299.0 5.4 scatter_fusion
  310.5 5.6 scatter_fusion.1
  328.1 5.1 convolution_multiply_fusion.4
  333.2 5.4 scatter_fusion
  344.7 5.5 scatter_fusion.1
  367.4 5.4 scatter_fusion
  378.9 5.5 scatter_fusion.1
  401.5 5.5 scatter_fusion
  413.1 5.5 scatter_fusion.1
  435.7 5.3 scatter_fusion
  447.1 5.5 scatter_fusion.1
  464.7 5.1 convolution_multiply_fusion.4
  469.7 5.4 scatter_fusion
  481.2 5.5 scatter_fusion.1
  498.8 5.1 convolution_multiply_fusion.4
  503.8 5.3 scatter_fusion
  515.3 5.6 scatter_fusion.1
  532.9 5.1 convolution_multiply_fusion.4
  538.0 5.4 scatter_fusion
  549.5 5.6 scatter_fusion.1
  567.1 5.1 convolution_multiply_fusion.4
  572.2 5.5 scatter_fusion
  583.8 5.5 scatter_fusion.1
  606.5 5.3 scatter_fusion
  617.9 5.6 scatter_fusion.1
  640.6 5.5 scatter_fusion
  652.2 5.5 scatter_fusion.1
  661.5 6.9 all-to-all-start.2
  668.8 9.1 %copy.28 = f32[48,256,128]{2,0,1:T(8,128)} copy(f32[48,256,128]{2,1,0:T(8,128)} %get-tuple-element.49) | data formatting | bytes 12582912 | tf_op jit(solution)/shard_map/while | solution.py:107
  (852 shorter events, 394.6 us)
Async XLA Ops:
  6.5 12.4 %copy-start = (bf16[16,32,256]{2,1,0:T(8,128)(2,1)S(1)}, bf16[16,32,256]{2,1,0:T(8,128)(2,1)}, u32[]{:S(2)}) copy-start(bf16[16,32,256]{2,1,0:T(8,128)(2,1)} %param.22) | copy-start | bytes 786436
  6.5 17.6 %copy-start.1 = (bf16[4096,128]{1,0:T(8,128)(2,1)S(1)}, bf16[4096,128]{1,0:T(8,128)(2,1)}, u32[]{:S(2)}) copy-start(bf16[4096,128]{1,0:T(8,128)(2,1)} %param.20) | copy-start | bytes 3145732
  8.0 16.0 %copy-start.30 = (pred[32]{0:T(512)(128)(4,1)}, pred[32]{0:T(512)(128)(4,1)S(1)}, u32[]{:S(2)}) copy-start(pred[32]{0:T(512)(128)(4,1)S(1)} %and_bitcast_fusion) | copy-start | bytes 100
  9.4 15.6 %copy-start.49 = (s32[1,8]{1,0:T(1,128)S(1)}, s32[1,8]{1,0:T(1,128)}, u32[]{:S(2)}) copy-start(s32[1,8]{1,0:T(1,128)} %param.31) | copy-start | bytes 100
  9.5 16.2 %copy-start.31 = (bf16[1,3,32]{2,1,0:T(4,128)(2,1)S(1)}, bf16[1,3,32]{2,1,0:T(4,128)(2,1)}, u32[]{:S(2)}) copy-start(bf16[1,3,32]{2,1,0:T(4,128)(2,1)} %param.26) | copy-start | bytes 580
  10.2 59.1 %all-to-all-start = ((bf16[32,1,3,256]{3,2,1,0:T(4,128)(2,1)}), bf16[32,1,3,256]{3,2,1,0:T(4,128)(2,1)}, u32[]{:S(2)}, u32[]{:S(2)}) async-start(bf16[32,1,3,256]{3,2,1,0:T(4,128)(2,1)} %copy.26), calls=%async_computation | async-start | bytes 131072 | tf_op jit(solution)/shard_map/all_to_all | solution.py:74
  18.9 44.2 %copy-start.50 = (s32[1,8]{1,0:T(1,128)S(1)}, s32[1,8]{1,0:T(1,128)}, u32[]{:S(2)}) copy-start(s32[1,8]{1,0:T(1,128)} %param.32) | copy-start | bytes 100
  18.9 659.0 %all-gather.7.cloned.1.call-start = ((), (), s32[]{:S(2)}) async-start(), calls=%async_computation.3 | async-start | bytes 1056768 | tf_op jit(solution)/shard_map/all_gather | solution.py:34
  18.9 44.8 %copy-start.51 = (s32[1,8]{1,0:T(1,128)S(1)}, s32[1,8]{1,0:T(1,128)}, u32[]{:S(2)}) copy-start(s32[1,8]{1,0:T(1,128)} %param.33) | copy-start | bytes 100
  21.3 658.6 %all-gather.9.cloned.1.call-start = ((), (), s32[]{:S(2)}) async-start(), calls=%async_computation.4 | async-start | bytes 1056768 | tf_op jit(solution)/shard_map/all_gather | solution.py:35
  22.8 45.1 %collective-permute-start = (f32[32,128]{1,0:T(8,128)}, f32[32,128]{1,0:T(8,128)}, u32[]{:S(2)}, u32[]{:S(2)}) collective-permute-start(f32[32,128]{1,0:T(8,128)} %convolution_bitcast_fusion.1), channel_id=1, source_target_pairs={{0,1},{1,0},{2,3},{3,2},{4,5},{5,4},{6,7},{7,6},{8,9},{9,8},{10,11... | collective-permute-start | bytes 49160 | tf_op jit(solution)/shard_map/ppermute | solution.py:12
  23.9 56.4 %collective-permute-start.2 = (f32[32,128]{1,0:T(8,128)S(1)}, f32[32,128]{1,0:T(8,128)}, u32[]{:S(2)}, u32[]{:S(2)}) collective-permute-start(f32[32,128]{1,0:T(8,128)S(1)} %convolution_bitcast_fusion), channel_id=1, source_target_pairs={{0,1},{1,0},{2,3},{3,2},{4,5},{5,4},{6,7},{7,6},{8,9},{9,8},{10,11... | collective-permute-start | bytes 49160 | tf_op jit(solution)/shard_map/ppermute | solution.py:12
  67.8 10.6 %copy-start.35 = (pred[8]{0:T(512)(128)(4,1)S(1)}, pred[8]{0:T(512)(128)(4,1)}, u32[]{:S(2)}) copy-start(pred[8]{0:T(512)(128)(4,1)} %compare_and_fusion.4) | copy-start | bytes 28
  67.8 11.3 %copy-start.37 = (pred[8]{0:T(512)(128)(4,1)S(1)}, pred[8]{0:T(512)(128)(4,1)}, u32[]{:S(2)}) copy-start(pred[8]{0:T(512)(128)(4,1)} %compare_and_fusion.3) | copy-start | bytes 28
  67.8 14.7 %copy-start.39 = (s32[8]{0:T(128)S(1)}, s32[8]{0:T(128)}, u32[]{:S(2)}) copy-start(s32[8]{0:T(128)} %fusion.107) | copy-start | bytes 100
  67.8 14.7 %copy-start.2 = (bf16[16,3,256]{2,0,1:T(8,128)(2,1)S(1)}, bf16[16,3,256]{2,0,1:T(8,128)(2,1)}, u32[]{:S(2)}) copy-start(bf16[16,3,256]{2,0,1:T(8,128)(2,1)} %param.21) | copy-start | bytes 73732
  67.8 14.7 %copy-start.6 = (bf16[16,32,32]{2,1,0:T(8,128)(2,1)S(1)}, bf16[16,32,32]{2,1,0:T(8,128)(2,1)}, u32[]{:S(2)}) copy-start(bf16[16,32,32]{2,1,0:T(8,128)(2,1)} %param.23) | copy-start | bytes 98308
  67.8 15.5 %copy-start.32 = (s32[256]{0:T(256)S(1)}, s32[256]{0:T(256)}, u32[]{:S(2)}) copy-start(s32[256]{0:T(256)} %param.28) | copy-start | bytes 3076
  67.8 15.6 %copy-start.33 = (s32[256]{0:T(256)S(1)}, s32[256]{0:T(256)}, u32[]{:S(2)}) copy-start(s32[256]{0:T(256)} %param.29) | copy-start | bytes 3076
  69.3 8.5 %copy-start.22 = (s32[1024]{0:T(1024)}, s32[1024]{0:T(1024)S(1)}, u32[]{:S(2)}) copy-start(s32[1024]{0:T(1024)S(1)} %pad_clamp_fusion.3) | copy-start | bytes 12292
  69.3 34.3 %all-to-all-start.1 = ((bf16[32,1,256,128]{3,2,1,0:T(8,128)(2,1)}), bf16[32,1,256,128]{3,2,1,0:T(8,128)(2,1)S(1)}, u32[]{:S(2)}, u32[]{:S(2)}) async-start(bf16[32,1,256,128]{3,2,1,0:T(8,128)(2,1)} %bitcast_select_fusion), calls=%async_computation.1 | async-start | bytes 4194304 | tf_op jit(solution)/shard_map/all_to_all | solution.py:73
  74.3 608.2 %all-gather.11.cloned.1.call-start = ((), (), s32[]{:S(2)}) async-start(), calls=%async_computation.5 | async-start | bytes 1056768 | tf_op jit(solution)/shard_map/all_gather | solution.py:36
  81.1 16.5 %collective-permute-start.3 = (f32[32,128]{1,0:T(8,128)S(1)}, f32[32,128]{1,0:T(8,128)S(1)}, u32[]{:S(2)}, u32[]{:S(2)}) collective-permute-start(f32[32,128]{1,0:T(8,128)S(1)} %add.215), channel_id=1, source_target_pairs={{0,2},{1,3},{2,0},{3,1},{4,6},{5,7},{6,4},{7,5},{8,10},{9,11},{10,... | collective-permute-start | bytes 49160 | tf_op jit(solution)/shard_map/ppermute | solution.py:12
  82.5 21.2 %copy-start.23 = (s32[1024]{0:T(1024)}, s32[1024]{0:T(1024)S(1)}, u32[]{:S(2)}) copy-start(s32[1024]{0:T(1024)S(1)} %pad_clamp_fusion.2) | copy-start | bytes 12292
  661.5 35.3 %all-to-all-start.2 = ((bf16[32,1,256,128]{3,2,1,0:T(8,128)(2,1)}), bf16[32,1,256,128]{3,2,1,0:T(8,128)(2,1)}, u32[]{:S(2)}, u32[]{:S(2)}) async-start(bf16[32,1,256,128]{3,2,1,0:T(8,128)(2,1)} %fusion.15), calls=%async_computation.2 | async-start | bytes 4194304 | tf_op jit(solution)/shard_map/all_to_all | solution.py:109
  668.6 13.0 %copy-start.27 = (f32[8,1,32]{2,1,0:T(1,128)S(1)}, f32[8,1,32]{2,1,0:T(1,128)}, u32[]{:S(2)}) copy-start(f32[8,1,32]{2,1,0:T(1,128)} %get-tuple-element.126) | copy-start | bytes 3076
  668.6 13.0 %copy-start.28 = (f32[8,1,32]{2,1,0:T(1,128)S(1)}, f32[8,1,32]{2,1,0:T(1,128)}, u32[]{:S(2)}) copy-start(f32[8,1,32]{2,1,0:T(1,128)} %get-tuple-element.127) | copy-start | bytes 3076
  668.6 13.0 %copy-start.29 = (f32[8,1,32]{2,1,0:T(1,128)S(1)}, f32[8,1,32]{2,1,0:T(1,128)}, u32[]{:S(2)}) copy-start(f32[8,1,32]{2,1,0:T(1,128)} %get-tuple-element.128) | copy-start | bytes 3076
  668.6 13.0 %copy-start.38 = (pred[8]{0:T(512)(128)(4,1)S(1)}, pred[8]{0:T(512)(128)(4,1)}, u32[]{:S(2)}) copy-start(pred[8]{0:T(512)(128)(4,1)} %compare_and_fusion.3) | copy-start | bytes 28
  668.6 13.0 %copy-start.46 = (f32[32]{0:T(128)S(1)}, f32[32]{0:T(128)}, u32[]{:S(2)}) copy-start(f32[32]{0:T(128)} %get-tuple-element.135) | copy-start | bytes 388
  668.7 13.0 %copy-start.47 = (f32[32]{0:T(128)S(1)}, f32[32]{0:T(128)}, u32[]{:S(2)}) copy-start(f32[32]{0:T(128)} %get-tuple-element.136) | copy-start | bytes 388
  668.7 13.0 %copy-start.48 = (f32[32]{0:T(128)S(1)}, f32[32]{0:T(128)}, u32[]{:S(2)}) copy-start(f32[32]{0:T(128)} %get-tuple-element.137) | copy-start | bytes 388
  668.7 15.4 %copy-start.43 = (f32[32]{0:T(128)S(1)}, f32[32]{0:T(128)}, u32[]{:S(2)}) copy-start(f32[32]{0:T(128)} %get-tuple-element.132) | copy-start | bytes 388
  668.7 15.4 %copy-start.44 = (f32[32]{0:T(128)S(1)}, f32[32]{0:T(128)}, u32[]{:S(2)}) copy-start(f32[32]{0:T(128)} %get-tuple-element.133) | copy-start | bytes 388
  668.7 15.4 %copy-start.45 = (f32[32]{0:T(128)S(1)}, f32[32]{0:T(128)}, u32[]{:S(2)}) copy-start(f32[32]{0:T(128)} %get-tuple-element.134) | copy-start | bytes 388
  668.7 16.1 %copy-start.24 = (f32[8,1,32]{2,1,0:T(1,128)S(1)}, f32[8,1,32]{2,1,0:T(1,128)}, u32[]{:S(2)}) copy-start(f32[8,1,32]{2,1,0:T(1,128)} %get-tuple-element.129) | copy-start | bytes 3076
  668.7 16.0 %copy-start.25 = (f32[8,1,32]{2,1,0:T(1,128)S(1)}, f32[8,1,32]{2,1,0:T(1,128)}, u32[]{:S(2)}) copy-start(f32[8,1,32]{2,1,0:T(1,128)} %get-tuple-element.130) | copy-start | bytes 3076
  668.7 16.0 %copy-start.26 = (f32[8,1,32]{2,1,0:T(1,128)S(1)}, f32[8,1,32]{2,1,0:T(1,128)}, u32[]{:S(2)}) copy-start(f32[8,1,32]{2,1,0:T(1,128)} %get-tuple-element.131) | copy-start | bytes 3076
  668.7 16.0 %copy-start.36 = (pred[8]{0:T(512)(128)(4,1)S(1)}, pred[8]{0:T(512)(128)(4,1)}, u32[]{:S(2)}) copy-start(pred[8]{0:T(512)(128)(4,1)} %compare_and_fusion.4) | copy-start | bytes 28
  668.7 16.0 %copy-start.40 = (f32[32]{0:T(128)S(1)}, f32[32]{0:T(128)}, u32[]{:S(2)}) copy-start(f32[32]{0:T(128)} %get-tuple-element.138) | copy-start | bytes 388
  668.8 16.0 %copy-start.41 = (f32[32]{0:T(128)S(1)}, f32[32]{0:T(128)}, u32[]{:S(2)}) copy-start(f32[32]{0:T(128)} %get-tuple-element.139) | copy-start | bytes 388
  668.8 16.0 %copy-start.42 = (f32[32]{0:T(128)S(1)}, f32[32]{0:T(128)}, u32[]{:S(2)}) copy-start(f32[32]{0:T(128)} %get-tuple-element.140) | copy-start | bytes 388
  677.8 9.4 %copy-start.15 = (bf16[1,32,32]{2,1,0:T(8,128)(2,1)S(1)}, bf16[1,32,32]{2,1,0:T(8,128)(2,1)}, u32[]{:S(2)}) copy-start(bf16[1,32,32]{2,1,0:T(8,128)(2,1)} %param.24) | copy-start | bytes 6148
  677.8 13.6 %copy-start.16 = (bf16[1,32,32]{2,1,0:T(8,128)(2,1)S(1)}, bf16[1,32,32]{2,1,0:T(8,128)(2,1)}, u32[]{:S(2)}) copy-start(bf16[1,32,32]{2,1,0:T(8,128)(2,1)} %param.25) | copy-start | bytes 6148
  677.8 13.8 %copy-start.5 = (bf16[16,32,32]{1,2,0:T(8,128)(2,1)S(1)}, bf16[16,32,32]{1,2,0:T(8,128)(2,1)}, u32[]{:S(2)}) copy-start(bf16[16,32,32]{1,2,0:T(8,128)(2,1)} %copy.30) | copy-start | bytes 98308
  682.0 5.1 collective-permute-start.1
  684.5 1.3 collective-permute-start.4
  685.7 5.7 collective-permute-start.5
  (182 other events, 725.9 us)
Sparse Core Ops, SparseCore 0:
  22.5 69.6 all-gather.6
  95.0 69.1 all-gather.8
  167.0 61.1 all-gather.10
where the time goes:
time: 715 us; the launch traced here: 710 us
  other arithmetic  281 us (39%)
  local copies, waits for them, and re-layouts  166 us (23%)
  matrix products  161 us (23%)
  blocking collectives  37.4 us (5%)
  starting transfers between devices  24.7 us (3%)
  waiting for transfers between devices  23.8 us (3%)
  between operations  13.8 us (2%)
    scatter-add x16, other arithmetic, near_step(): accum = accum.at[second].add(to_second * back[:, None, None])  88.7 us
    scatter-add x16, other arithmetic, near_step(): accum = accum.at[first].add(to_first * live[:, None, None])  86.4 us
    dot_general x16, matrix products, near_step(): jnp.einsum('pij,pjr->pir', tile, jnp.take(table, second, axis=0), preferr...  80.9 us
    dot_general x16, matrix products, near_step(): jnp.einsum('pij,pir->pjr', tile, jnp.take(table, first, axis=0), preferre...  68.9 us
    while x448, local copies, waits for them, and re-layouts  50.7 us
    all_gather x1, blocking collectives, spread(): lax.all_gather(fourth_item, ('group', 'dev'), axis=0, tiled=True)  37.4 us
    mul x16, other arithmetic, near_step(): back = live * (first != second).astype(jnp.float32)  30.7 us
    gather x16, local copies, waits for them, and re-layouts, near_step(): jnp.take(table, second, axis=0)  28.2 us
  transfers between devices with their start and end apart: 12, of which 5 were waited for; matrix products, arithmetic and copies ran while one was open for 84% of the time, Pallas kernels for 0%

commit v1 on v0

v1 whole, which is shorter than its diff:
```python
import functools

import jax
import jax.numpy as jnp
from jax import lax
from jax.experimental import pallas as pl
from jax.experimental.pallas import tpu as pltpu
from jax.sharding import PartitionSpec as P

KCOEF = 0.005
DELTA = 0.02
F32 = jnp.float32
BF16 = jnp.bfloat16
GROUP = 8
FEAT = 16
VMEM = pl.BlockSpec(memory_space=pltpu.VMEM)
SMEM = pl.BlockSpec(memory_space=pltpu.SMEM)
PARAMS = pltpu.CompilerParams(vmem_limit_bytes=56 << 20)


def dot(left, right, dims=((1,), (0,))):
    return lax.dot_general(left, right, (dims, ((), ())), preferred_element_type=F32)


def halves(value):
    high = value.astype(BF16)
    return high, (value - high.astype(F32)).astype(BF16)


def thirds(value):
    high = value.astype(BF16)
    rest = value - high.astype(F32)
    mid = rest.astype(BF16)
    return high.astype(F32), mid.astype(F32), (rest - mid.astype(F32))


def prep_kernel(slots, charges, coords, basis, trans, qt, fa, fb, outgoing, top, rows_a, rows_b):
    clusters = coords.shape[0]
    x = coords[...].astype(F32)
    axes = [x[:, d, :] for d in range(3)]
    norm = axes[0] * axes[0] + axes[1] * axes[1] + axes[2] * axes[2]
    one = jnp.ones_like(norm)
    rows_a[...] = jnp.zeros_like(rows_a)
    rows_b[...] = jnp.zeros_like(rows_b)
    for d, row in enumerate((*axes, *thirds(norm + DELTA * DELTA), one, one, one)):
        rows_a[:, d, :] = row
    for d, row in enumerate((*(-2.0 * a for a in axes), one, one, one, *thirds(norm))):
        rows_b[:, d, :] = row
    total = jnp.zeros(top.shape, F32)
    for c in range(clusters):
        fb[c] = rows_b[c].astype(BF16)
        fa[c] = rows_a[c].T.astype(BF16)
        block = charges[c]
        qt[c] = block.T
        leaf = dot(basis[c], block).astype(BF16)
        total += dot(trans[c], leaf)
    top[...] = total.astype(BF16)

    def send(h, carry):
        c = slots[h]
        outgoing[h, : qt.shape[1], :] = qt[c]
        outgoing[h, qt.shape[1] :, :] = fb[c]
        return carry

    lax.fori_loop(0, outgoing.shape[0], send, 0)


def prep(slots, charges, coords, basis, trans, peers):
    clusters, width, conductors = charges.shape
    rank = basis.shape[1]
    return pl.pallas_call(
        prep_kernel,
        out_shape=(
            jax.ShapeDtypeStruct((clusters, conductors, width), BF16),
            jax.ShapeDtypeStruct((clusters, width, FEAT), BF16),
            jax.ShapeDtypeStruct((clusters, FEAT, width), BF16),
            jax.ShapeDtypeStruct((peers, conductors + FEAT, width), BF16),
            jax.ShapeDtypeStruct((rank, conductors), BF16),
        ),
        in_specs=[SMEM] + [VMEM] * 4,
        out_specs=(VMEM,) * 5,
        scratch_shapes=[pltpu.VMEM((clusters, FEAT, width), F32)] * 2,
        compiler_params=PARAMS,
        name="prep",
    )(slots, charges, coords, basis, trans)


def tiles(count, table, weight, fa, feat, left, right, add_first, add_second, kbuf):
    def tile(j):
        key = table[j]
        s = dot(fa[lax.rem(key, 16)], feat(key // 16))
        return lax.rsqrt(s.astype(BF16)) * weight[j].astype(BF16)

    for g in range(GROUP):
        kbuf[0, g] = tile(g)

    def body(i, carry):
        now = lax.rem(i, 2)
        for g in range(GROUP):
            j = i * GROUP + g
            key = table[j]
            a, b = lax.rem(key, 16), key // 16
            k = kbuf[now, g]
            add_first(a, dot(right(b), k, ((1,), (1,))))
            add_second(b, dot(left(a), k))
            kbuf[1 - now, g] = tile(j + GROUP)
        return carry

    lax.fori_loop(0, pl.cdiv(count, GROUP), body, 0)


def own_kernel(count, table, weight, qt, fa, fb, acc, kbuf):
    acc[...] = jnp.zeros_like(acc)

    def add(i, value):
        acc[i] += value

    tiles(count[0], table, weight, fa, lambda b: fb[b], lambda a: qt[a], lambda b: qt[b], add, add, kbuf)


def own_near(count, table, weight, qt, fa, fb):
    width = qt.shape[2]
    return pl.pallas_call(
        own_kernel,
        out_shape=jax.ShapeDtypeStruct(qt.shape, F32),
        in_specs=[SMEM] * 3 + [VMEM] * 3,
        out_specs=VMEM,
        scratch_shapes=[pltpu.VMEM((2, GROUP, width, width), BF16)],
        compiler_params=PARAMS,
        cost_estimate=pl.CostEstimate(flops=6 << 30, bytes_accessed=4 << 20, transcendentals=0),
        name="own_near",
    )(count, table, weight, qt, fa, fb)


def remote_kernel(count, table, weight, qt, fa, incoming, acc_in, acc, back, sums, kbuf):
    conductors = qt.shape[1]
    acc[...] = acc_in[...]
    sums[...] = jnp.zeros_like(sums)

    def add_own(i, value):
        acc[i] += value

    def add_remote(i, value):
        sums[i] += value

    tiles(
        count[0],
        table,
        weight,
        fa,
        lambda b: incoming[b, conductors:, :],
        lambda a: qt[a],
        lambda b: incoming[b, :conductors, :],
        add_own,
        add_remote,
        kbuf,
    )

    def finish(b, carry):
        back[b] = (sums[b] * KCOEF).astype(BF16)
        return carry

    lax.fori_loop(0, back.shape[0], finish, 0)


def remote_near(count, table, weight, qt, fa, incoming, acc):
    peers = incoming.shape[0]
    _, conductors, width = qt.shape
    return pl.pallas_call(
        remote_kernel,
        out_shape=(
            jax.ShapeDtypeStruct(acc.shape, F32),
            jax.ShapeDtypeStruct((peers, conductors, width), BF16),
        ),
        in_specs=[SMEM] * 3 + [VMEM] * 4,
        out_specs=(VMEM, VMEM),
        scratch_shapes=[
            pltpu.VMEM((peers, conductors, width), F32),
            pltpu.VMEM((2, GROUP, width, width), BF16),
        ],
        compiler_params=PARAMS,
        cost_estimate=pl.CostEstimate(flops=12 << 30, bytes_accessed=8 << 20, transcendentals=0),
        name="remote_near",
    )(count, table, weight, qt, fa, incoming, acc)


def far_kernel(ids, own_points, nodes, trans, leaf, sources):
    rank = 32

    def skel(n):
        return nodes[n, :rank, :]

    def transfer(n, which):
        rows = nodes[n, rank : rank + 16, :]
        lo = 64 * which
        return jnp.concatenate([rows[:, lo : lo + 32], rows[:, lo + 32 : lo + 64]], axis=0)

    def points(n):
        return nodes[n, rank + 16 : rank + 32, :].astype(F32)[:1]

    def kernel_tile(mine, theirs):
        gap = mine - theirs
        sq = gap * gap
        s = ((DELTA * DELTA + sq[:, :32]) + sq[:, 32:64]) + sq[:, 64:96]
        return halves(KCOEF * lax.rsqrt(s))

    def apply(tile, source):
        return dot(tile[0], source) + dot(tile[1], source)

    mine = [own_points[level] for level in range(3)]
    zero = jnp.zeros((rank, nodes.shape[2]), F32)

    def one(f, total):
        n = ids[f]
        return total + apply(kernel_tile(mine[0], points(n)), skel(n))

    def two(f, total):
        n = 2 * ids[8 + f]
        source = dot(transfer(n, 0), skel(n)) + dot(transfer(n + 1, 0), skel(n + 1))
        theirs = 0.5 * (points(n) + points(n + 1))
        return total + apply(kernel_tile(mine[1], theirs), source.astype(BF16))

    def three(f, total):
        n = 4 * ids[24 + f]
        terms = [dot(transfer(n + i, 1), skel(n + i)) for i in range(4)]
        source = (terms[0] + terms[1]) + (terms[2] + terms[3])
        left = 0.5 * (points(n) + points(n + 1))
        right = 0.5 * (points(n + 2) + points(n + 3))
        return total + apply(kernel_tile(mine[2], 0.5 * (left + right)), source.astype(BF16))

    far_one = lax.fori_loop(0, 8, one, zero, unroll=True)
    far_two = lax.fori_loop(0, 16, two, zero, unroll=4)
    far_three = lax.fori_loop(0, 32, three, zero, unroll=4)
    me = ids[56]

    def down_by(which, value):
        high, low = halves(value)
        mat = transfer(me, which)
        return dot(mat, high, ((0,), (0,))) + dot(mat, low, ((0,), (0,)))

    down = far_one + down_by(0, far_two) + down_by(1, far_three)
    high, low = halves(down.T)
    for c in range(trans.shape[0]):
        leaf[c] = (dot(high, trans[c]) + dot(low, trans[c])).astype(BF16)


def far_field(ids, own_points, nodes, trans):
    clusters, rank, _ = trans.shape
    return pl.pallas_call(
        far_kernel,
        out_shape=jax.ShapeDtypeStruct((clusters, nodes.shape[2], rank), BF16),
        in_specs=[SMEM] + [VMEM] * 3,
        out_specs=VMEM,
        scratch_shapes=[pltpu.VMEM((8, 128), F32)],
        compiler_params=PARAMS,
        cost_estimate=pl.CostEstimate(flops=6 << 30, bytes_accessed=4 << 20, transcendentals=0),
        name="far_field",
    )(ids, own_points, nodes, trans)


def final_kernel(slots, acc, returned, leaf, basis, out, sums):
    def scale(c, carry):
        sums[c] = acc[c] * KCOEF + dot(leaf[c], basis[c])
        return carry

    lax.fori_loop(0, acc.shape[0], scale, 0)

    def collect(h, carry):
        sums[slots[h]] += returned[h].astype(F32)
        return carry

    lax.fori_loop(0, returned.shape[0], collect, 0)

    def turn(c, carry):
        out[c] = sums[c].T
        return carry

    lax.fori_loop(0, acc.shape[0], turn, 0)


def finish(slots, acc, returned, leaf, basis):
    clusters, conductors, width = acc.shape
    return pl.pallas_call(
        final_kernel,
        out_shape=jax.ShapeDtypeStruct((clusters, width, conductors), F32),
        in_specs=[SMEM] + [VMEM] * 4,
        out_specs=VMEM,
        scratch_shapes=[pltpu.VMEM(acc.shape, F32)],
        compiler_params=PARAMS,
        name="finish",
    )(slots, acc, returned, leaf, basis)


def pair_lists(first, second, count, clusters, entries):
    live = jnp.arange(first.shape[0], dtype=jnp.int32) < count
    own = second < clusters
    a = jnp.where(own, jnp.minimum(first, second), first)
    b = jnp.where(own, jnp.maximum(first, second), second)
    key = jnp.where(live, b * clusters + a, -1)
    keys = jnp.arange(entries * clusters, dtype=jnp.int32)
    times = jnp.sum((keys[:, None] == key[None, :]).astype(F32), axis=1)
    times = jnp.where(keys % clusters == keys // clusters, 0.5 * times, times)
    lists = []
    for lo, hi in ((0, clusters * clusters), (clusters * clusters, entries * clusters)):
        part = times[lo:hi]
        held = part > 0
        spots = jnp.arange(hi - lo, dtype=jnp.int32)
        rank = jnp.sum(((spots[None, :] < spots[:, None]) & held[None, :]).astype(jnp.int32), axis=1)
        slots = jnp.arange(256 + 2 * GROUP, dtype=jnp.int32)
        match = (rank[None, :] == slots[:, None]) & held[None, :]
        table = jnp.sum(jnp.where(match, spots[None, :], 0), axis=1)
        weight = jnp.sum(jnp.where(match, part[None, :], 0.0), axis=1)
        lists.append((jnp.sum(held.astype(jnp.int32)).reshape(1), table, weight))
    return lists


def shards(
    charges,
    panel_coords,
    cluster_basis,
    trans_leaf,
    trans_pair,
    trans_quad,
    skel_points,
    send_slots,
    pair_first,
    pair_second,
    pair_count,
    far_one,
    far_two,
    far_three,
):
    clusters, _, width = panel_coords.shape
    conductors = charges.shape[1]
    peers = lax.axis_size("dev")
    slots = send_slots.reshape(-1)
    blocks = charges.reshape(clusters, width, conductors)
    qt, fa, fb, outgoing, top = prep(slots, blocks, panel_coords, cluster_basis, trans_leaf, peers)
    incoming = lax.all_to_all(outgoing, "dev", split_axis=0, concat_axis=0, tiled=True)

    def folded(mat):
        return jnp.concatenate([mat[0, :16], mat[0, 16:]], axis=1)

    points_row = skel_points.reshape(1, -1)
    lists_row = jnp.concatenate([far_two, far_three], axis=1).astype(BF16)
    payload = jnp.concatenate(
        [
            top,
            jnp.concatenate([folded(trans_pair), folded(trans_quad)], axis=1),
            jnp.pad(points_row, ((0, 0), (0, conductors - points_row.shape[1]))),
            jnp.pad(lists_row, ((0, 14), (0, conductors - lists_row.shape[1]))),
        ],
        axis=0,
    )
    nodes = lax.all_gather(payload, ("group", "dev"), axis=0)

    own_list, remote_list = pair_lists(pair_first, pair_second, pair_count[0], clusters, clusters + peers)
    acc = own_near(*own_list, qt, fa, fb)
    acc, back = remote_near(*remote_list, qt, fa, incoming, acc)
    returned = lax.all_to_all(back, "dev", split_axis=0, concat_axis=0, tiled=True)

    owner = lax.axis_index("group") * peers + lax.axis_index("dev")
    quad = lax.dynamic_slice_in_dim(nodes, owner // 4 * 4, 4, axis=0)
    quad_lists = quad[:, 49, :16].astype(jnp.int32)
    pair_list = lax.dynamic_slice_in_dim(quad_lists[:, :8], owner % 4 // 2 * 2, 2, axis=0)
    ids = jnp.concatenate(
        [far_one[0], pair_list.reshape(-1), quad_lists[:, 8:].reshape(-1), owner.reshape(1)]
    )
    quad_points = quad[:, 48, :96].astype(F32).reshape(4, 3, 32)
    pair_points = 0.5 * (quad_points[0::2] + quad_points[1::2])
    own_points = jnp.stack(
        [
            skel_points[0].astype(F32),
            jnp.take(pair_points, owner % 4 // 2, axis=0),
            0.5 * (pair_points[0] + pair_points[1]),
        ]
    )
    own_points = jnp.repeat(jnp.swapaxes(own_points, 1, 2), 32, axis=2)
    own_points = jnp.pad(own_points, ((0, 0), (0, 0), (0, 32)))
    leaf = far_field(ids, own_points, nodes, trans_leaf)
    out = finish(slots, acc, returned, leaf, cluster_basis)
    return out.reshape(clusters * width, conductors)


def solution(mesh):
    owners = ("group", "dev")
    rows, block, flat = P(owners, None), P(owners, None, None), P(owners)
    placed = (rows, *(block,) * 6, rows, *(flat,) * 3, *(rows,) * 3)
    return jax.shard_map(shards, mesh=mesh, in_specs=placed, out_specs=rows, check_vma=False)
```

time: 715 us -> 141 us (0.20)
  the two profiles are of different devices: /device:TPU:1 before, /device:TPU:7 now
where the time goes in v1:
time: 141 us; the launch traced here: 140 us
  Pallas kernels  55.8 us (40%)
  waiting for transfers between devices  38.3 us (27%)
  starting transfers between devices  15 us (11%)
  between operations  14.2 us (10%)
  other arithmetic  9.73 us (7%)
  local copies, waits for them, and re-layouts  7.01 us (5%)
    all_gather x1, waiting for transfers between devices, shards(): nodes = lax.all_gather(payload, ('group', 'dev'), axis=0)  25.9 us
    pallas_call x1, Pallas kernels, remote_near(): pl.pallas_call(remote_kernel, out_shape=(jax.ShapeDtypeStruct(acc.shape,...  22.2 us
    all_to_all x1, waiting for transfers between devices, shards(): lax.all_to_all(outgoing, 'dev', split_axis=0, concat_axis=0, tiled=True)  12.4 us
    pallas_call x1, Pallas kernels, own_near(): pl.pallas_call(own_kernel, out_shape=jax.ShapeDtypeStruct(qt.shape, F32),...  11.2 us
    pallas_call x1, Pallas kernels, far_field(): pl.pallas_call(far_kernel, out_shape=jax.ShapeDtypeStruct((clusters, node...  9.59 us
    all_to_all x1, starting transfers between devices, shards(): lax.all_to_all(outgoing, 'dev', split_axis=0, concat_axis=0, tiled=True)  7.95 us
    pallas_call x1, Pallas kernels, finish(): pl.pallas_call(final_kernel, out_shape=jax.ShapeDtypeStruct((clusters, wi...  7.92 us
    all_to_all x1, starting transfers between devices, shards(): lax.all_to_all(back, 'dev', split_axis=0, concat_axis=0, tiled=True)  7.03 us
  transfers between devices with their start and end apart: 3, of which 2 were waited for; matrix products, arithmetic and copies ran while one was open for 6% of the time, Pallas kernels for 31%

profile of v1, /device:TPU:7, one launch (start us, length us, event | category | flops | bytes accessed | tf_op | source)
XLA Modules:
  0.0 140.1 jit_solution(15623253627355702561)
XLA Ops:
  6.5 0.0 all-gather.3.cloned.1.call-start
  6.5 1.4 copy.19.coords
  7.9 0.8 reshape.86
  8.7 0.7 convert.9
  9.3 0.7 convert.8
  10.0 0.1 fusion.20
  10.1 0.7 slice_bitcast_fusion.1
  10.8 4.8 %prep.1 = (bf16[16,128,256]{2,1,0:T(8,128)(2,1)}, bf16[16,256,16]{2,1,0:T(8,128)(2,1)}, bf16[16,16,256]{2,1,0:T(8,128)(2,1)}, bf16[32,144,256]{2,1,0:T(8,128)(2,1)}, bf16[32,128]{1,0:T(8,128)(2,1)}) custom-call(s32[32]{0:T(128)} %bitcast.23, bf16[16,256,128]{2,1,0:T(8,128)(2,1)} %bitcast.21, bf16[16,3,256]{2,1,0:T(4,128)(2,1)} %copy.19.coords, ...), custom_call_target="tpu_custom_call" | custom-call | tf_op jit(solution)/shard_map/prep/pallas_call | solution.py:71
  15.6 1.4 fusion.7
  17.0 0.0 all-gather.3.cloned.1.call-update
  17.0 0.0 copy-start.2
  17.0 0.0 copy-start.3
  17.1 7.9 %all-to-all-start = ((bf16[32,144,256]{2,1,0:T(8,128)(2,1)}), bf16[32,144,256]{2,1,0:T(8,128)(2,1)S(1)}, u32[]{:S(2)}, u32[]{:S(2)}) async-start(bf16[32,144,256]{2,1,0:T(8,128)(2,1)} %get-tuple-element.14), calls=%async_computation | async-start | bytes 4718592 | tf_op jit(solution)/shard_map/all_to_all | solution.py:339
  25.7 0.0 copy-done.2
  25.7 0.0 copy-done.3
  25.7 0.2 convert_reduce_fusion.1
  25.9 0.6 convert_reduce_fusion.4
  26.6 0.1 convert_reduce_fusion.2
  26.7 0.8 select_reduce_fusion.3.table
  27.4 0.7 select_reduce_fusion.2.weight
  28.2 0.7 convert_reduce_fusion.3
  28.9 0.1 convert_reduce_fusion
  29.0 0.8 select_reduce_fusion.1.table
  29.8 0.7 select_reduce_fusion.weight
  30.6 11.2 %own_near.1.acc_in = f32[16,128,256]{2,1,0:T(8,128)} custom-call(s32[1]{0:T(128)} %bitcast.4.count, s32[272]{0:T(512)} %select_reduce_fusion.3.table, f32[272]{0:T(512)} %select_reduce_fusion.2.weight, bf16[16,128,256]{2,1,0:T(8,128)(2,1)} %get-tuple-element.12.qt, bf16[16,256,16]{2,1,0:T(8,128)(2,1)} %get-tuple-element.13.fa, ...), custom_call_target="tpu_custom_call" | custom-call | flops 6442450944 | bytes 4194304 | tf_op jit(solution)/shard_map/own_near/pallas_call | solution.py:123
  41.8 12.4 %all-to-all-done.incoming = bf16[32,144,256]{2,1,0:T(8,128)(2,1)S(1)} async-done(((bf16[32,144,256]{2,1,0:T(8,128)(2,1)}), bf16[32,144,256]{2,1,0:T(8,128)(2,1)S(1)}, u32[]{:S(2)}, u32[]{:S(2)}) %all-to-all-start) | async-done | bytes 2359328 | tf_op jit(solution)/shard_map/all_to_all | solution.py:339
  54.2 0.0 copy-start.1
  54.2 1.4 %copy-done.1 = bf16[32,144,256]{2,1,0:T(8,128)(2,1)} copy-done((bf16[32,144,256]{2,1,0:T(8,128)(2,1)}, bf16[32,144,256]{2,1,0:T(8,128)(2,1)S(1)}, u32[]{:S(2)}) %copy-start.1) | copy-done | bytes 2359320
  55.6 22.2 %remote_near.1 = (f32[16,128,256]{2,1,0:T(8,128)}, bf16[32,128,256]{2,1,0:T(8,128)(2,1)}) custom-call(s32[1]{0:T(128)} %bitcast.2.count, s32[272]{0:T(512)} %select_reduce_fusion.1.table, f32[272]{0:T(512)} %select_reduce_fusion.weight, bf16[16,128,256]{2,1,0:T(8,128)(2,1)} %get-tuple-element.12.qt, bf16[16,256,16]{2,1,0:T(8,128)(2,1)} %get-tuple-element.13.fa, ...), custom_call_target="tpu_custom_call" | custom-call | flops 12884901888 | bytes 8388608 | tf_op jit(solution)/shard_map/remote_near/pallas_call | solution.py:169
  77.8 7.0 %all-to-all-start.1 = ((bf16[32,128,256]{2,1,0:T(8,128)(2,1)}), bf16[32,128,256]{2,1,0:T(8,128)(2,1)S(1)}, u32[]{:S(2)}, u32[]{:S(2)}) async-start(bf16[32,128,256]{2,1,0:T(8,128)(2,1)} %get-tuple-element.17), calls=%async_computation.1 | async-start | bytes 4194304 | tf_op jit(solution)/shard_map/all_to_all | solution.py:360
  84.9 0.0 copy-done.4
  85.0 25.9 %all-gather.3.cloned.1.call-done = bf16[8192,128]{1,0:T(8,128)(2,1)} async-done(((bf16[64,128]{1,0:T(8,128)(2,1)}), bf16[8192,128]{1,0:T(8,128)(2,1)}) %all-gather.3.cloned.1.call-update) | async-done | bytes 2097168 | tf_op jit(solution)/shard_map/all_gather | solution.py:355
  110.9 0.7 dynamic-slice_convert_fusion.1
  111.6 0.1 fusion.26
  111.7 0.1 reshape.88
  111.8 0.1 reshape.87
  111.9 0.7 fusion.23
  112.6 0.1 reshape.119
  112.7 0.1 copy.20
  112.8 0.2 broadcast_in_dim.97
  113.0 0.1 reshape.90
  113.1 0.6 pad.14.own_points
  113.7 0.0 copy-done.5
  113.7 0.7 pad_add_fusion.ids
  114.4 9.6 %far_field.1.leaf = bf16[16,128,32]{2,1,0:T(8,128)(2,1)} custom-call(s32[57]{0:T(128)} %pad_add_fusion.ids, f32[3,32,128]{2,1,0:T(8,128)} %pad.14.own_points, bf16[128,64,128]{2,1,0:T(8,128)(2,1)} %bitcast.28, bf16[16,32,32]{2,1,0:T(8,128)(2,1)} %trans.3), custom_call_target="tpu_custom_call" | custom-call | flops 6442450944 | bytes 4194304 | tf_op jit(solution)/shard_map/far_field/pallas_call | solution.py:249
  124.0 0.0 all-to-all-done.1.returned
  124.0 1.4 copy-done
  125.3 7.9 %finish.1 = f32[16,256,128]{2,1,0:T(8,128)} custom-call(s32[32]{0:T(128)} %bitcast.24, f32[16,128,256]{2,1,0:T(8,128)} %get-tuple-element.16.acc, bf16[32,128,256]{2,1,0:T(8,128)(2,1)} %copy-done, bf16[16,128,32]{2,1,0:T(8,128)(2,1)} %far_field.1.leaf, bf16[16,32,256]{2,1,0:T(8,128)(2,1)} %basis.3), custom_call_target="tpu_custom_call" | custom-call | tf_op jit(solution)/shard_map/finish/pallas_call | solution.py:283
  (12 shorter events, 0.1 us)
Async XLA Ops:
  6.5 104.4 %all-gather.3.cloned.1.call-start = ((), (), s32[]{:S(2)}) async-start(), calls=%async_computation.2 | async-start | bytes 2113536 | tf_op jit(solution)/shard_map/all_gather | solution.py:355
  17.0 8.6 %copy-start.2 = (s32[256]{0:T(256)S(1)}, s32[256]{0:T(256)}, u32[]{:S(2)}) copy-start(s32[256]{0:T(256)} %param.23) | copy-start | bytes 3076
  17.0 8.6 %copy-start.3 = (s32[256]{0:T(256)S(1)}, s32[256]{0:T(256)}, u32[]{:S(2)}) copy-start(s32[256]{0:T(256)} %param.22) | copy-start | bytes 3076
  17.1 37.1 %all-to-all-start = ((bf16[32,144,256]{2,1,0:T(8,128)(2,1)}), bf16[32,144,256]{2,1,0:T(8,128)(2,1)S(1)}, u32[]{:S(2)}, u32[]{:S(2)}) async-start(bf16[32,144,256]{2,1,0:T(8,128)(2,1)} %get-tuple-element.14), calls=%async_computation | async-start | bytes 4718592 | tf_op jit(solution)/shard_map/all_to_all | solution.py:339
  54.2 1.4 %copy-start.1 = (bf16[32,144,256]{2,1,0:T(8,128)(2,1)}, bf16[32,144,256]{2,1,0:T(8,128)(2,1)S(1)}, u32[]{:S(2)}) copy-start(bf16[32,144,256]{2,1,0:T(8,128)(2,1)S(1)} %all-to-all-done.incoming) | copy-start | bytes 7077892
  77.8 7.1 %copy-start.4 = (bf16[1,3,32]{2,1,0:T(4,128)(2,1)S(1)}, bf16[1,3,32]{2,1,0:T(4,128)(2,1)}, u32[]{:S(2)}) copy-start(bf16[1,3,32]{2,1,0:T(4,128)(2,1)} %param.20) | copy-start | bytes 580
  77.8 35.9 %copy-start.5 = (s32[1,8]{1,0:T(1,128)S(1)}, s32[1,8]{1,0:T(1,128)}, u32[]{:S(2)}) copy-start(s32[1,8]{1,0:T(1,128)} %param.25) | copy-start | bytes 100
  77.8 46.2 %all-to-all-start.1 = ((bf16[32,128,256]{2,1,0:T(8,128)(2,1)}), bf16[32,128,256]{2,1,0:T(8,128)(2,1)S(1)}, u32[]{:S(2)}, u32[]{:S(2)}) async-start(bf16[32,128,256]{2,1,0:T(8,128)(2,1)} %get-tuple-element.17), calls=%async_computation.1 | async-start | bytes 4194304 | tf_op jit(solution)/shard_map/all_to_all | solution.py:360
  124.0 1.4 copy-start
Sparse Core Ops, SparseCore 0:
  17.1 93.7 all-gather.2

commit v2 on v1

v2 whole, which is shorter than its diff:
```python
import functools

import jax
import jax.numpy as jnp
from jax import lax
from jax.experimental import pallas as pl
from jax.experimental.pallas import tpu as pltpu
from jax.sharding import PartitionSpec as P

KCOEF = 0.005
DELTA = 0.02
F32 = jnp.float32
BF16 = jnp.bfloat16
GROUP = 8
FEAT = 16
VMEM = pl.BlockSpec(memory_space=pltpu.VMEM)
SMEM = pl.BlockSpec(memory_space=pltpu.SMEM)
MESH = pl.DeviceIdType.MESH
PARAMS = pltpu.CompilerParams(vmem_limit_bytes=56 << 20)


def dot(left, right, dims=((1,), (0,))):
    return lax.dot_general(left, right, (dims, ((), ())), preferred_element_type=F32)


def halves(value):
    high = value.astype(BF16)
    return high, (value - high.astype(F32)).astype(BF16)


def thirds(value):
    high = value.astype(BF16)
    rest = value - high.astype(F32)
    mid = rest.astype(BF16)
    return high.astype(F32), mid.astype(F32), (rest - mid.astype(F32))


def prep_kernel(slots, charges, axes, qt, fa, fb, outgoing, rows_a, rows_b, sems):
    clusters = charges.shape[0]
    x = [axes[d] for d in range(3)]
    norm = x[0] * x[0] + x[1] * x[1] + x[2] * x[2]
    one = jnp.ones_like(norm)
    rows_a[...] = jnp.zeros_like(rows_a)
    rows_b[...] = jnp.zeros_like(rows_b)
    for d, row in enumerate((*x, *thirds(norm + DELTA * DELTA), one, one, one)):
        rows_a[:, d, :] = row
    for d, row in enumerate((*(-2.0 * a for a in x), one, one, one, *thirds(norm))):
        rows_b[:, d, :] = row
    for c in range(clusters):
        fb[c] = rows_b[c].astype(BF16)
        qt[c] = charges[c].T
    split = qt.shape[1]

    def copies(h):
        c = slots[h, 0]
        return (
            pltpu.make_async_copy(qt.at[c], outgoing.at[h, pl.ds(0, split)], sems.at[h, 0]),
            pltpu.make_async_copy(fb.at[c], outgoing.at[h, pl.ds(split, FEAT)], sems.at[h, 1]),
        )

    def send(h, carry):
        for copy in copies(h):
            copy.start()
        return carry

    def wait(h, carry):
        for copy in copies(h):
            copy.wait()
        return carry

    lax.fori_loop(0, outgoing.shape[0], send, 0)
    for c in range(clusters):
        fa[c] = rows_a[c].T.astype(BF16)
    lax.fori_loop(0, outgoing.shape[0], wait, 0)


def prep(slots, charges, axes):
    clusters, width, conductors = charges.shape
    peers = slots.shape[0]
    return pl.pallas_call(
        prep_kernel,
        out_shape=(
            jax.ShapeDtypeStruct((clusters, conductors, width), BF16),
            jax.ShapeDtypeStruct((clusters, width, FEAT), BF16),
            jax.ShapeDtypeStruct((clusters, FEAT, width), BF16),
            jax.ShapeDtypeStruct((peers, conductors + FEAT, width), BF16),
        ),
        in_specs=[SMEM] + [VMEM] * 2,
        out_specs=(VMEM, VMEM, VMEM, pl.BlockSpec(memory_space=pl.ANY)),
        scratch_shapes=[pltpu.VMEM((clusters, FEAT, width), F32)] * 2
        + [pltpu.SemaphoreType.DMA((peers, 2))],
        compiler_params=PARAMS,
        name="prep",
    )(slots, charges, axes)


def gather_kernel(charges, basis, trans, rest, nodes, send_sem, recv_sem):
    z, d = lax.axis_index("group"), lax.axis_index("dev")
    x, y, c = d // 8, lax.rem(d // 2, 4), lax.rem(d, 2)

    def place(x, y, z, c):
        return {"group": z, "dev": (x * 4 + y) * 2 + c}

    def turn(i, k):
        return lax.rem(i + k, 4)

    stages = (
        (((c * 4 + z) * 4 + y) * 4 + x, 1, [place(turn(x, k), y, z, c) for k in (1, 2, 3)]),
        (((c * 4 + z) * 4 + y) * 4, 4, [place(x, turn(y, k), z, c) for k in (1, 2, 3)]),
        ((c * 4 + z) * 16, 16, [place(x, y, turn(z, k), c) for k in (1, 2, 3)]),
        (c * 64, 64, [place(x, y, z, 1 - c)]),
    )
    barrier = pltpu.get_barrier_semaphore()
    for _, _, peers in stages:
        for peer in peers:
            pl.semaphore_signal(barrier, inc=1, device_id=peer, device_id_type=MESH)

    rank = trans.shape[1]
    total = jnp.zeros((rank, charges.shape[2]), F32)
    for i in range(trans.shape[0]):
        leaf = dot(basis[i], charges[i]).astype(BF16)
        total += dot(trans[i], leaf)
    me = stages[0][0]
    nodes[me, :rank, :] = total.astype(BF16)
    nodes[me, rank:, :] = rest[...]
    pl.semaphore_wait(barrier, 10)

    for level, (start, length, peers) in enumerate(stages):
        held = nodes.at[pl.ds(start, length)]
        copies = [
            pltpu.make_async_remote_copy(
                src_ref=held,
                dst_ref=held,
                send_sem=send_sem.at[level, k],
                recv_sem=recv_sem.at[level, k],
                device_id=peer,
                device_id_type=MESH,
            )
            for k, peer in enumerate(peers)
        ]
        for copy in copies:
            copy.start()
        for copy in copies:
            copy.wait()


def gather_nodes(charges, basis, trans, rest):
    rank, conductors = trans.shape[1], charges.shape[2]
    return pl.pallas_call(
        gather_kernel,
        out_shape=jax.ShapeDtypeStruct((128, rank + rest.shape[0], conductors), BF16),
        in_specs=[VMEM] * 4,
        out_specs=VMEM,
        scratch_shapes=[pltpu.SemaphoreType.DMA((4, 3))] * 2,
        compiler_params=pltpu.CompilerParams(
            vmem_limit_bytes=32 << 20, collective_id=0, has_side_effects=True
        ),
        cost_estimate=pl.CostEstimate(flops=12 << 30, bytes_accessed=4 << 20, transcendentals=0),
        name="gather_nodes",
    )(charges, basis, trans, rest)


def tiles(count, table, weight, fa, feat, left, right, add_first, add_second, kbuf):
    def tile(j):
        key = table[j]
        s = dot(fa[lax.rem(key, 16)], feat(key // 16))
        return lax.rsqrt(s.astype(BF16)) * weight[j].astype(BF16)

    for g in range(GROUP):
        kbuf[0, g] = tile(g)

    def body(i, carry):
        now = lax.rem(i, 2)
        for g in range(GROUP):
            j = i * GROUP + g
            key = table[j]
            a, b = lax.rem(key, 16), key // 16
            k = kbuf[now, g]
            add_first(a, dot(right(b), k, ((1,), (1,))))
            add_second(b, dot(left(a), k))
            kbuf[1 - now, g] = tile(j + GROUP)
        return carry

    lax.fori_loop(0, pl.cdiv(count, GROUP), body, 0)


def own_kernel(count, table, weight, qt, fa, fb, acc, kbuf):
    acc[...] = jnp.zeros_like(acc)

    def add(i, value):
        acc[i] += value

    tiles(count[0], table, weight, fa, lambda b: fb[b], lambda a: qt[a], lambda b: qt[b], add, add, kbuf)


def own_near(count, table, weight, qt, fa, fb):
    width = qt.shape[2]
    return pl.pallas_call(
        own_kernel,
        out_shape=jax.ShapeDtypeStruct(qt.shape, F32),
        in_specs=[SMEM] * 3 + [VMEM] * 3,
        out_specs=VMEM,
        scratch_shapes=[pltpu.VMEM((2, GROUP, width, width), BF16)],
        compiler_params=PARAMS,
        cost_estimate=pl.CostEstimate(flops=6 << 30, bytes_accessed=4 << 20, transcendentals=0),
        name="own_near",
    )(count, table, weight, qt, fa, fb)


def reply_kernel(count, table, weight, qt, fa, incoming, back, kbuf):
    conductors, width = qt.shape[1:]
    back[...] = jnp.zeros_like(back)

    def tile(j):
        key = table[j]
        s = dot(fa[lax.rem(key, 16)], incoming[key // 16, conductors:, :])
        return lax.rsqrt(s.astype(BF16)) * weight[j].astype(BF16)

    for g in range(GROUP):
        kbuf[0, g] = tile(g)

    def body(i, total):
        now = lax.rem(i, 2)
        for g in range(GROUP):
            j = i * GROUP + g
            before = table[jnp.maximum(j - 1, 0)] // 16
            key = table[j]
            a, b = lax.rem(key, 16), key // 16
            keep = jnp.where(before == b, 1.0, 0.0).astype(F32)
            total = total * keep + dot(qt[a], kbuf[now, g])
            back[b] = total.astype(BF16)
            kbuf[1 - now, g] = tile(j + GROUP)
        return total

    lax.fori_loop(0, pl.cdiv(count[0], GROUP), body, jnp.zeros((conductors, width), F32))


def reply(count, table, weight, qt, fa, incoming):
    peers = incoming.shape[0]
    _, conductors, width = qt.shape
    return pl.pallas_call(
        reply_kernel,
        out_shape=jax.ShapeDtypeStruct((peers, conductors, width), BF16),
        in_specs=[SMEM] * 3 + [VMEM] * 3,
        out_specs=VMEM,
        scratch_shapes=[pltpu.VMEM((2, GROUP, width, width), BF16)],
        compiler_params=PARAMS,
        cost_estimate=pl.CostEstimate(flops=6 << 30, bytes_accessed=8 << 20, transcendentals=0),
        name="reply",
    )(count, table, weight, qt, fa, incoming)


def remote_kernel(count, table, weight, fa, incoming, acc_in, acc, kbuf):
    conductors = acc.shape[1]
    acc[...] = acc_in[...]

    def tile(j):
        key = table[j]
        s = dot(fa[lax.rem(key, 16)], incoming[key // 16, conductors:, :])
        return lax.rsqrt(s.astype(BF16)) * weight[j].astype(BF16)

    for g in range(GROUP):
        kbuf[0, g] = tile(g)

    def body(i, carry):
        now = lax.rem(i, 2)
        for g in range(GROUP):
            j = i * GROUP + g
            key = table[j]
            a, b = lax.rem(key, 16), key // 16
            acc[a] += dot(incoming[b, :conductors, :], kbuf[now, g], ((1,), (1,)))
            kbuf[1 - now, g] = tile(j + GROUP)
        return carry

    lax.fori_loop(0, pl.cdiv(count[0], GROUP), body, 0)


def remote_near(count, table, weight, fa, incoming, acc):
    width = acc.shape[2]
    return pl.pallas_call(
        remote_kernel,
        out_shape=jax.ShapeDtypeStruct(acc.shape, F32),
        in_specs=[SMEM] * 3 + [VMEM] * 3,
        out_specs=VMEM,
        scratch_shapes=[pltpu.VMEM((2, GROUP, width, width), BF16)],
        compiler_params=PARAMS,
        cost_estimate=pl.CostEstimate(flops=6 << 30, bytes_accessed=8 << 20, transcendentals=0),
        name="remote_near",
    )(count, table, weight, fa, incoming, acc)


def far_kernel(ids, own_points, nodes, trans, leaf, sources):
    rank = 32

    def skel(n):
        return nodes[n, :rank, :]

    def transfer(n, which):
        rows = nodes[n, rank : rank + 16, :]
        lo = 64 * which
        return jnp.concatenate([rows[:, lo : lo + 32], rows[:, lo + 32 : lo + 64]], axis=0)

    def points(n):
        return nodes[n, rank + 16 : rank + 32, :].astype(F32)[:1]

    def kernel_tile(mine, theirs):
        gap = mine - theirs
        sq = gap * gap
        s = ((DELTA * DELTA + sq[:, :32]) + sq[:, 32:64]) + sq[:, 64:96]
        return halves(KCOEF * lax.rsqrt(s))

    def apply(tile, source):
        return dot(tile[0], source) + dot(tile[1], source)

    mine = [own_points[level] for level in range(3)]
    zero = jnp.zeros((rank, nodes.shape[2]), F32)

    def one(f, total):
        n = ids[f]
        return total + apply(kernel_tile(mine[0], points(n)), skel(n))

    def two(f, total):
        n, m = ids[8 + f], ids[8 + f] + 64
        source = dot(transfer(n, 0), skel(n)) + dot(transfer(m, 0), skel(m))
        theirs = 0.5 * (points(n) + points(m))
        return total + apply(kernel_tile(mine[1], theirs), source.astype(BF16))

    def three(f, total):
        n = [ids[24 + f] + step for step in (0, 64, 4, 68)]
        terms = [dot(transfer(i, 1), skel(i)) for i in n]
        source = (terms[0] + terms[1]) + (terms[2] + terms[3])
        left = 0.5 * (points(n[0]) + points(n[1]))
        right = 0.5 * (points(n[2]) + points(n[3]))
        return total + apply(kernel_tile(mine[2], 0.5 * (left + right)), source.astype(BF16))

    far_one = lax.fori_loop(0, 8, one, zero, unroll=True)
    far_two = lax.fori_loop(0, 16, two, zero, unroll=4)
    far_three = lax.fori_loop(0, 32, three, zero, unroll=4)
    me = ids[56]

    def down_by(which, value):
        high, low = halves(value)
        mat = transfer(me, which)
        return dot(mat, high, ((0,), (0,))) + dot(mat, low, ((0,), (0,)))

    down = far_one + down_by(0, far_two) + down_by(1, far_three)
    high, low = halves(down.T)
    for c in range(trans.shape[0]):
        leaf[c] = (dot(high, trans[c]) + dot(low, trans[c])).astype(BF16)


def far_field(ids, own_points, nodes, trans):
    clusters, rank, _ = trans.shape
    return pl.pallas_call(
        far_kernel,
        out_shape=jax.ShapeDtypeStruct((clusters, nodes.shape[2], rank), BF16),
        in_specs=[SMEM] + [VMEM] * 3,
        out_specs=VMEM,
        scratch_shapes=[pltpu.VMEM((8, 128), F32)],
        compiler_params=PARAMS,
        cost_estimate=pl.CostEstimate(flops=6 << 30, bytes_accessed=4 << 20, transcendentals=0),
        name="far_field",
    )(ids, own_points, nodes, trans)


def base_kernel(acc, leaf, basis, base):
    def one(c, carry):
        base[c] = acc[c] * KCOEF + dot(leaf[c], basis[c])
        return carry

    lax.fori_loop(0, acc.shape[0], one, 0)


def base_sum(acc, leaf, basis):
    return pl.pallas_call(
        base_kernel,
        out_shape=jax.ShapeDtypeStruct(acc.shape, F32),
        in_specs=[VMEM] * 3,
        out_specs=VMEM,
        compiler_params=PARAMS,
        cost_estimate=pl.CostEstimate(flops=2 << 30, bytes_accessed=4 << 20, transcendentals=0),
        name="base_sum",
    )(acc, leaf, basis)


def final_kernel(order, starts, base, returned, out, rows, sems):
    clusters = base.shape[0]

    def copy(c):
        return pltpu.make_async_copy(rows.at[c], out.at[c], sems.at[c])

    for c in range(clusters):

        def collect(i, total):
            return total + returned[order[i]].astype(F32)

        zero = jnp.zeros(base.shape[1:], F32)
        total = lax.fori_loop(starts[c], starts[c + 1], collect, zero)
        rows[c] = (base[c] + KCOEF * total).T
        copy(c).start()
    for c in range(clusters):
        copy(c).wait()


def finish(order, starts, base, returned):
    clusters, conductors, width = base.shape
    return pl.pallas_call(
        final_kernel,
        out_shape=jax.ShapeDtypeStruct((clusters, width, conductors), F32),
        in_specs=[SMEM] * 2 + [VMEM] * 2,
        out_specs=pl.BlockSpec(memory_space=pl.ANY),
        scratch_shapes=[
            pltpu.VMEM((clusters, width, conductors), F32),
            pltpu.SemaphoreType.DMA((clusters,)),
        ],
        compiler_params=PARAMS,
        name="finish",
    )(order, starts, base, returned)


def pair_lists(first, second, count, clusters, entries):
    live = jnp.arange(first.shape[0], dtype=jnp.int32) < count
    own = second < clusters
    a = jnp.where(own, jnp.minimum(first, second), first)
    b = jnp.where(own, jnp.maximum(first, second), second)
    key = jnp.where(live, b * clusters + a, -1)
    keys = jnp.arange(entries * clusters, dtype=jnp.int32)
    times = jnp.sum((keys[:, None] == key[None, :]).astype(F32), axis=1)
    times = jnp.where(keys % clusters == keys // clusters, 0.5 * times, times)
    lists = []
    for lo, hi in ((0, clusters * clusters), (clusters * clusters, entries * clusters)):
        part = times[lo:hi]
        held = part > 0
        spots = jnp.arange(hi - lo, dtype=jnp.int32)
        rank = jnp.sum(((spots[None, :] < spots[:, None]) & held[None, :]).astype(jnp.int32), axis=1)
        slots = jnp.arange(256 + 2 * GROUP, dtype=jnp.int32)
        match = (rank[None, :] == slots[:, None]) & held[None, :]
        total = jnp.sum(held.astype(jnp.int32))
        last = jnp.max(jnp.where(held, spots, 0))
        table = jnp.sum(jnp.where(match, spots[None, :], 0), axis=1)
        table = jnp.where(slots < total, table, last)
        weight = jnp.sum(jnp.where(match, part[None, :], 0.0), axis=1)
        lists.append((total.reshape(1), table, weight))
    return lists


def shards(
    charges,
    panel_coords,
    cluster_basis,
    trans_leaf,
    trans_pair,
    trans_quad,
    skel_points,
    send_slots,
    pair_first,
    pair_second,
    pair_count,
    far_one,
    far_two,
    far_three,
):
    clusters, _, width = panel_coords.shape
    conductors = charges.shape[1]
    peers = lax.axis_size("dev")
    blocks = charges.reshape(clusters, width, conductors)
    axes = jnp.swapaxes(panel_coords, 0, 1).astype(F32)
    qt, fa, fb, outgoing = prep(send_slots, blocks, axes)
    incoming = lax.all_to_all(outgoing, "dev", split_axis=0, concat_axis=0, tiled=True)

    def folded(mat):
        return jnp.concatenate([mat[0, :16], mat[0, 16:]], axis=1)

    points_row = skel_points.reshape(1, -1)
    lists_row = jnp.concatenate([far_two, far_three], axis=1).astype(BF16)
    rest = jnp.concatenate(
        [
            jnp.concatenate([folded(trans_pair), folded(trans_quad)], axis=1),
            jnp.pad(points_row, ((0, 0), (0, conductors - points_row.shape[1]))),
            jnp.pad(lists_row, ((0, 14), (0, conductors - lists_row.shape[1]))),
        ],
        axis=0,
    )
    nodes = gather_nodes(blocks, cluster_basis, trans_leaf, rest)

    own_list, remote_list = pair_lists(pair_first, pair_second, pair_count[0], clusters, clusters + peers)
    acc = own_near(*own_list, qt, fa, fb)
    back = reply(*remote_list, qt, fa, incoming)
    returned = lax.all_to_all(back, "dev", split_axis=0, concat_axis=0, tiled=True)
    acc = remote_near(*remote_list, fa, incoming, acc)

    z, d = lax.axis_index("group"), lax.axis_index("dev")
    x, y, c = d // 8, d // 2 % 4, d % 2

    def place(owner):
        z, d = owner // 32, owner % 32
        return ((d % 2 * 4 + z) * 4 + d // 2 % 4) * 4 + d // 8

    info = nodes[:, 48:50, :].reshape(2, 4, 4, 4, 2, conductors)
    quad = lax.dynamic_slice(info, (0, z, y // 2 * 2, x, 0, 0), (2, 1, 2, 1, 2, conductors))
    quad = jnp.swapaxes(quad.reshape(2, 2, 2, conductors), 0, 1)
    quad_lists = quad[:, :, 1, :16].astype(jnp.int32)
    pair_list = lax.dynamic_index_in_dim(quad_lists[..., :8], y % 2, axis=0, keepdims=False)
    ids = jnp.concatenate(
        [
            place(far_one[0]),
            place(2 * pair_list.reshape(-1)),
            place(4 * quad_lists[..., 8:].reshape(-1)),
            place(z * peers + d).reshape(1),
        ]
    )
    quad_points = quad[:, :, 0, :96].astype(F32).reshape(2, 2, 3, 32)
    pair_points = 0.5 * (quad_points[:, 0] + quad_points[:, 1])
    own_points = jnp.stack(
        [
            skel_points[0].astype(F32),
            lax.dynamic_index_in_dim(pair_points, y % 2, axis=0, keepdims=False),
            0.5 * (pair_points[0] + pair_points[1]),
        ]
    )
    own_points = jnp.repeat(jnp.swapaxes(own_points, 1, 2), 32, axis=2)
    own_points = jnp.pad(own_points, ((0, 0), (0, 0), (0, 32)))
    leaf = far_field(ids, own_points, nodes, trans_leaf)
    base = base_sum(acc, leaf, cluster_basis)

    slots = send_slots[:, 0]
    spots = jnp.arange(peers, dtype=jnp.int32)
    rank = jnp.sum(
        (slots[None, :] < slots[:, None])
        | ((slots[None, :] == slots[:, None]) & (spots[None, :] < spots[:, None])),
        axis=1,
        dtype=jnp.int32,
    )
    order = jnp.sum(jnp.where(rank[None, :] == spots[:, None], spots[None, :], 0), axis=1)
    edges = jnp.arange(clusters + 1, dtype=jnp.int32)
    starts = jnp.sum(slots[None, :] < edges[:, None], axis=1, dtype=jnp.int32)
    out = finish(order, starts, base, returned)
    return out.reshape(clusters * width, conductors)


def solution(mesh):
    owners = ("group", "dev")
    rows, block, flat = P(owners, None), P(owners, None, None), P(owners)
    placed = (rows, *(block,) * 6, rows, *(flat,) * 3, *(rows,) * 3)
    return jax.shard_map(shards, mesh=mesh, in_specs=placed, out_specs=rows, check_vma=False)
```

time: 141 us -> 151 us (1.071)
  the two profiles are of different devices: /device:TPU:7 before, /device:TPU:16 now
where the time goes in v2:
time: 151 us
  Pallas kernels  120 us (79%)
  other arithmetic  13 us (9%)
  starting transfers between devices  12.6 us (8%)
  local copies, waits for them, and re-layouts  4.15 us (3%)
    pallas_call x1, Pallas kernels, gather_nodes(): pl.pallas_call(gather_kernel, out_shape=jax.ShapeDtypeStruct((128, rank +...  49.8 us
    pallas_call x1, Pallas kernels, remote_near(): pl.pallas_call(remote_kernel, out_shape=jax.ShapeDtypeStruct(acc.shape, F...  18 us
    pallas_call x1, Pallas kernels, reply(): pl.pallas_call(reply_kernel, out_shape=jax.ShapeDtypeStruct((peers, condu...  15.7 us
    pallas_call x1, Pallas kernels, own_near(): pl.pallas_call(own_kernel, out_shape=jax.ShapeDtypeStruct(qt.shape, F32),...  11.2 us
    pallas_call x1, Pallas kernels, far_field(): pl.pallas_call(far_kernel, out_shape=jax.ShapeDtypeStruct((clusters, node...  9.55 us
    all_to_all x1, starting transfers between devices, shards(): lax.all_to_all(outgoing, 'dev', split_axis=0, concat_axis=0, tiled=True)  7.61 us
    pallas_call x1, Pallas kernels, finish(): pl.pallas_call(final_kernel, out_shape=jax.ShapeDtypeStruct((clusters, wi...  5.47 us
    pallas_call x1, Pallas kernels, base_sum(): pl.pallas_call(base_kernel, out_shape=jax.ShapeDtypeStruct(acc.shape, F32...  5.28 us
  transfers between devices with their start and end apart: 2, of which 0 were waited for; matrix products, arithmetic and copies ran while one was open for 9% of the time, Pallas kernels for 62%

profile of v2, /device:TPU:16, one launch (start us, length us, event | category | flops | bytes accessed | tf_op | source)
XLA Modules:
  0.0 150.9 jit_solution(8036884485930294648)
XLA Ops:
  0.0 1.3 copy.27.slots
  1.3 1.4 convert_bitcast_fusion.axes
  2.7 5.0 %prep.1 = (bf16[16,128,256]{2,1,0:T(8,128)(2,1)}, bf16[16,256,16]{2,1,0:T(8,128)(2,1)}, bf16[16,16,256]{2,1,0:T(8,128)(2,1)}, bf16[32,144,256]{2,1,0:T(8,128)(2,1)}) custom-call(s32[32,1]{1,0:T(8,128)} %copy.27.slots, bf16[16,256,128]{2,1,0:T(8,128)(2,1)} %bitcast.46, f32[3,16,256]{2,1,0:T(8,128)} %convert_bitcast_fusion.axes), custom_call_target="tpu_custom_call" | custom-call | tf_op jit(solution)/shard_map/prep/pallas_call | solution.py:80
  7.7 0.0 copy-start.10
  7.7 0.0 copy-start.9
  7.8 0.0 copy-start.8
  7.8 0.0 copy-start.11
  7.8 0.0 copy-start.5
  7.8 0.0 copy-start.6
  7.8 0.0 copy-start.3
  7.9 7.6 %all-to-all-start = ((bf16[32,144,256]{2,1,0:T(8,128)(2,1)}), bf16[32,144,256]{2,1,0:T(8,128)(2,1)}, u32[]{:S(2)}, u32[]{:S(2)}) async-start(bf16[32,144,256]{2,1,0:T(8,128)(2,1)} %get-tuple-element.10), calls=%async_computation | async-start | bytes 4718592 | tf_op jit(solution)/shard_map/all_to_all | solution.py:469
  15.6 0.7 convert_reduce_fusion.4.starts
  16.3 0.8 convert_reduce_fusion.3
  17.1 0.1 reshape.89
  17.9 0.2 convert_reduce_fusion.1
  18.1 0.1 fusion.22
  18.2 0.1 fusion.9.rest
  18.3 49.8 %gather_nodes.1.nodes = bf16[128,64,128]{2,1,0:T(8,128)(2,1)S(1)} custom-call(bf16[16,256,128]{2,1,0:T(8,128)(2,1)S(1)} %bitcast.47, bf16[16,32,256]{2,1,0:T(8,128)(2,1)S(1)} %copy-done.2, bf16[16,32,32]{2,1,0:T(8,128)(2,1)S(1)} %copy-done.3, bf16[32,128]{1,0:T(8,128)(2,1)S(1)} %fusion.9.rest), custom_call_target="tpu_custom_call" | custom-call | flops 12884901888 | bytes 4194304 | tf_op jit(solution)/shard_map/gather_nodes/pallas_call | solution.py:149
  68.1 0.1 slice.53
  68.3 1.3 select_reduce_fusion.4.order
  69.7 0.1 fusion.43
  69.7 0.1 mul.88
  69.8 0.1 mul.93
  69.9 0.1 reshape.96
  70.0 0.6 select_reduce_fusion.6
  70.7 0.1 convert_reduce_fusion.2
  70.8 0.2 select_reduce_fusion.3
  71.0 0.8 select_reduce_fusion.2.weight
  71.7 0.7 select_reduce_fusion.5
  72.4 0.1 convert_reduce_fusion
  72.6 0.2 select_reduce_fusion.1
  72.8 0.8 select_reduce_fusion.weight
  73.6 0.7 multiply_add_fusion.2
  74.3 1.7 %fusion.27.table = s32[272]{0:T(512)} fusion(s32[272]{0:T(512)S(1)} %select_reduce_fusion.3, s32[]{:T(128)} %get-tuple-element.13, s32[]{:T(128)} %get-tuple-element.14), kind=kLoop, calls=%fused_computation.76 | loop fusion | flops 544 | bytes 2184 | tf_op jit(solution)/shard_map/jit(_where)/select_n | solution.py:441
  76.0 1.8 %fusion.26.table = s32[272]{0:T(512)} fusion(s32[272]{0:T(512)S(1)} %select_reduce_fusion.1, s32[]{:T(128)} %get-tuple-element.15, s32[]{:T(128)} %get-tuple-element.16), kind=kLoop, calls=%fused_computation.75 | loop fusion | flops 544 | bytes 2184 | tf_op jit(solution)/shard_map/jit(_where)/select_n | solution.py:441
  77.9 15.7 %reply.1 = bf16[32,128,256]{2,1,0:T(8,128)(2,1)} custom-call(s32[1]{0:T(128)} %bitcast.2.count, s32[272]{0:T(512)} %fusion.26.table, f32[272]{0:T(512)} %select_reduce_fusion.weight, bf16[16,128,256]{2,1,0:T(8,128)(2,1)} %get-tuple-element.11.qt, bf16[16,256,16]{2,1,0:T(8,128)(2,1)} %get-tuple-element.9.fa, bf16[32,144,256]{2,1,0:T(8,128)(2,1)} %all-to-all-done.incoming), custom_call_target="tpu_custom_call" | custom-call | flops 6442450944 | bytes 8388608 | tf_op jit(solution)/shard_map/reply/pallas_call | solution.py:241
  93.6 5.0 %all-to-all-start.1 = ((bf16[32,128,256]{2,1,0:T(8,128)(2,1)}), bf16[32,128,256]{2,1,0:T(8,128)(2,1)S(1)}, u32[]{:S(2)}, u32[]{:S(2)}) async-start(bf16[32,128,256]{2,1,0:T(8,128)(2,1)} %reply.1), calls=%async_computation.1 | async-start | bytes 4194304 | tf_op jit(solution)/shard_map/all_to_all | solution.py:489
  98.5 0.6 pad_add_fusion.ids
  99.1 0.1 copy.30
  99.2 0.2 broadcast_in_dim.117
  99.4 0.1 reshape.93
  99.5 0.6 pad.14.own_points
  100.1 9.5 %far_field.1.leaf = bf16[16,128,32]{2,1,0:T(8,128)(2,1)} custom-call(s32[57]{0:T(128)} %pad_add_fusion.ids, f32[3,32,128]{2,1,0:T(8,128)} %pad.14.own_points, bf16[128,64,128]{2,1,0:T(8,128)(2,1)} %copy-done.1, bf16[16,32,32]{2,1,0:T(8,128)(2,1)} %trans.3), custom_call_target="tpu_custom_call" | custom-call | flops 6442450944 | bytes 4194304 | tf_op jit(solution)/shard_map/far_field/pallas_call | solution.py:354
  109.7 11.2 %own_near.1.acc_in = f32[16,128,256]{2,1,0:T(8,128)} custom-call(s32[1]{0:T(128)} %bitcast.5.count, s32[272]{0:T(512)} %fusion.27.table, f32[272]{0:T(512)} %select_reduce_fusion.2.weight, bf16[16,128,256]{2,1,0:T(8,128)(2,1)} %get-tuple-element.11.qt, bf16[16,256,16]{2,1,0:T(8,128)(2,1)} %get-tuple-element.9.fa, bf16[16,16,256]{2,1,0:T(8,128)(2,1)} %get-tuple-element.12.fb), custom_call_target="tpu_custom_call" | custom-call | flops 6442450944 | bytes 4194304 | tf_op jit(solution)/shard_map/own_near/pallas_call | solution.py:198
  120.9 18.0 %remote_near.1.acc = f32[16,128,256]{2,1,0:T(8,128)} custom-call(s32[1]{0:T(128)} %bitcast.2.count, s32[272]{0:T(512)} %fusion.26.table, f32[272]{0:T(512)} %select_reduce_fusion.weight, bf16[16,256,16]{2,1,0:T(8,128)(2,1)} %get-tuple-element.9.fa, bf16[32,144,256]{2,1,0:T(8,128)(2,1)} %all-to-all-done.incoming, f32[16,128,256]{2,1,0:T(8,128)} %own_near.1.acc_in), custom_call_target="tpu_custom_call" | custom-call | flops 6442450944 | bytes 8388608 | tf_op jit(solution)/shard_map/remote_near/pallas_call | solution.py:280
  138.9 5.3 %base_sum.1.base = f32[16,128,256]{2,1,0:T(8,128)} custom-call(f32[16,128,256]{2,1,0:T(8,128)} %remote_near.1.acc, bf16[16,128,32]{2,1,0:T(8,128)(2,1)} %far_field.1.leaf, bf16[16,32,256]{2,1,0:T(8,128)(2,1)} %basis.3), custom_call_target="tpu_custom_call" | custom-call | flops 2147483648 | bytes 4194304 | tf_op jit(solution)/shard_map/base_sum/pallas_call | solution.py:375
  144.2 1.3 copy-done.4
  145.5 5.5 %finish.1 = f32[16,256,128]{2,1,0:T(8,128)} custom-call(s32[32]{0:T(128)} %select_reduce_fusion.4.order, s32[17]{0:T(128)} %convert_reduce_fusion.4.starts, f32[16,128,256]{2,1,0:T(8,128)} %base_sum.1.base, bf16[32,128,256]{2,1,0:T(8,128)(2,1)} %copy-done.4), custom_call_target="tpu_custom_call" | custom-call | tf_op jit(solution)/shard_map/finish/pallas_call | solution.py:407
  (40 shorter events, 0.2 us)
Async XLA Ops:
  7.7 7.9 %copy-start.10 = (s32[32,1]{0,1:T(1,128)S(1)}, s32[32,1]{0,1:T(1,128)}, u32[]{:S(2)}) copy-start(s32[32,1]{0,1:T(1,128)} %param.21) | copy-start | bytes 388
  7.7 9.3 %copy-start.9 = (bf16[1,3,32]{2,1,0:T(4,128)(2,1)S(1)}, bf16[1,3,32]{2,1,0:T(4,128)(2,1)}, u32[]{:S(2)}) copy-start(bf16[1,3,32]{2,1,0:T(4,128)(2,1)} %param.20) | copy-start | bytes 580
  7.7 10.1 %copy-start.7 = (s32[256]{0:T(256)S(1)}, s32[256]{0:T(256)}, u32[]{:S(2)}) copy-start(s32[256]{0:T(256)} %param.23) | copy-start | bytes 3076
  7.8 10.1 %copy-start.8 = (s32[256]{0:T(256)S(1)}, s32[256]{0:T(256)}, u32[]{:S(2)}) copy-start(s32[256]{0:T(256)} %param.22) | copy-start | bytes 3076
  7.8 10.3 %copy-start.11 = (s32[1,8]{1,0:T(1,128)S(1)}, s32[1,8]{1,0:T(1,128)}, u32[]{:S(2)}) copy-start(s32[1,8]{1,0:T(1,128)} %param.26) | copy-start | bytes 100
  7.8 10.3 %copy-start.12 = (s32[1,8]{1,0:T(1,128)S(1)}, s32[1,8]{1,0:T(1,128)}, u32[]{:S(2)}) copy-start(s32[1,8]{1,0:T(1,128)} %param.27) | copy-start | bytes 100
  7.8 10.4 %copy-start.5 = (bf16[1,32,32]{2,1,0:T(8,128)(2,1)S(1)}, bf16[1,32,32]{2,1,0:T(8,128)(2,1)}, u32[]{:S(2)}) copy-start(bf16[1,32,32]{2,1,0:T(8,128)(2,1)} %param.19) | copy-start | bytes 6148
  7.8 10.4 %copy-start.6 = (bf16[1,32,32]{2,1,0:T(8,128)(2,1)S(1)}, bf16[1,32,32]{2,1,0:T(8,128)(2,1)}, u32[]{:S(2)}) copy-start(bf16[1,32,32]{2,1,0:T(8,128)(2,1)} %param.18) | copy-start | bytes 6148
  7.8 10.5 %copy-start = (bf16[4096,128]{1,0:T(8,128)(2,1)S(1)}, bf16[4096,128]{1,0:T(8,128)(2,1)}, u32[]{:S(2)}) copy-start(bf16[4096,128]{1,0:T(8,128)(2,1)} %param.14) | copy-start | bytes 3145732
  7.8 10.5 %copy-start.2 = (bf16[16,32,256]{2,1,0:T(8,128)(2,1)S(1)}, bf16[16,32,256]{2,1,0:T(8,128)(2,1)}, u32[]{:S(2)}) copy-start(bf16[16,32,256]{2,1,0:T(8,128)(2,1)} %basis.3) | copy-start | bytes 786436
  7.8 10.4 %copy-start.3 = (bf16[16,32,32]{2,1,0:T(8,128)(2,1)S(1)}, bf16[16,32,32]{2,1,0:T(8,128)(2,1)}, u32[]{:S(2)}) copy-start(bf16[16,32,32]{2,1,0:T(8,128)(2,1)} %trans.3) | copy-start | bytes 98308
  7.9 70.0 %all-to-all-start = ((bf16[32,144,256]{2,1,0:T(8,128)(2,1)}), bf16[32,144,256]{2,1,0:T(8,128)(2,1)}, u32[]{:S(2)}, u32[]{:S(2)}) async-start(bf16[32,144,256]{2,1,0:T(8,128)(2,1)} %get-tuple-element.10), calls=%async_computation | async-start | bytes 4718592 | tf_op jit(solution)/shard_map/all_to_all | solution.py:469
  68.1 25.4 %copy-start.1 = (bf16[128,64,128]{2,1,0:T(8,128)(2,1)}, bf16[128,64,128]{2,1,0:T(8,128)(2,1)S(1)}, u32[]{:S(2)}) copy-start(bf16[128,64,128]{2,1,0:T(8,128)(2,1)S(1)} %gather_nodes.1.nodes) | copy-start | bytes 6291460
  93.6 50.6 %all-to-all-start.1 = ((bf16[32,128,256]{2,1,0:T(8,128)(2,1)}), bf16[32,128,256]{2,1,0:T(8,128)(2,1)S(1)}, u32[]{:S(2)}, u32[]{:S(2)}) async-start(bf16[32,128,256]{2,1,0:T(8,128)(2,1)} %reply.1), calls=%async_computation.1 | async-start | bytes 4194304 | tf_op jit(solution)/shard_map/all_to_all | solution.py:489
  144.2 1.3 copy-start.4

commit v3 on v2

--- a/solution.py
+++ b/solution.py
@@ -16,7 +16,7 @@
 VMEM = pl.BlockSpec(memory_space=pltpu.VMEM)
 SMEM = pl.BlockSpec(memory_space=pltpu.SMEM)
 MESH = pl.DeviceIdType.MESH
-PARAMS = pltpu.CompilerParams(vmem_limit_bytes=56 << 20)
+PARAMS = pltpu.CompilerParams(vmem_limit_bytes=20 << 20)
 
 
 def dot(left, right, dims=((1,), (0,))):
@@ -35,8 +35,20 @@
     return high.astype(F32), mid.astype(F32), (rest - mid.astype(F32))
 
 
-def prep_kernel(slots, charges, axes, qt, fa, fb, outgoing, rows_a, rows_b, sems):
+def prep_kernel(
+    slots, charges, axes, basis, trans, rest, qt, fa, fb, outgoing, rows_a, rows_b, node, sems
+):
     clusters = charges.shape[0]
+    conductors = charges.shape[2]
+    total = jnp.zeros((trans.shape[1], conductors), F32)
+    for i in range(clusters):
+        leaf = dot(basis[i], charges[i]).astype(BF16)
+        total += dot(trans[i], leaf)
+    top = total.astype(BF16)
+    node[:16, :conductors] = top[:16]
+    node[:16, conductors:] = top[16:]
+    node[16:, :conductors] = rest[:16]
+    node[16:, conductors:] = rest[16:]
     x = [axes[d] for d in range(3)]
     norm = x[0] * x[0] + x[1] * x[1] + x[2] * x[2]
     one = jnp.ones_like(norm)
@@ -56,6 +68,7 @@
         return (
             pltpu.make_async_copy(qt.at[c], outgoing.at[h, pl.ds(0, split)], sems.at[h, 0]),
             pltpu.make_async_copy(fb.at[c], outgoing.at[h, pl.ds(split, FEAT)], sems.at[h, 1]),
+            pltpu.make_async_copy(node, outgoing.at[h, pl.ds(split + FEAT, 32)], sems.at[h, 2]),
         )
 
     def send(h, carry):
@@ -74,7 +87,7 @@
     lax.fori_loop(0, outgoing.shape[0], wait, 0)
 
 
-def prep(slots, charges, axes):
+def prep(slots, charges, axes, basis, trans, rest):
     clusters, width, conductors = charges.shape
     peers = slots.shape[0]
     return pl.pallas_call(
@@ -83,81 +96,15 @@
             jax.ShapeDtypeStruct((clusters, conductors, width), BF16),
             jax.ShapeDtypeStruct((clusters, width, FEAT), BF16),
             jax.ShapeDtypeStruct((clusters, FEAT, width), BF16),
-            jax.ShapeDtypeStruct((peers, conductors + FEAT, width), BF16),
+            jax.ShapeDtypeStruct((peers, conductors + FEAT + 32, width), BF16),
         ),
-        in_specs=[SMEM] + [VMEM] * 2,
+        in_specs=[SMEM] + [VMEM] * 5,
         out_specs=(VMEM, VMEM, VMEM, pl.BlockSpec(memory_space=pl.ANY)),
         scratch_shapes=[pltpu.VMEM((clusters, FEAT, width), F32)] * 2
-        + [pltpu.SemaphoreType.DMA((peers, 2))],
+        + [pltpu.VMEM((32, width), BF16), pltpu.SemaphoreType.DMA((peers, 3))],
         compiler_params=PARAMS,
         name="prep",
-    )(slots, charges, axes)
-
-
-def gather_kernel(charges, basis, trans, rest, nodes, send_sem, recv_sem):
-    z, d = lax.axis_index("group"), lax.axis_index("dev")
-    x, y, c = d // 8, lax.rem(d // 2, 4), lax.rem(d, 2)
-
-    def place(x, y, z, c):
-        return {"group": z, "dev": (x * 4 + y) * 2 + c}
-
-    def turn(i, k):
-        return lax.rem(i + k, 4)
-
-    stages = (
-        (((c * 4 + z) * 4 + y) * 4 + x, 1, [place(turn(x, k), y, z, c) for k in (1, 2, 3)]),
-        (((c * 4 + z) * 4 + y) * 4, 4, [place(x, turn(y, k), z, c) for k in (1, 2, 3)]),
-        ((c * 4 + z) * 16, 16, [place(x, y, turn(z, k), c) for k in (1, 2, 3)]),
-        (c * 64, 64, [place(x, y, z, 1 - c)]),
-    )
-    barrier = pltpu.get_barrier_semaphore()
-    for _, _, peers in stages:
-        for peer in peers:
-            pl.semaphore_signal(barrier, inc=1, device_id=peer, device_id_type=MESH)
-
-    rank = trans.shape[1]
-    total = jnp.zeros((rank, charges.shape[2]), F32)
-    for i in range(trans.shape[0]):
-        leaf = dot(basis[i], charges[i]).astype(BF16)
-        total += dot(trans[i], leaf)
-    me = stages[0][0]
-    nodes[me, :rank, :] = total.astype(BF16)
-    nodes[me, rank:, :] = rest[...]
-    pl.semaphore_wait(barrier, 10)
-
-    for level, (start, length, peers) in enumerate(stages):
-        held = nodes.at[pl.ds(start, length)]
-        copies = [
-            pltpu.make_async_remote_copy(
-                src_ref=held,
-                dst_ref=held,
-                send_sem=send_sem.at[level, k],
-                recv_sem=recv_sem.at[level, k],
-                device_id=peer,
-                device_id_type=MESH,
-            )
-            for k, peer in enumerate(peers)
-        ]
-        for copy in copies:
-            copy.start()
-        for copy in copies:
-            copy.wait()
-
-
-def gather_nodes(charges, basis, trans, rest):
-    rank, conductors = trans.shape[1], charges.shape[2]
-    return pl.pallas_call(
-        gather_kernel,
-        out_shape=jax.ShapeDtypeStruct((128, rank + rest.shape[0], conductors), BF16),
-        in_specs=[VMEM] * 4,
-        out_specs=VMEM,
-        scratch_shapes=[pltpu.SemaphoreType.DMA((4, 3))] * 2,
-        compiler_params=pltpu.CompilerParams(
-            vmem_limit_bytes=32 << 20, collective_id=0, has_side_effects=True
-        ),
-        cost_estimate=pl.CostEstimate(flops=12 << 30, bytes_accessed=4 << 20, transcendentals=0),
-        name="gather_nodes",
-    )(charges, basis, trans, rest)
+    )(slots, charges, axes, basis, trans, rest)
 
 
 def tiles(count, table, weight, fa, feat, left, right, add_first, add_second, kbuf):
@@ -213,7 +160,7 @@
 
     def tile(j):
         key = table[j]
-        s = dot(fa[lax.rem(key, 16)], incoming[key // 16, conductors:, :])
+        s = dot(fa[lax.rem(key, 16)], incoming[key // 16, conductors : conductors + FEAT, :])
         return lax.rsqrt(s.astype(BF16)) * weight[j].astype(BF16)
 
     for g in range(GROUP):
@@ -256,7 +203,7 @@
 
     def tile(j):
         key = table[j]
-        s = dot(fa[lax.rem(key, 16)], incoming[key // 16, conductors:, :])
+        s = dot(fa[lax.rem(key, 16)], incoming[key // 16, conductors : conductors + FEAT, :])
         return lax.rsqrt(s.astype(BF16)) * weight[j].astype(BF16)
 
     for g in range(GROUP):
@@ -293,15 +240,16 @@
     rank = 32
 
     def skel(n):
-        return nodes[n, :rank, :]
+        rows = nodes[n, :16, :]
+        return jnp.concatenate([rows[:, :128], rows[:, 128:]], axis=0)
 
     def transfer(n, which):
-        rows = nodes[n, rank : rank + 16, :]
+        rows = nodes[n, 16:, :128]
         lo = 64 * which
         return jnp.concatenate([rows[:, lo : lo + 32], rows[:, lo + 32 : lo + 64]], axis=0)
 
     def points(n):
-        return nodes[n, rank + 16 : rank + 32, :].astype(F32)[:1]
+        return nodes[n, 16:, 128:].astype(F32)[:1]
 
     def kernel_tile(mine, theirs):
         gap = mine - theirs
@@ -313,20 +261,20 @@
         return dot(tile[0], source) + dot(tile[1], source)
 
     mine = [own_points[level] for level in range(3)]
-    zero = jnp.zeros((rank, nodes.shape[2]), F32)
+    zero = jnp.zeros((rank, 128), F32)
 
     def one(f, total):
         n = ids[f]
         return total + apply(kernel_tile(mine[0], points(n)), skel(n))
 
     def two(f, total):
-        n, m = ids[8 + f], ids[8 + f] + 64
+        n, m = ids[8 + f], lax.rem(ids[8 + f] + 64, 128)
         source = dot(transfer(n, 0), skel(n)) + dot(transfer(m, 0), skel(m))
         theirs = 0.5 * (points(n) + points(m))
         return total + apply(kernel_tile(mine[1], theirs), source.astype(BF16))
 
     def three(f, total):
-        n = [ids[24 + f] + step for step in (0, 64, 4, 68)]
+        n = [lax.rem(ids[24 + f] + step, 128) for step in (0, 64, 1, 65)]
         terms = [dot(transfer(i, 1), skel(i)) for i in n]
         source = (terms[0] + terms[1]) + (terms[2] + terms[3])
         left = 0.5 * (points(n[0]) + points(n[1]))
@@ -353,7 +301,7 @@
     clusters, rank, _ = trans.shape
     return pl.pallas_call(
         far_kernel,
-        out_shape=jax.ShapeDtypeStruct((clusters, nodes.shape[2], rank), BF16),
+        out_shape=jax.ShapeDtypeStruct((clusters, 128, rank), BF16),
         in_specs=[SMEM] + [VMEM] * 3,
         out_specs=VMEM,
         scratch_shapes=[pltpu.VMEM((8, 128), F32)],
@@ -465,23 +413,35 @@
     peers = lax.axis_size("dev")
     blocks = charges.reshape(clusters, width, conductors)
     axes = jnp.swapaxes(panel_coords, 0, 1).astype(F32)
-    qt, fa, fb, outgoing = prep(send_slots, blocks, axes)
-    incoming = lax.all_to_all(outgoing, "dev", split_axis=0, concat_axis=0, tiled=True)
 
     def folded(mat):
         return jnp.concatenate([mat[0, :16], mat[0, 16:]], axis=1)
 
-    points_row = skel_points.reshape(1, -1)
-    lists_row = jnp.concatenate([far_two, far_three], axis=1).astype(BF16)
+    def padded(row):
+        return jnp.pad(row, ((0, 0), (0, conductors - row.shape[1])))
+
     rest = jnp.concatenate(
         [
             jnp.concatenate([folded(trans_pair), folded(trans_quad)], axis=1),
-            jnp.pad(points_row, ((0, 0), (0, conductors - points_row.shape[1]))),
-            jnp.pad(lists_row, ((0, 14), (0, conductors - lists_row.shape[1]))),
+            padded(skel_points.reshape(1, -1)),
+            padded(jnp.concatenate([far_two, far_three], axis=1).astype(BF16)),
+            jnp.zeros((14, conductors), BF16),
         ],
         axis=0,
     )
-    nodes = gather_nodes(blocks, cluster_basis, trans_leaf, rest)
+    qt, fa, fb, outgoing = prep(send_slots, blocks, axes, cluster_basis, trans_leaf, rest)
+    incoming = lax.all_to_all(outgoing, "dev", split_axis=0, concat_axis=0, tiled=True)
+
+    z, d = lax.axis_index("group"), lax.axis_index("dev")
+    xy, c = d // 2, d % 2
+    same = incoming.reshape(peers // 2, 2, -1, width)[:, :, conductors + FEAT :]
+    same = lax.dynamic_index_in_dim(same, c, axis=1, keepdims=False)
+    along = [same]
+    for step in (1, 2, 3):
+        along.append(lax.ppermute(same, "group", [(i, (i + step) % 4) for i in range(4)]))
+    along = jnp.stack(along)
+    other = lax.ppermute(along, "dev", [(i, i ^ 1) for i in range(32)])
+    nodes = jnp.stack([along, other]).reshape(128, 32, width)
 
     own_list, remote_list = pair_lists(pair_first, pair_second, pair_count[0], clusters, clusters + peers)
     acc = own_near(*own_list, qt, fa, fb)
@@ -489,32 +449,27 @@
     returned = lax.all_to_all(back, "dev", split_axis=0, concat_axis=0, tiled=True)
     acc = remote_near(*remote_list, fa, incoming, acc)
 
-    z, d = lax.axis_index("group"), lax.axis_index("dev")
-    x, y, c = d // 8, d // 2 % 4, d % 2
-
     def place(owner):
-        z, d = owner // 32, owner % 32
-        return ((d % 2 * 4 + z) * 4 + d // 2 % 4) * 4 + d // 8
-
-    info = nodes[:, 48:50, :].reshape(2, 4, 4, 4, 2, conductors)
-    quad = lax.dynamic_slice(info, (0, z, y // 2 * 2, x, 0, 0), (2, 1, 2, 1, 2, conductors))
-    quad = jnp.swapaxes(quad.reshape(2, 2, 2, conductors), 0, 1)
-    quad_lists = quad[:, :, 1, :16].astype(jnp.int32)
-    pair_list = lax.dynamic_index_in_dim(quad_lists[..., :8], y % 2, axis=0, keepdims=False)
+        step = (z - owner // peers) % 4
+        return ((c ^ owner % 2) * 4 + step) * 16 + owner % peers // 2
+
+    quad = lax.dynamic_slice_in_dim(incoming[:, 160:162, 128:], d // 4 * 4, 4, axis=0)
+    quad_lists = quad[:, 1, :16].astype(jnp.int32)
+    pair_list = lax.dynamic_slice_in_dim(quad_lists[:, :8], d % 4 // 2 * 2, 2, axis=0)
     ids = jnp.concatenate(
         [
             place(far_one[0]),
             place(2 * pair_list.reshape(-1)),
-            place(4 * quad_lists[..., 8:].reshape(-1)),
-            place(z * peers + d).reshape(1),
+            place(4 * quad_lists[:, 8:].reshape(-1)),
+            xy.reshape(1),
         ]
     )
-    quad_points = quad[:, :, 0, :96].astype(F32).reshape(2, 2, 3, 32)
-    pair_points = 0.5 * (quad_points[:, 0] + quad_points[:, 1])
+    quad_points = quad[:, 0, :96].astype(F32).reshape(4, 3, 32)
+    pair_points = 0.5 * (quad_points[0::2] + quad_points[1::2])
     own_points = jnp.stack(
         [
             skel_points[0].astype(F32),
-            lax.dynamic_index_in_dim(pair_points, y % 2, axis=0, keepdims=False),
+            lax.dynamic_index_in_dim(pair_points, d % 4 // 2, axis=0, keepdims=False),
             0.5 * (pair_points[0] + pair_points[1]),
         ]
     )

time: 151 us -> 135 us (0.89)
  the two profiles are of different devices: /device:TPU:16 before, /device:TPU:37 now
where the time goes in v3:
time: 135 us; the launch traced here: 134 us
  Pallas kernels  58.6 us (43%)
  local copies, waits for them, and re-layouts  25.7 us (19%)
  starting transfers between devices  20.6 us (15%)
  waiting for transfers between devices  15.9 us (12%)
  other arithmetic  11.8 us (9%)
    unnamed x53, local copies, waits for them, and re-layouts  22.5 us
    all_to_all x1, waiting for transfers between devices, shards(): lax.all_to_all(outgoing, 'dev', split_axis=0, concat_axis=0, tiled=True)  15.9 us
    pallas_call x1, Pallas kernels, remote_near(): pl.pallas_call(remote_kernel, out_shape=jax.ShapeDtypeStruct(acc.shape, F...  15.3 us
    pallas_call x1, Pallas kernels, reply(): pl.pallas_call(reply_kernel, out_shape=jax.ShapeDtypeStruct((peers, condu...  13.2 us
    pallas_call x1, Pallas kernels, own_near(): pl.pallas_call(own_kernel, out_shape=jax.ShapeDtypeStruct(qt.shape, F32),...  8.93 us
    all_to_all x1, starting transfers between devices, shards(): lax.all_to_all(outgoing, 'dev', split_axis=0, concat_axis=0, tiled=True)  8.06 us
    pallas_call x1, Pallas kernels, far_field(): pl.pallas_call(far_kernel, out_shape=jax.ShapeDtypeStruct((clusters, 128,...  7.68 us
    pallas_call x1, Pallas kernels, prep(): pl.pallas_call(prep_kernel, out_shape=(jax.ShapeDtypeStruct((clusters, co...  7.5 us
  transfers between devices with their start and end apart: 6, of which 1 were waited for; matrix products, arithmetic and copies ran while one was open for 8% of the time, Pallas kernels for 35%

profile of v3, /device:TPU:37, one launch (start us, length us, event | category | flops | bytes accessed | tf_op | source)
XLA Modules:
  0.0 133.8 jit_solution(15384458678575618226)
XLA Ops:
  0.0 0.7 convert.10
  0.7 0.7 convert.9
  1.3 0.8 reshape.79
  2.1 0.7 convert_bitcast_fusion.axes
  2.8 0.7 copy.19.slots
  3.6 0.7 slice_bitcast_fusion.1
  4.5 1.2 copy-done.6
  5.8 0.9 copy-done.7
  6.7 0.9 copy-done.9
  7.6 7.5 %prep.1 = (bf16[16,128,256]{2,1,0:T(8,128)(2,1)S(1)}, bf16[16,256,16]{2,1,0:T(8,128)(2,1)S(1)}, bf16[16,16,256]{2,1,0:T(8,128)(2,1)S(1)}, bf16[32,176,256]{2,1,0:T(8,128)(2,1)S(1)}) custom-call(s32[32,1]{1,0:T(8,128)S(1)} %copy.19.slots, bf16[16,256,128]{2,1,0:T(8,128)(2,1)S(1)} %bitcast.53, f32[3,16,256]{2,1,0:T(8,128)S(1)} %convert_bitcast_fusion.axes, ...), custom_call_target="tpu_custom_call" | custom-call | tf_op jit(solution)/shard_map/prep/pallas_call | solution.py:93
  15.1 1.6 %copy-done.2 = bf16[32,176,256]{2,1,0:T(8,128)(2,1)} copy-done((bf16[32,176,256]{2,1,0:T(8,128)(2,1)}, bf16[32,176,256]{2,1,0:T(8,128)(2,1)S(1)}, u32[]{:S(2)}) %copy-start.2) | copy-done | bytes 2883608
  16.7 1.0 copy-done.11
  17.7 1.0 copy-done.15
  18.7 8.1 %all-to-all-start = ((bf16[32,176,256]{2,1,0:T(8,128)(2,1)}), bf16[32,176,256]{2,1,0:T(8,128)(2,1)S(1)}, u32[]{:S(2)}, u32[]{:S(2)}) async-start(bf16[32,176,256]{2,1,0:T(8,128)(2,1)} %copy-done.2), calls=%async_computation | async-start | bytes 5767168 | tf_op jit(solution)/shard_map/all_to_all | solution.py:433
  27.5 0.2 convert_reduce_fusion.1
  27.9 0.2 convert_reduce_fusion.3
  28.2 0.7 select_reduce_fusion.6
  29.3 0.6 select_reduce_fusion.5
  30.1 0.2 select_reduce_fusion.1
  30.3 0.2 select_reduce_fusion.weight
  30.6 1.2 fusion.22.table
  31.8 1.2 fusion.21.table
  33.1 1.2 copy-done.12
  34.3 1.2 copy-done.16
  35.5 8.9 %own_near.1.acc_in = f32[16,128,256]{2,1,0:T(8,128)S(1)} custom-call(s32[1]{0:T(128)} %bitcast.9.count, s32[272]{0:T(512)S(1)} %fusion.22.table, f32[272]{0:T(512)S(1)} %select_reduce_fusion.2.weight, bf16[16,128,256]{2,1,0:T(8,128)(2,1)S(1)} %copy-done.16, bf16[16,256,16]{2,1,0:T(8,128)(2,1)S(1)} %copy-done.12, bf16[16,16,256]{2,1,0:T(8,128)(2,1)S(1)} %get-tuple-element.12.fb), custom_call_target="tpu_custom_call" | custom-call | flops 6442450944 | bytes 4194304 | tf_op jit(solution)/shard_map/own_near/pallas_call | solution.py:145
  44.5 1.3 copy-done.18
  45.8 15.9 %all-to-all-done.incoming = bf16[32,176,256]{2,1,0:T(8,128)(2,1)S(1)} async-done(((bf16[32,176,256]{2,1,0:T(8,128)(2,1)}), bf16[32,176,256]{2,1,0:T(8,128)(2,1)S(1)}, u32[]{:S(2)}, u32[]{:S(2)}) %all-to-all-start) | async-done | bytes 2883616 | tf_op jit(solution)/shard_map/all_to_all | solution.py:433
  61.7 0.9 dynamic-slice_bitcast_fusion.1
  62.6 1.6 %collective-permute-start = (bf16[16,32,256]{2,1,0:T(8,128)(2,1)}, bf16[16,32,256]{2,1,0:T(8,128)(2,1)S(1)}, u32[]{:S(2)}, u32[]{:S(2)}) collective-permute-start(bf16[16,32,256]{2,1,0:T(8,128)(2,1)} %get-tuple-element.22), channel_id=1, source_target_pairs={{0,32},{32,64},{64,96},{96,0},{1,33},{33,65},{65,97},{97,1},{2,34}... | collective-permute-start | bytes 786440 | tf_op jit(solution)/shard_map/ppermute | solution.py:441
  64.3 1.1 collective-permute-start.1
  65.3 2.1 %collective-permute-start.2 = (bf16[16,32,256]{2,1,0:T(8,128)(2,1)}, bf16[16,32,256]{2,1,0:T(8,128)(2,1)}, u32[]{:S(2)}, u32[]{:S(2)}) collective-permute-start(bf16[16,32,256]{2,1,0:T(8,128)(2,1)} %get-tuple-element.22), channel_id=1, source_target_pairs={{0,96},{32,0},{64,32},{96,64},{1,97},{33,1},{65,33},{97,65},{2,98}... | collective-permute-start | bytes 786440 | tf_op jit(solution)/shard_map/ppermute | solution.py:441
  67.7 1.2 copy-done.13
  69.0 1.2 copy-done.17
  70.2 13.2 %reply.1 = bf16[32,128,256]{2,1,0:T(8,128)(2,1)S(1)} custom-call(s32[1]{0:T(128)} %bitcast.2.count, s32[272]{0:T(512)S(1)} %fusion.21.table, f32[272]{0:T(512)S(1)} %select_reduce_fusion.weight, bf16[16,128,256]{2,1,0:T(8,128)(2,1)S(1)} %copy-done.17, bf16[16,256,16]{2,1,0:T(8,128)(2,1)S(1)} %copy-done.13, bf16[32,176,256]{2,1,0:T(8,128)(2,1)S(1)} %all-to-all-done.incoming), custom_call_target="tpu_custom_call" | custom-call | flops 6442450944 | bytes 8388608 | tf_op jit(solution)/shard_map/reply/pallas_call | solution.py:188
  83.4 1.3 copy-done.3
  84.8 7.4 %all-to-all-start.1 = ((bf16[32,128,256]{2,1,0:T(8,128)(2,1)}), bf16[32,128,256]{2,1,0:T(8,128)(2,1)S(1)}, u32[]{:S(2)}, u32[]{:S(2)}) async-start(bf16[32,128,256]{2,1,0:T(8,128)(2,1)} %copy-done.3), calls=%async_computation.1 | async-start | bytes 4194304 | tf_op jit(solution)/shard_map/all_to_all | solution.py:449
  92.3 2.5 %fusion.36 = (bf16[1,4,16,32,256]{4,3,2,1,0:T(8,128)(2,1)}, bf16[4,16,32,256]{3,2,1,0:T(8,128)(2,1)}) fusion(bf16[1,16,32,256]{3,2,1,0:T(8,128)(2,1)} %bitcast.19, bf16[1,16,32,256]{3,2,1,0:T(8,128)(2,1)} %bitcast.18, bf16[1,16,32,256]{3,2,1,0:T(8,128)(2,1)S(1)} %bitcast.54, bf16[1,16,32,256]{3,2,1,0:T(8,128)(2,1)S(1)} %get-tuple-element.21), kind=kLoop, calls=%fused_computation.136 | loop fusion | flops 1572864 | bytes 3145728 | tf_op jit(solution)/shard_map/stack | solution.py:444
  94.8 0.4 collective-permute-start.3
  95.8 1.8 %copy-done.1 = bf16[32,176,256]{2,1,0:T(8,128)(2,1)S(1)} copy-done((bf16[32,176,256]{2,1,0:T(8,128)(2,1)S(1)}, bf16[32,176,256]{2,1,0:T(8,128)(2,1)}, u32[]{:S(2)}) %copy-start.1) | copy-done | bytes 2883608
  97.6 1.2 copy-done.14
  98.8 1.6 %copy-done.19 = f32[16,128,256]{2,1,0:T(8,128)S(1)} copy-done((f32[16,128,256]{2,1,0:T(8,128)S(1)}, f32[16,128,256]{2,1,0:T(8,128)}, u32[]{:S(2)}) %copy-start.19) | copy-done | bytes 2097176
  100.4 15.3 %remote_near.1.acc = f32[16,128,256]{2,1,0:T(8,128)S(1)} custom-call(s32[1]{0:T(128)} %bitcast.2.count, s32[272]{0:T(512)S(1)} %fusion.21.table, f32[272]{0:T(512)S(1)} %select_reduce_fusion.weight, bf16[16,256,16]{2,1,0:T(8,128)(2,1)S(1)} %copy-done.14, bf16[32,176,256]{2,1,0:T(8,128)(2,1)S(1)} %copy-done.1, f32[16,128,256]{2,1,0:T(8,128)S(1)} %copy-done.19), custom_call_target="tpu_custom_call" | custom-call | flops 6442450944 | bytes 8388608 | tf_op jit(solution)/shard_map/remote_near/pallas_call | solution.py:227
  115.8 1.5 %pad_maximum_fusion = bf16[2,4,16,32,256]{4,3,2,1,0:T(8,128)(2,1)S(1)} fusion(bf16[1,4,16,32,256]{4,3,2,1,0:T(8,128)(2,1)} %bitcast.21, bf16[1,4,16,32,256]{4,3,2,1,0:T(8,128)(2,1)S(1)} %copy-done.20), kind=kLoop, calls=%fused_computation | loop fusion | flops 1048576 | bytes 4194304 | tf_op jit(solution)/shard_map/stack | solution.py:444
  117.3 7.7 %far_field.1.leaf = bf16[16,128,32]{2,1,0:T(8,128)(2,1)S(1)} custom-call(s32[57]{0:T(128)S(1)} %pad_add_fusion.ids, f32[3,32,128]{2,1,0:T(8,128)S(1)} %pad.14.own_points, bf16[128,32,256]{2,1,0:T(8,128)(2,1)S(1)} %bitcast.52, bf16[16,32,32]{2,1,0:T(8,128)(2,1)S(1)} %copy-done.10), custom_call_target="tpu_custom_call" | custom-call | flops 6442450944 | bytes 4194304 | tf_op jit(solution)/shard_map/far_field/pallas_call | solution.py:302
  125.0 2.2 %base_sum.1.base = f32[16,128,256]{2,1,0:T(8,128)S(1)} custom-call(f32[16,128,256]{2,1,0:T(8,128)S(1)} %remote_near.1.acc, bf16[16,128,32]{2,1,0:T(8,128)(2,1)S(1)} %far_field.1.leaf, bf16[16,32,256]{2,1,0:T(8,128)(2,1)S(1)} %copy-done.8), custom_call_target="tpu_custom_call" | custom-call | flops 2147483648 | bytes 4194304 | tf_op jit(solution)/shard_map/base_sum/pallas_call | solution.py:323
  127.1 1.3 copy-done.4
  128.4 1.6 %copy-done.5 = f32[16,128,256]{2,1,0:T(8,128)S(1)} copy-done((f32[16,128,256]{2,1,0:T(8,128)S(1)}, f32[16,128,256]{2,1,0:T(8,128)}, u32[]{:S(2)}) %copy-start.5) | copy-done | bytes 2097176
  130.0 3.8 %finish.1 = f32[16,256,128]{2,1,0:T(8,128)} custom-call(s32[32]{0:T(128)S(1)} %select_reduce_fusion.4.order, s32[17]{0:T(128)S(1)} %convert_reduce_fusion.4.starts, f32[16,128,256]{2,1,0:T(8,128)S(1)} %copy-done.5, bf16[32,128,256]{2,1,0:T(8,128)(2,1)S(1)} %all-to-all-done.1.returned), custom_call_target="tpu_custom_call" | custom-call | tf_op jit(solution)/shard_map/finish/pallas_call | solution.py:355
  (75 shorter events, 2.2 us)
Async XLA Ops:
  4.5 1.2 copy-start.6
  5.8 0.9 copy-start.7
  6.7 0.9 copy-start.9
  15.1 1.6 %copy-start.2 = (bf16[32,176,256]{2,1,0:T(8,128)(2,1)}, bf16[32,176,256]{2,1,0:T(8,128)(2,1)S(1)}, u32[]{:S(2)}) copy-start(bf16[32,176,256]{2,1,0:T(8,128)(2,1)S(1)} %get-tuple-element.10) | copy-start | bytes 8650756
  16.7 1.0 copy-start.11
  17.7 1.0 copy-start.15
  18.7 8.1 %copy-start.21 = (bf16[1,3,32]{2,1,0:T(4,128)(2,1)S(1)}, bf16[1,3,32]{2,1,0:T(4,128)(2,1)}, u32[]{:S(2)}) copy-start(bf16[1,3,32]{2,1,0:T(4,128)(2,1)} %param.20) | copy-start | bytes 580
  18.7 8.8 %copy-start.22 = (s32[256]{0:T(256)S(1)}, s32[256]{0:T(256)}, u32[]{:S(2)}) copy-start(s32[256]{0:T(256)} %param.23) | copy-start | bytes 3076
  18.7 8.8 %copy-start.23 = (s32[256]{0:T(256)S(1)}, s32[256]{0:T(256)}, u32[]{:S(2)}) copy-start(s32[256]{0:T(256)} %param.22) | copy-start | bytes 3076
  18.7 9.1 %copy-start.24 = (s32[32,1]{0,1:T(1,128)S(1)}, s32[32,1]{0,1:T(1,128)}, u32[]{:S(2)}) copy-start(s32[32,1]{0,1:T(1,128)} %param.21) | copy-start | bytes 388
  18.7 11.9 %copy-start.25 = (s32[1,8]{1,0:T(1,128)S(1)}, s32[1,8]{1,0:T(1,128)}, u32[]{:S(2)}) copy-start(s32[1,8]{1,0:T(1,128)} %param.25) | copy-start | bytes 100
  18.7 43.0 %all-to-all-start = ((bf16[32,176,256]{2,1,0:T(8,128)(2,1)}), bf16[32,176,256]{2,1,0:T(8,128)(2,1)S(1)}, u32[]{:S(2)}, u32[]{:S(2)}) async-start(bf16[32,176,256]{2,1,0:T(8,128)(2,1)} %copy-done.2), calls=%async_computation | async-start | bytes 5767168 | tf_op jit(solution)/shard_map/all_to_all | solution.py:433
  33.1 1.2 copy-start.12
  34.3 1.2 copy-start.16
  44.5 1.3 copy-start.18
  61.7 21.7 %copy-start = (bf16[32,176,256]{2,1,0:T(8,128)(2,1)}, bf16[32,176,256]{2,1,0:T(8,128)(2,1)S(1)}, u32[]{:S(2)}) copy-start(bf16[32,176,256]{2,1,0:T(8,128)(2,1)S(1)} %all-to-all-done.incoming) | copy-start | bytes 8650756
  62.6 29.6 %collective-permute-start = (bf16[16,32,256]{2,1,0:T(8,128)(2,1)}, bf16[16,32,256]{2,1,0:T(8,128)(2,1)S(1)}, u32[]{:S(2)}, u32[]{:S(2)}) collective-permute-start(bf16[16,32,256]{2,1,0:T(8,128)(2,1)} %get-tuple-element.22), channel_id=1, source_target_pairs={{0,32},{32,64},{64,96},{96,0},{1,33},{33,65},{65,97},{97,1},{2,34}... | collective-permute-start | bytes 786440 | tf_op jit(solution)/shard_map/ppermute | solution.py:441
  64.3 28.0 %collective-permute-start.1 = (bf16[16,32,256]{2,1,0:T(8,128)(2,1)}, bf16[16,32,256]{2,1,0:T(8,128)(2,1)}, u32[]{:S(2)}, u32[]{:S(2)}) collective-permute-start(bf16[16,32,256]{2,1,0:T(8,128)(2,1)} %get-tuple-element.22), channel_id=1, source_target_pairs={{0,64},{32,96},{64,0},{96,32},{1,65},{33,97},{65,1},{97,33},{2,66}... | collective-permute-start | bytes 786440 | tf_op jit(solution)/shard_map/ppermute | solution.py:441
  65.3 26.9 %collective-permute-start.2 = (bf16[16,32,256]{2,1,0:T(8,128)(2,1)}, bf16[16,32,256]{2,1,0:T(8,128)(2,1)}, u32[]{:S(2)}, u32[]{:S(2)}) collective-permute-start(bf16[16,32,256]{2,1,0:T(8,128)(2,1)} %get-tuple-element.22), channel_id=1, source_target_pairs={{0,96},{32,0},{64,32},{96,64},{1,97},{33,1},{65,33},{97,65},{2,98}... | collective-permute-start | bytes 786440 | tf_op jit(solution)/shard_map/ppermute | solution.py:441
  67.7 1.2 copy-start.13
  69.0 1.2 copy-start.17
  83.4 1.3 %copy-start.3 = (bf16[32,128,256]{2,1,0:T(8,128)(2,1)}, bf16[32,128,256]{2,1,0:T(8,128)(2,1)S(1)}, u32[]{:S(2)}) copy-start(bf16[32,128,256]{2,1,0:T(8,128)(2,1)S(1)} %reply.1) | copy-start | bytes 6291460
  84.8 43.7 %all-to-all-start.1 = ((bf16[32,128,256]{2,1,0:T(8,128)(2,1)}), bf16[32,128,256]{2,1,0:T(8,128)(2,1)S(1)}, u32[]{:S(2)}, u32[]{:S(2)}) async-start(bf16[32,128,256]{2,1,0:T(8,128)(2,1)} %copy-done.3), calls=%async_computation.1 | async-start | bytes 4194304 | tf_op jit(solution)/shard_map/all_to_all | solution.py:449
  94.8 21.0 %collective-permute-start.3 = (bf16[4,16,32,256]{3,2,1,0:T(8,128)(2,1)}, bf16[4,16,32,256]{3,2,1,0:T(8,128)(2,1)}, u32[]{:S(2)}, u32[]{:S(2)}) collective-permute-start(bf16[4,16,32,256]{3,2,1,0:T(8,128)(2,1)} %get-tuple-element.20), channel_id=1, source_target_pairs={{0,1},{1,0},{2,3},{3,2},{4,5},{5,4},{6,7},{7,6},{8,9},{9,8},{10,11... | collective-permute-start | bytes 3145736 | tf_op jit(solution)/shard_map/ppermute | solution.py:443
  95.8 1.8 %copy-start.1 = (bf16[32,176,256]{2,1,0:T(8,128)(2,1)S(1)}, bf16[32,176,256]{2,1,0:T(8,128)(2,1)}, u32[]{:S(2)}) copy-start(bf16[32,176,256]{2,1,0:T(8,128)(2,1)} %copy-done) | copy-start | bytes 8650756
  97.6 1.2 copy-start.14
  98.8 1.6 %copy-start.19 = (f32[16,128,256]{2,1,0:T(8,128)S(1)}, f32[16,128,256]{2,1,0:T(8,128)}, u32[]{:S(2)}) copy-start(f32[16,128,256]{2,1,0:T(8,128)} %copy-done.18) | copy-start | bytes 6291460
  100.4 15.4 %copy-start.20 = (bf16[1,4,16,32,256]{4,3,2,1,0:T(8,128)(2,1)S(1)}, bf16[1,4,16,32,256]{4,3,2,1,0:T(8,128)(2,1)}, u32[]{:S(2)}) copy-start(bf16[1,4,16,32,256]{4,3,2,1,0:T(8,128)(2,1)} %get-tuple-element.19) | copy-start | bytes 3145732
  115.8 1.5 %copy-start.10 = (bf16[16,32,32]{2,1,0:T(8,128)(2,1)S(1)}, bf16[16,32,32]{2,1,0:T(8,128)(2,1)}, u32[]{:S(2)}) copy-start(bf16[16,32,32]{2,1,0:T(8,128)(2,1)} %trans.3) | copy-start | bytes 98308
  117.2 7.7 %copy-start.8 = (bf16[16,32,256]{2,1,0:T(8,128)(2,1)S(1)}, bf16[16,32,256]{2,1,0:T(8,128)(2,1)}, u32[]{:S(2)}) copy-start(bf16[16,32,256]{2,1,0:T(8,128)(2,1)} %basis.3) | copy-start | bytes 786436
  127.1 1.3 copy-start.4
  128.4 1.6 %copy-start.5 = (f32[16,128,256]{2,1,0:T(8,128)S(1)}, f32[16,128,256]{2,1,0:T(8,128)}, u32[]{:S(2)}) copy-start(f32[16,128,256]{2,1,0:T(8,128)} %copy-done.4) | copy-start | bytes 6291460

commit v4 on v3

v4 whole, which is shorter than its diff:
```python
import functools

import jax
import jax.numpy as jnp
from jax import lax
from jax.experimental import pallas as pl
from jax.experimental.pallas import tpu as pltpu
from jax.sharding import PartitionSpec as P

KCOEF = 0.005
DELTA = 0.02
F32 = jnp.float32
BF16 = jnp.bfloat16
GROUP = 8
FEAT = 16
VMEM = pl.BlockSpec(memory_space=pltpu.VMEM)
SMEM = pl.BlockSpec(memory_space=pltpu.SMEM)
MESH = pl.DeviceIdType.MESH
PARAMS = pltpu.CompilerParams(vmem_limit_bytes=14 << 20)
WIDE = pltpu.CompilerParams(vmem_limit_bytes=56 << 20)


def dot(left, right, dims=((1,), (0,))):
    return lax.dot_general(left, right, (dims, ((), ())), preferred_element_type=F32)


def halves(value):
    high = value.astype(BF16)
    return high, (value - high.astype(F32)).astype(BF16)


def thirds(value):
    high = value.astype(BF16)
    rest = value - high.astype(F32)
    mid = rest.astype(BF16)
    return high.astype(F32), mid.astype(F32), (rest - mid.astype(F32))


def prep_kernel(ints, charges, axes, basis, trans, pair, quad, stage, fa, outgoing, rows_a, rows_b, sems):
    clusters, _, rhs = charges.shape
    width = stage.shape[2]
    peers = outgoing.shape[0]
    total = jnp.zeros((trans.shape[1], rhs), F32)
    for i in range(clusters):
        leaf = dot(basis[i], charges[i]).astype(BF16)
        total += dot(trans[i], leaf)
    top = total.astype(BF16)
    top = jnp.concatenate([top[:16], top[16:]], axis=1)
    mats = [mat[0].astype(F32) for mat in (pair, quad)]
    moves = jnp.concatenate([mat[8 * i : 8 * i + 8] for mat in mats for i in range(4)], axis=1).astype(BF16)

    x = [axes[d, :clusters] for d in range(3)]
    norm = x[0] * x[0] + x[1] * x[1] + x[2] * x[2]
    one = jnp.ones_like(norm)
    rows_a[...] = jnp.zeros_like(rows_a)
    rows_b[...] = jnp.zeros_like(rows_b)
    for d, row in enumerate((*x, *thirds(norm + DELTA * DELTA), one, one, one)):
        rows_a[:, d, :] = row
    lane = lax.broadcasted_iota(jnp.int32, (1, width), 1)
    info = axes[0, clusters : clusters + 1]
    for i in range(16):
        info = jnp.where(lane == rhs + i, ints[peers + i].astype(F32), info)
    info = jnp.broadcast_to(info, norm.shape)
    for d, row in enumerate((*(-2.0 * a for a in x), one, one, one, *thirds(norm), info)):
        rows_b[:, d, :] = row
    for c in range(clusters):
        stage[c, :rhs] = charges[c].T
        stage[c, rhs : rhs + FEAT] = rows_b[c].astype(BF16)
        stage[c, rhs + FEAT : rhs + FEAT + 16] = top
        stage[c, rhs + FEAT + 16 :] = moves

    def copy(h):
        return pltpu.make_async_copy(stage.at[ints[h]], outgoing.at[h], sems.at[h])

    def send(h, carry):
        copy(h).start()
        return carry

    def wait(h, carry):
        copy(h).wait()
        return carry

    lax.fori_loop(0, peers, send, 0)
    for c in range(clusters):
        fa[c] = rows_a[c].T.astype(BF16)
    lax.fori_loop(0, peers, wait, 0)


def prep(ints, charges, axes, basis, trans, pair, quad, peers):
    clusters, width, rhs = charges.shape
    rows = rhs + FEAT + 24
    return pl.pallas_call(
        prep_kernel,
        out_shape=(
            jax.ShapeDtypeStruct((clusters, rows, width), BF16),
            jax.ShapeDtypeStruct((clusters, width, FEAT), BF16),
            jax.ShapeDtypeStruct((peers, rows, width), BF16),
        ),
        in_specs=[SMEM] + [VMEM] * 6,
        out_specs=(VMEM, VMEM, pl.BlockSpec(memory_space=pl.ANY)),
        scratch_shapes=[pltpu.VMEM((clusters, FEAT, width), F32)] * 2
        + [pltpu.SemaphoreType.DMA((peers,))],
        compiler_params=WIDE,
        name="prep",
    )(ints, charges, axes, basis, trans, pair, quad)


def unpack(code):
    return code & 15, (code >> 4) & 63, (code >> 10).astype(F32) * 0.5


def tile(code, fa, table):
    a, b, times = unpack(code)
    s = dot(fa[a], table[b, table.shape[1] - 24 - FEAT : table.shape[1] - 24])
    return lax.rsqrt(s.astype(BF16)) * times.astype(BF16)


def own_kernel(pairs, stage, fa, acc, kbuf):
    rhs = acc.shape[1]
    acc[...] = jnp.zeros_like(acc)
    for g in range(GROUP):
        kbuf[0, g] = tile(pairs[1 + g], fa, stage)

    def body(i, carry):
        now = lax.rem(i, 2)
        for g in range(GROUP):
            j = 1 + i * GROUP + g
            a, b, _ = unpack(pairs[j])
            k = kbuf[now, g]
            acc[a] += dot(stage[b, :rhs], k, ((1,), (1,)))
            acc[b] += dot(stage[a, :rhs], k)
            kbuf[1 - now, g] = tile(pairs[j + GROUP], fa, stage)
        return carry

    lax.fori_loop(0, pl.cdiv(pairs[0], GROUP), body, 0)


def own_near(pairs, stage, fa):
    clusters, rows, width = stage.shape
    return pl.pallas_call(
        own_kernel,
        out_shape=jax.ShapeDtypeStruct((clusters, rows - 24 - FEAT, width), F32),
        in_specs=[SMEM] + [VMEM] * 2,
        out_specs=VMEM,
        scratch_shapes=[pltpu.VMEM((2, GROUP, width, width), BF16)],
        compiler_params=PARAMS,
        cost_estimate=pl.CostEstimate(flops=6 << 30, bytes_accessed=4 << 20, transcendentals=0),
        name="own_near",
    )(pairs, stage, fa)


def reply_kernel(pairs, stage, fa, incoming, back, kbuf):
    rhs, width = back.shape[1:]
    back[...] = jnp.zeros_like(back)
    for g in range(GROUP):
        kbuf[0, g] = tile(pairs[1 + g], fa, incoming)

    def body(i, total):
        now = lax.rem(i, 2)
        for g in range(GROUP):
            j = 1 + i * GROUP + g
            a, b, _ = unpack(pairs[j])
            before = unpack(pairs[jnp.maximum(j - 1, 1)])[1]
            keep = jnp.where(before == b, 1.0, 0.0).astype(F32)
            total = total * keep + dot(stage[a, :rhs], kbuf[now, g])
            back[b] = total.astype(BF16)
            kbuf[1 - now, g] = tile(pairs[j + GROUP], fa, incoming)
        return total

    lax.fori_loop(0, pl.cdiv(pairs[0], GROUP), body, jnp.zeros((rhs, width), F32))


def reply(pairs, stage, fa, incoming):
    peers, rows, width = incoming.shape
    return pl.pallas_call(
        reply_kernel,
        out_shape=jax.ShapeDtypeStruct((peers, rows - 24 - FEAT, width), BF16),
        in_specs=[SMEM] + [VMEM] * 3,
        out_specs=VMEM,
        scratch_shapes=[pltpu.VMEM((2, GROUP, width, width), BF16)],
        compiler_params=PARAMS,
        cost_estimate=pl.CostEstimate(flops=6 << 30, bytes_accessed=8 << 20, transcendentals=0),
        name="reply",
    )(pairs, stage, fa, incoming)


def remote_kernel(pairs, fa, incoming, acc_in, acc, kbuf):
    rhs = acc.shape[1]
    acc[...] = acc_in[...]
    for g in range(GROUP):
        kbuf[0, g] = tile(pairs[1 + g], fa, incoming)

    def body(i, carry):
        now = lax.rem(i, 2)
        for g in range(GROUP):
            j = 1 + i * GROUP + g
            a, b, _ = unpack(pairs[j])
            acc[a] += dot(incoming[b, :rhs], kbuf[now, g], ((1,), (1,)))
            kbuf[1 - now, g] = tile(pairs[j + GROUP], fa, incoming)
        return carry

    lax.fori_loop(0, pl.cdiv(pairs[0], GROUP), body, 0)


def remote_near(pairs, fa, incoming, acc):
    width = acc.shape[2]
    return pl.pallas_call(
        remote_kernel,
        out_shape=jax.ShapeDtypeStruct(acc.shape, F32),
        in_specs=[SMEM] + [VMEM] * 3,
        out_specs=VMEM,
        scratch_shapes=[pltpu.VMEM((2, GROUP, width, width), BF16)],
        compiler_params=PARAMS,
        cost_estimate=pl.CostEstimate(flops=6 << 30, bytes_accessed=8 << 20, transcendentals=0),
        name="remote_near",
    )(pairs, fa, incoming, acc)


def far_kernel(ids, own_points, nodes, trans, leaf, sources):
    rank = 32

    def skel(n):
        rows = nodes[n, 16:32, :]
        return jnp.concatenate([rows[:, :128], rows[:, 128:]], axis=0)

    def transfer(n, which):
        rows = nodes[n, 32:, 128 * which : 128 * which + 128].astype(F32)
        return jnp.concatenate([rows[:, 32 * i : 32 * i + 32] for i in range(4)], axis=0).astype(BF16)

    def points(n):
        return nodes[n, :16, :128].astype(F32)[9:10]

    def kernel_tile(mine, theirs):
        gap = mine - theirs
        sq = gap * gap
        s = ((DELTA * DELTA + sq[:, :32]) + sq[:, 32:64]) + sq[:, 64:96]
        return halves(KCOEF * lax.rsqrt(s))

    def apply(tile, source):
        return dot(tile[0], source) + dot(tile[1], source)

    mine = [own_points[level] for level in range(3)]
    zero = jnp.zeros((rank, 128), F32)

    def one(f, total):
        n = ids[f]
        return total + apply(kernel_tile(mine[0], points(n)), skel(n))

    def two(f, total):
        n, m = ids[8 + f], lax.rem(ids[8 + f] + 64, 128)
        source = dot(transfer(n, 0), skel(n)) + dot(transfer(m, 0), skel(m))
        theirs = 0.5 * (points(n) + points(m))
        return total + apply(kernel_tile(mine[1], theirs), source.astype(BF16))

    def three(f, total):
        n = [lax.rem(ids[24 + f] + step, 128) for step in (0, 64, 1, 65)]
        terms = [dot(transfer(i, 1), skel(i)) for i in n]
        source = (terms[0] + terms[1]) + (terms[2] + terms[3])
        left = 0.5 * (points(n[0]) + points(n[1]))
        right = 0.5 * (points(n[2]) + points(n[3]))
        return total + apply(kernel_tile(mine[2], 0.5 * (left + right)), source.astype(BF16))

    far_one = lax.fori_loop(0, 8, one, zero, unroll=True)
    far_two = lax.fori_loop(0, 16, two, zero, unroll=4)
    far_three = lax.fori_loop(0, 32, three, zero, unroll=4)
    me = ids[56]

    def down_by(which, value):
        high, low = halves(value)
        mat = transfer(me, which)
        return dot(mat, high, ((0,), (0,))) + dot(mat, low, ((0,), (0,)))

    down = far_one + down_by(0, far_two) + down_by(1, far_three)
    high, low = halves(down.T)
    for c in range(trans.shape[0]):
        leaf[c] = (dot(high, trans[c]) + dot(low, trans[c])).astype(BF16)


def far_field(ids, own_points, nodes, trans):
    clusters, rank, _ = trans.shape
    return pl.pallas_call(
        far_kernel,
        out_shape=jax.ShapeDtypeStruct((clusters, 128, rank), BF16),
        in_specs=[SMEM] + [VMEM] * 3,
        out_specs=VMEM,
        scratch_shapes=[pltpu.VMEM((8, 128), F32)],
        compiler_params=PARAMS,
        cost_estimate=pl.CostEstimate(flops=6 << 30, bytes_accessed=4 << 20, transcendentals=0),
        name="far_field",
    )(ids, own_points, nodes, trans)


def base_kernel(acc, leaf, basis, base):
    def one(c, carry):
        base[c] = acc[c] * KCOEF + dot(leaf[c], basis[c])
        return carry

    lax.fori_loop(0, acc.shape[0], one, 0)


def base_sum(acc, leaf, basis):
    return pl.pallas_call(
        base_kernel,
        out_shape=jax.ShapeDtypeStruct(acc.shape, F32),
        in_specs=[VMEM] * 3,
        out_specs=VMEM,
        compiler_params=PARAMS,
        cost_estimate=pl.CostEstimate(flops=2 << 30, bytes_accessed=4 << 20, transcendentals=0),
        name="base_sum",
    )(acc, leaf, basis)


def final_kernel(order, starts, base, returned, out, rows, sems):
    clusters = base.shape[0]

    def copy(c):
        return pltpu.make_async_copy(rows.at[c], out.at[c], sems.at[c])

    for c in range(clusters):

        def collect(i, total):
            return total + returned[order[i]].astype(F32)

        zero = jnp.zeros(base.shape[1:], F32)
        total = lax.fori_loop(starts[c], starts[c + 1], collect, zero)
        rows[c] = (base[c] + KCOEF * total).T
        copy(c).start()
    for c in range(clusters):
        copy(c).wait()


def finish(order, starts, base, returned):
    clusters, conductors, width = base.shape
    return pl.pallas_call(
        final_kernel,
        out_shape=jax.ShapeDtypeStruct((clusters, width, conductors), F32),
        in_specs=[SMEM] * 2 + [VMEM] * 2,
        out_specs=pl.BlockSpec(memory_space=pl.ANY),
        scratch_shapes=[
            pltpu.VMEM((clusters, width, conductors), F32),
            pltpu.SemaphoreType.DMA((clusters,)),
        ],
        compiler_params=PARAMS,
        name="finish",
    )(order, starts, base, returned)


def pair_lists(first, second, count, clusters, entries):
    live = jnp.arange(first.shape[0], dtype=jnp.int32) < count
    own = second < clusters
    a = jnp.where(own, jnp.minimum(first, second), first)
    b = jnp.where(own, jnp.maximum(first, second), second)
    key = jnp.where(live, b * clusters + a, -1)
    keys = jnp.arange(entries * clusters, dtype=jnp.int32)
    times = jnp.sum((keys[:, None] == key[None, :]).astype(jnp.int32), axis=1)
    times = jnp.where(keys % clusters == keys // clusters, times, 2 * times)
    lists = []
    for lo, hi in ((0, clusters * clusters), (clusters * clusters, entries * clusters)):
        part = times[lo:hi]
        held = part > 0
        spots = jnp.arange(hi - lo, dtype=jnp.int32)
        rank = jnp.sum(((spots[None, :] < spots[:, None]) & held[None, :]).astype(jnp.int32), axis=1)
        slots = jnp.arange(256 + 2 * GROUP, dtype=jnp.int32)
        match = (rank[None, :] == slots[:, None]) & held[None, :]
        total = jnp.sum(held.astype(jnp.int32))
        last = jnp.max(jnp.where(held, spots, 0))
        code = jnp.sum(jnp.where(match, (spots + 1024 * part)[None, :], 0), axis=1)
        code = jnp.where(slots < total, code, last)
        lists.append(jnp.concatenate([total.reshape(1), code]))
    return lists


def shards(
    charges,
    panel_coords,
    cluster_basis,
    trans_leaf,
    trans_pair,
    trans_quad,
    skel_points,
    send_slots,
    pair_first,
    pair_second,
    pair_count,
    far_one,
    far_two,
    far_three,
):
    clusters, _, width = panel_coords.shape
    conductors = charges.shape[1]
    peers = lax.axis_size("dev")
    blocks = charges.reshape(clusters, width, conductors)
    points = jnp.pad(skel_points.reshape(1, 1, -1), ((0, 2), (0, 0), (0, width - skel_points.size)))
    axes = jnp.concatenate([jnp.swapaxes(panel_coords, 0, 1), points], axis=1).astype(F32)
    slots = send_slots[:, 0]
    ints = jnp.concatenate([slots, far_two[0], far_three[0]])
    stage, fa, outgoing = prep(
        ints, blocks, axes, cluster_basis, trans_leaf, trans_pair, trans_quad, peers
    )
    incoming = lax.all_to_all(outgoing, "dev", split_axis=0, concat_axis=0, tiled=True)

    own_list, remote_list = pair_lists(pair_first, pair_second, pair_count[0], clusters, clusters + peers)
    acc = own_near(own_list, stage, fa)
    back = reply(remote_list, stage, fa, incoming)
    returned = lax.all_to_all(back, "dev", split_axis=0, concat_axis=0, tiled=True)
    acc = remote_near(remote_list, fa, incoming, acc)

    z, d = lax.axis_index("group"), lax.axis_index("dev")
    xy, c = d // 2, d % 2
    nodes, _ = lax.optimization_barrier((incoming, back))
    same = nodes.reshape(peers // 2, 2, -1, width)[:, :, conductors:]
    same = lax.dynamic_index_in_dim(same, c, axis=1, keepdims=False)
    along = [same]
    for step in (1, 2, 3):
        along.append(lax.ppermute(same, "group", [(i, (i + step) % 4) for i in range(4)]))
    along = jnp.stack(along)
    other = lax.ppermute(along, "dev", [(i, i ^ 1) for i in range(32)])
    nodes = jnp.stack([along, other]).reshape(128, 40, width)

    def place(owner):
        step = (z - owner // peers) % 4
        return ((c ^ owner % 2) * 4 + step) * 16 + owner % peers // 2

    quad = lax.dynamic_slice(incoming, (d // 4 * 4, conductors + 9, 0), (4, 1, width))[:, 0]
    quad_lists = quad[:, 128:144].astype(jnp.int32)
    pair_list = lax.dynamic_slice_in_dim(quad_lists[:, :8], d % 4 // 2 * 2, 2, axis=0)
    ids = jnp.concatenate(
        [
            place(far_one[0]),
            place(2 * pair_list.reshape(-1)),
            place(4 * quad_lists[:, 8:].reshape(-1)),
            xy.reshape(1),
        ]
    )
    quad_points = quad[:, :96].astype(F32).reshape(4, 3, 32)
    pair_points = 0.5 * (quad_points[0::2] + quad_points[1::2])
    own_points = jnp.stack(
        [
            skel_points[0].astype(F32),
            lax.dynamic_index_in_dim(pair_points, d % 4 // 2, axis=0, keepdims=False),
            0.5 * (pair_points[0] + pair_points[1]),
        ]
    )
    own_points = jnp.repeat(jnp.swapaxes(own_points, 1, 2), 32, axis=2)
    own_points = jnp.pad(own_points, ((0, 0), (0, 0), (0, 32)))
    leaf = far_field(ids, own_points, nodes, trans_leaf)
    base = base_sum(acc, leaf, cluster_basis)

    spots = jnp.arange(peers, dtype=jnp.int32)
    rank = jnp.sum(
        (slots[None, :] < slots[:, None])
        | ((slots[None, :] == slots[:, None]) & (spots[None, :] < spots[:, None])),
        axis=1,
        dtype=jnp.int32,
    )
    order = jnp.sum(jnp.where(rank[None, :] == spots[:, None], spots[None, :], 0), axis=1)
    edges = jnp.arange(clusters + 1, dtype=jnp.int32)
    starts = jnp.sum(slots[None, :] < edges[:, None], axis=1, dtype=jnp.int32)
    out = finish(order, starts, base, returned)
    return out.reshape(clusters * width, conductors)


def solution(mesh):
    owners = ("group", "dev")
    rows, block, flat = P(owners, None), P(owners, None, None), P(owners)
    placed = (rows, *(block,) * 6, rows, *(flat,) * 3, *(rows,) * 3)
    return jax.shard_map(shards, mesh=mesh, in_specs=placed, out_specs=rows, check_vma=False)
```

time: 135 us -> 140 us (1.037)
  the two profiles are of different devices: /device:TPU:37 before, /device:TPU:1 now
where the time goes in v4:
time: 140 us; the launch traced here: 139 us
  Pallas kernels  55.7 us (40%)
  waiting for transfers between devices  32.3 us (23%)
  local copies, waits for them, and re-layouts  18.9 us (13%)
  starting transfers between devices  17.5 us (12%)
  other arithmetic  13.9 us (10%)
    ppermute x3, waiting for transfers between devices, shards(): lax.ppermute(same, 'group', [(i, (i + step) % 4) for i in range(4)])  16.8 us
    unnamed x41, local copies, waits for them, and re-layouts  16.3 us
    all_to_all x1, waiting for transfers between devices, shards(): lax.all_to_all(outgoing, 'dev', split_axis=0, concat_axis=0, tiled=True)  15.6 us
    pallas_call x1, Pallas kernels, remote_near(): pl.pallas_call(remote_kernel, out_shape=jax.ShapeDtypeStruct(acc.shape, F...  15.4 us
    pallas_call x1, Pallas kernels, reply(): pl.pallas_call(reply_kernel, out_shape=jax.ShapeDtypeStruct((peers, rows...  12.8 us
    all_to_all x1, starting transfers between devices, shards(): lax.all_to_all(outgoing, 'dev', split_axis=0, concat_axis=0, tiled=True)  8.73 us
    pallas_call x1, Pallas kernels, own_near(): pl.pallas_call(own_kernel, out_shape=jax.ShapeDtypeStruct((clusters, rows...  8.48 us
    pallas_call x1, Pallas kernels, far_field(): pl.pallas_call(far_kernel, out_shape=jax.ShapeDtypeStruct((clusters, 128,...  7.16 us
  transfers between devices with their start and end apart: 6, of which 3 were waited for; matrix products, arithmetic and copies ran while one was open for 9% of the time, Pallas kernels for 24%

profile of v4, /device:TPU:1, one launch (start us, length us, event | category | flops | bytes accessed | tf_op | source)
XLA Modules:
  0.0 139.3 jit_solution(7729057880175987237)
XLA Ops:
  0.0 0.8 reshape.51
  0.8 1.4 fusion.6.axes
  2.1 1.3 pad_add_fusion.2.ints
  3.5 5.9 %prep.1 = (bf16[16,168,256]{2,1,0:T(8,128)(2,1)}, bf16[16,256,16]{2,1,0:T(8,128)(2,1)}, bf16[32,168,256]{2,1,0:T(8,128)(2,1)}) custom-call(s32[48]{0:T(128)} %pad_add_fusion.2.ints, bf16[16,256,128]{2,1,0:T(8,128)(2,1)} %bitcast.48, f32[3,17,256]{2,1,0:T(8,128)} %fusion.6.axes, bf16[16,32,256]{2,1,0:T(8,128)(2,1)} %basis.3, bf16[16,32,32]{2,1,0:T(8,128)(2,1)} %trans.3, ...), custom_call_target="tpu_custom_call" | custom-call | tf_op jit(solution)/shard_map/prep/pallas_call | solution.py:92
  9.5 8.7 %all-to-all-start = ((bf16[32,168,256]{2,1,0:T(8,128)(2,1)}), bf16[32,168,256]{2,1,0:T(8,128)(2,1)S(1)}, u32[]{:S(2)}, u32[]{:S(2)}) async-start(bf16[32,168,256]{2,1,0:T(8,128)(2,1)} %get-tuple-element.10), calls=%async_computation | async-start | bytes 5505024 | tf_op jit(solution)/shard_map/all_to_all | solution.py:400
  18.9 0.2 convert_reduce_fusion.1
  19.1 0.7 convert_reduce_fusion.6
  19.8 0.1 convert_reduce_fusion.2
  19.9 0.2 select_reduce_fusion.1
  20.0 1.3 fusion.19
  21.3 0.7 pad_add_fusion.1.pairs
  22.1 0.7 convert_reduce_fusion.5
  22.7 0.1 convert_reduce_fusion
  22.9 0.2 select_reduce_fusion
  23.1 1.3 fusion.18
  24.4 0.7 pad_add_fusion.pairs
  25.1 0.1 convert_reduce_fusion.4.starts
  25.2 0.2 convert_reduce_fusion.3
  25.4 0.1 select_reduce_fusion.2.order
  25.6 1.3 copy-done.7
  26.9 1.2 copy-done.9
  28.1 8.5 %own_near.1.acc_in = f32[16,128,256]{2,1,0:T(8,128)S(1)} custom-call(s32[273]{0:T(512)S(1)} %pad_add_fusion.1.pairs, bf16[16,168,256]{2,1,0:T(8,128)(2,1)S(1)} %copy-done.7, bf16[16,256,16]{2,1,0:T(8,128)(2,1)S(1)} %copy-done.9), custom_call_target="tpu_custom_call" | custom-call | flops 6442450944 | bytes 4194304 | tf_op jit(solution)/shard_map/own_near/pallas_call | solution.py:140
  36.6 1.3 copy-done.12
  37.9 15.6 %all-to-all-done.incoming = bf16[32,168,256]{2,1,0:T(8,128)(2,1)S(1)} async-done(((bf16[32,168,256]{2,1,0:T(8,128)(2,1)}), bf16[32,168,256]{2,1,0:T(8,128)(2,1)S(1)}, u32[]{:S(2)}, u32[]{:S(2)}) %all-to-all-start) | async-done | bytes 2752544 | tf_op jit(solution)/shard_map/all_to_all | solution.py:400
  53.6 2.3 %copy-done.8 = bf16[16,168,256]{2,1,0:T(8,128)(2,1)S(1)} copy-done((bf16[16,168,256]{2,1,0:T(8,128)(2,1)S(1)}, bf16[16,168,256]{2,1,0:T(8,128)(2,1)}, u32[]{:S(2)}) %copy-start.8) | copy-done | bytes 1376280
  55.9 1.2 copy-done.10
  57.1 12.8 %reply.1 = bf16[32,128,256]{2,1,0:T(8,128)(2,1)S(1)} custom-call(s32[273]{0:T(512)S(1)} %pad_add_fusion.pairs, bf16[16,168,256]{2,1,0:T(8,128)(2,1)S(1)} %copy-done.8, bf16[16,256,16]{2,1,0:T(8,128)(2,1)S(1)} %copy-done.10, bf16[32,168,256]{2,1,0:T(8,128)(2,1)S(1)} %all-to-all-done.incoming), custom_call_target="tpu_custom_call" | custom-call | flops 6442450944 | bytes 8388608 | tf_op jit(solution)/shard_map/reply/pallas_call | solution.py:175
  69.9 1.3 copy-done.2
  71.2 3.8 %all-to-all-start.1 = ((bf16[32,128,256]{2,1,0:T(8,128)(2,1)}), bf16[32,128,256]{2,1,0:T(8,128)(2,1)S(1)}, u32[]{:S(2)}, u32[]{:S(2)}) async-start(bf16[32,128,256]{2,1,0:T(8,128)(2,1)} %copy-done.2), calls=%async_computation.1 | async-start | bytes 4194304 | tf_op jit(solution)/shard_map/all_to_all | solution.py:405
  75.0 1.1 slice.48
  76.2 3.5 %collective-permute-start.2 = (bf16[16,40,256]{2,1,0:T(8,128)(2,1)S(1)}, bf16[16,40,256]{2,1,0:T(8,128)(2,1)S(1)}, u32[]{:S(2)}, u32[]{:S(2)}) collective-permute-start(bf16[16,40,256]{2,1,0:T(8,128)(2,1)S(1)} %get-tuple-element.22), channel_id=1, source_target_pairs={{0,96},{32,0},{64,32},{96,64},{1,97},{33,1},{65,33},{97,65},{2,98}... | collective-permute-start | bytes 983048 | tf_op jit(solution)/shard_map/ppermute | solution.py:415
  79.7 0.7 collective-permute-start
  80.6 13.0 %collective-permute-done.2 = bf16[16,40,256]{2,1,0:T(8,128)(2,1)S(1)} collective-permute-done((bf16[16,40,256]{2,1,0:T(8,128)(2,1)S(1)}, bf16[16,40,256]{2,1,0:T(8,128)(2,1)S(1)}, u32[]{:S(2)}, u32[]{:S(2)}) %collective-permute-start.2) | collective-permute-done | bytes 327712 | tf_op jit(solution)/shard_map/ppermute | solution.py:415
  93.6 3.8 %collective-permute-done = bf16[16,40,256]{2,1,0:T(8,128)(2,1)} collective-permute-done((bf16[16,40,256]{2,1,0:T(8,128)(2,1)S(1)}, bf16[16,40,256]{2,1,0:T(8,128)(2,1)}, u32[]{:S(2)}, u32[]{:S(2)}) %collective-permute-start) | collective-permute-done | bytes 327712 | tf_op jit(solution)/shard_map/ppermute | solution.py:415
  97.4 2.7 %fusion.31 = (bf16[1,4,16,40,256]{4,3,2,1,0:T(8,128)(2,1)}, bf16[4,16,40,256]{3,2,1,0:T(8,128)(2,1)}) fusion(bf16[1,16,40,256]{3,2,1,0:T(8,128)(2,1)S(1)} %bitcast.49, bf16[1,16,40,256]{3,2,1,0:T(8,128)(2,1)S(1)} %bitcast.50, bf16[1,16,40,256]{3,2,1,0:T(8,128)(2,1)} %bitcast.14, bf16[1,16,40,256]{3,2,1,0:T(8,128)(2,1)S(1)} %get-tuple-element.21), kind=kLoop, calls=%fused_computation.128 | loop fusion | flops 1966080 | bytes 3932160 | tf_op jit(solution)/shard_map/stack | solution.py:418
  100.1 0.8 collective-permute-start.3
  101.1 0.2 broadcast_in_dim.81
  101.3 0.1 reshape.56
  101.5 1.8 %copy-done.1 = bf16[32,168,256]{2,1,0:T(8,128)(2,1)S(1)} copy-done((bf16[32,168,256]{2,1,0:T(8,128)(2,1)S(1)}, bf16[32,168,256]{2,1,0:T(8,128)(2,1)}, u32[]{:S(2)}) %copy-start.1) | copy-done | bytes 2752536
  103.3 1.2 copy-done.11
  104.5 1.6 %copy-done.13 = f32[16,128,256]{2,1,0:T(8,128)S(1)} copy-done((f32[16,128,256]{2,1,0:T(8,128)S(1)}, f32[16,128,256]{2,1,0:T(8,128)}, u32[]{:S(2)}) %copy-start.13) | copy-done | bytes 2097176
  106.1 15.4 %remote_near.1.acc = f32[16,128,256]{2,1,0:T(8,128)S(1)} custom-call(s32[273]{0:T(512)S(1)} %pad_add_fusion.pairs, bf16[16,256,16]{2,1,0:T(8,128)(2,1)S(1)} %copy-done.11, bf16[32,168,256]{2,1,0:T(8,128)(2,1)S(1)} %copy-done.1, f32[16,128,256]{2,1,0:T(8,128)S(1)} %copy-done.13), custom_call_target="tpu_custom_call" | custom-call | flops 6442450944 | bytes 8388608 | tf_op jit(solution)/shard_map/remote_near/pallas_call | solution.py:207
  121.6 1.6 %pad_maximum_fusion = bf16[2,4,16,40,256]{4,3,2,1,0:T(8,128)(2,1)S(1)} fusion(bf16[1,4,16,40,256]{4,3,2,1,0:T(8,128)(2,1)} %bitcast.18, bf16[1,4,16,40,256]{4,3,2,1,0:T(8,128)(2,1)S(1)} %copy-done.14), kind=kLoop, calls=%fused_computation | loop fusion | flops 1310720 | bytes 5242880 | tf_op jit(solution)/shard_map/stack | solution.py:418
  123.2 7.2 %far_field.1.leaf = bf16[16,128,32]{2,1,0:T(8,128)(2,1)S(1)} custom-call(s32[57]{0:T(128)S(1)} %pad_add_fusion.3.ids, f32[3,32,128]{2,1,0:T(8,128)S(1)} %pad.9.own_points, bf16[128,40,256]{2,1,0:T(8,128)(2,1)S(1)} %bitcast.47, bf16[16,32,32]{2,1,0:T(8,128)(2,1)S(1)} %copy-done.6), custom_call_target="tpu_custom_call" | custom-call | flops 6442450944 | bytes 4194304 | tf_op jit(solution)/shard_map/far_field/pallas_call | solution.py:281
  130.4 2.2 %base_sum.1.base = f32[16,128,256]{2,1,0:T(8,128)S(1)} custom-call(f32[16,128,256]{2,1,0:T(8,128)S(1)} %remote_near.1.acc, bf16[16,128,32]{2,1,0:T(8,128)(2,1)S(1)} %far_field.1.leaf, bf16[16,32,256]{2,1,0:T(8,128)(2,1)S(1)} %copy-done.5), custom_call_target="tpu_custom_call" | custom-call | flops 2147483648 | bytes 4194304 | tf_op jit(solution)/shard_map/base_sum/pallas_call | solution.py:302
  132.6 1.3 copy-done.3
  133.9 1.6 %copy-done.4 = f32[16,128,256]{2,1,0:T(8,128)S(1)} copy-done((f32[16,128,256]{2,1,0:T(8,128)S(1)}, f32[16,128,256]{2,1,0:T(8,128)}, u32[]{:S(2)}) %copy-start.4) | copy-done | bytes 2097176
  135.5 3.8 %finish.1 = f32[16,256,128]{2,1,0:T(8,128)} custom-call(s32[32]{0:T(128)S(1)} %select_reduce_fusion.2.order, s32[17]{0:T(128)S(1)} %convert_reduce_fusion.4.starts, f32[16,128,256]{2,1,0:T(8,128)S(1)} %copy-done.4, bf16[32,128,256]{2,1,0:T(8,128)(2,1)S(1)} %all-to-all-done.1.returned), custom_call_target="tpu_custom_call" | custom-call | tf_op jit(solution)/shard_map/finish/pallas_call | solution.py:334
  (55 shorter events, 0.8 us)
Async XLA Ops:
  9.4 9.5 %copy-start.15 = (s32[256]{0:T(256)S(1)}, s32[256]{0:T(256)}, u32[]{:S(2)}) copy-start(s32[256]{0:T(256)} %param.23) | copy-start | bytes 3076
  9.4 9.4 %copy-start.16 = (s32[256]{0:T(256)S(1)}, s32[256]{0:T(256)}, u32[]{:S(2)}) copy-start(s32[256]{0:T(256)} %param.22) | copy-start | bytes 3076
  9.4 10.3 %copy-start.17 = (bf16[1,3,32]{2,1,0:T(4,128)(2,1)S(1)}, bf16[1,3,32]{2,1,0:T(4,128)(2,1)}, u32[]{:S(2)}) copy-start(bf16[1,3,32]{2,1,0:T(4,128)(2,1)} %param.20) | copy-start | bytes 580
  9.4 15.7 %copy-start.18 = (s32[32,1]{0,1:T(1,128)S(1)}, s32[32,1]{0,1:T(1,128)}, u32[]{:S(2)}) copy-start(s32[32,1]{0,1:T(1,128)} %param.21) | copy-start | bytes 388
  9.4 16.1 %copy-start.19 = (s32[1,8]{1,0:T(1,128)S(1)}, s32[1,8]{1,0:T(1,128)}, u32[]{:S(2)}) copy-start(s32[1,8]{1,0:T(1,128)} %param.25) | copy-start | bytes 100
  9.5 44.0 %all-to-all-start = ((bf16[32,168,256]{2,1,0:T(8,128)(2,1)}), bf16[32,168,256]{2,1,0:T(8,128)(2,1)S(1)}, u32[]{:S(2)}, u32[]{:S(2)}) async-start(bf16[32,168,256]{2,1,0:T(8,128)(2,1)} %get-tuple-element.10), calls=%async_computation | async-start | bytes 5505024 | tf_op jit(solution)/shard_map/all_to_all | solution.py:400
  25.6 1.3 copy-start.7
  26.9 1.2 copy-start.9
  36.6 1.3 copy-start.12
  53.5 16.3 %copy-start = (bf16[32,168,256]{2,1,0:T(8,128)(2,1)}, bf16[32,168,256]{2,1,0:T(8,128)(2,1)S(1)}, u32[]{:S(2)}) copy-start(bf16[32,168,256]{2,1,0:T(8,128)(2,1)S(1)} %all-to-all-done.incoming) | copy-start | bytes 8257540
  53.5 2.3 %copy-start.8 = (bf16[16,168,256]{2,1,0:T(8,128)(2,1)S(1)}, bf16[16,168,256]{2,1,0:T(8,128)(2,1)}, u32[]{:S(2)}) copy-start(bf16[16,168,256]{2,1,0:T(8,128)(2,1)} %get-tuple-element.11.stage) | copy-start | bytes 4128772
  55.8 1.2 copy-start.10
  69.8 1.3 copy-start.2
  71.2 62.7 %all-to-all-start.1 = ((bf16[32,128,256]{2,1,0:T(8,128)(2,1)}), bf16[32,128,256]{2,1,0:T(8,128)(2,1)S(1)}, u32[]{:S(2)}, u32[]{:S(2)}) async-start(bf16[32,128,256]{2,1,0:T(8,128)(2,1)} %copy-done.2), calls=%async_computation.1 | async-start | bytes 4194304 | tf_op jit(solution)/shard_map/all_to_all | solution.py:405
  76.2 17.4 %collective-permute-start.2 = (bf16[16,40,256]{2,1,0:T(8,128)(2,1)S(1)}, bf16[16,40,256]{2,1,0:T(8,128)(2,1)S(1)}, u32[]{:S(2)}, u32[]{:S(2)}) collective-permute-start(bf16[16,40,256]{2,1,0:T(8,128)(2,1)S(1)} %get-tuple-element.22), channel_id=1, source_target_pairs={{0,96},{32,0},{64,32},{96,64},{1,97},{33,1},{65,33},{97,65},{2,98}... | collective-permute-start | bytes 983048 | tf_op jit(solution)/shard_map/ppermute | solution.py:415
  79.7 13.9 %collective-permute-start.1 = (bf16[16,40,256]{2,1,0:T(8,128)(2,1)S(1)}, bf16[16,40,256]{2,1,0:T(8,128)(2,1)S(1)}, u32[]{:S(2)}, u32[]{:S(2)}) collective-permute-start(bf16[16,40,256]{2,1,0:T(8,128)(2,1)S(1)} %get-tuple-element.22), channel_id=1, source_target_pairs={{0,64},{32,96},{64,0},{96,32},{1,65},{33,97},{65,1},{97,33},{2,66}... | collective-permute-start | bytes 983048 | tf_op jit(solution)/shard_map/ppermute | solution.py:415
  79.7 17.7 %collective-permute-start = (bf16[16,40,256]{2,1,0:T(8,128)(2,1)S(1)}, bf16[16,40,256]{2,1,0:T(8,128)(2,1)}, u32[]{:S(2)}, u32[]{:S(2)}) collective-permute-start(bf16[16,40,256]{2,1,0:T(8,128)(2,1)S(1)} %get-tuple-element.22), channel_id=1, source_target_pairs={{0,32},{32,64},{64,96},{96,0},{1,33},{33,65},{65,97},{97,1},{2,34}... | collective-permute-start | bytes 983048 | tf_op jit(solution)/shard_map/ppermute | solution.py:415
  100.1 21.5 %collective-permute-start.3 = (bf16[4,16,40,256]{3,2,1,0:T(8,128)(2,1)}, bf16[4,16,40,256]{3,2,1,0:T(8,128)(2,1)}, u32[]{:S(2)}, u32[]{:S(2)}) collective-permute-start(bf16[4,16,40,256]{3,2,1,0:T(8,128)(2,1)} %get-tuple-element.20), channel_id=1, source_target_pairs={{0,1},{1,0},{2,3},{3,2},{4,5},{5,4},{6,7},{7,6},{8,9},{9,8},{10,11... | collective-permute-start | bytes 3932168 | tf_op jit(solution)/shard_map/ppermute | solution.py:417
  101.5 1.8 %copy-start.1 = (bf16[32,168,256]{2,1,0:T(8,128)(2,1)S(1)}, bf16[32,168,256]{2,1,0:T(8,128)(2,1)}, u32[]{:S(2)}) copy-start(bf16[32,168,256]{2,1,0:T(8,128)(2,1)} %copy-done) | copy-start | bytes 8257540
  103.3 1.2 copy-start.11
  104.5 1.6 %copy-start.13 = (f32[16,128,256]{2,1,0:T(8,128)S(1)}, f32[16,128,256]{2,1,0:T(8,128)}, u32[]{:S(2)}) copy-start(f32[16,128,256]{2,1,0:T(8,128)} %copy-done.12) | copy-start | bytes 6291460
  106.1 15.5 %copy-start.14 = (bf16[1,4,16,40,256]{4,3,2,1,0:T(8,128)(2,1)S(1)}, bf16[1,4,16,40,256]{4,3,2,1,0:T(8,128)(2,1)}, u32[]{:S(2)}) copy-start(bf16[1,4,16,40,256]{4,3,2,1,0:T(8,128)(2,1)} %get-tuple-element.19) | copy-start | bytes 3932164
  121.6 1.6 %copy-start.6 = (bf16[16,32,32]{2,1,0:T(8,128)(2,1)S(1)}, bf16[16,32,32]{2,1,0:T(8,128)(2,1)}, u32[]{:S(2)}) copy-start(bf16[16,32,32]{2,1,0:T(8,128)(2,1)} %trans.3) | copy-start | bytes 98308
  123.2 7.2 %copy-start.5 = (bf16[16,32,256]{2,1,0:T(8,128)(2,1)S(1)}, bf16[16,32,256]{2,1,0:T(8,128)(2,1)}, u32[]{:S(2)}) copy-start(bf16[16,32,256]{2,1,0:T(8,128)(2,1)} %basis.3) | copy-start | bytes 786436
  132.6 1.3 copy-start.3
  133.9 1.6 %copy-start.4 = (f32[16,128,256]{2,1,0:T(8,128)S(1)}, f32[16,128,256]{2,1,0:T(8,128)}, u32[]{:S(2)}) copy-start(f32[16,128,256]{2,1,0:T(8,128)} %copy-done.3) | copy-start | bytes 6291460

commit v5 on v4

--- a/solution.py
+++ b/solution.py
@@ -178,7 +178,7 @@
         in_specs=[SMEM] + [VMEM] * 3,
         out_specs=VMEM,
         scratch_shapes=[pltpu.VMEM((2, GROUP, width, width), BF16)],
-        compiler_params=PARAMS,
+        compiler_params=WIDE,
         cost_estimate=pl.CostEstimate(flops=6 << 30, bytes_accessed=8 << 20, transcendentals=0),
         name="reply",
     )(pairs, stage, fa, incoming)
@@ -210,13 +210,13 @@
         in_specs=[SMEM] + [VMEM] * 3,
         out_specs=VMEM,
         scratch_shapes=[pltpu.VMEM((2, GROUP, width, width), BF16)],
-        compiler_params=PARAMS,
+        compiler_params=WIDE,
         cost_estimate=pl.CostEstimate(flops=6 << 30, bytes_accessed=8 << 20, transcendentals=0),
         name="remote_near",
     )(pairs, fa, incoming, acc)
 
 
-def far_kernel(ids, own_points, nodes, trans, leaf, sources):
+def far_kernel(ids, own_points, nodes, trans, acc, basis, base):
     rank = 32
 
     def skel(n):
@@ -273,41 +273,20 @@
     down = far_one + down_by(0, far_two) + down_by(1, far_three)
     high, low = halves(down.T)
     for c in range(trans.shape[0]):
-        leaf[c] = (dot(high, trans[c]) + dot(low, trans[c])).astype(BF16)
-
-
-def far_field(ids, own_points, nodes, trans):
-    clusters, rank, _ = trans.shape
+        leaf = (dot(high, trans[c]) + dot(low, trans[c])).astype(BF16)
+        base[c] = acc[c] * KCOEF + dot(leaf, basis[c])
+
+
+def far_field(ids, own_points, nodes, trans, acc, basis):
     return pl.pallas_call(
         far_kernel,
-        out_shape=jax.ShapeDtypeStruct((clusters, 128, rank), BF16),
-        in_specs=[SMEM] + [VMEM] * 3,
+        out_shape=jax.ShapeDtypeStruct(acc.shape, F32),
+        in_specs=[SMEM] + [VMEM] * 5,
         out_specs=VMEM,
-        scratch_shapes=[pltpu.VMEM((8, 128), F32)],
-        compiler_params=PARAMS,
+        compiler_params=WIDE,
         cost_estimate=pl.CostEstimate(flops=6 << 30, bytes_accessed=4 << 20, transcendentals=0),
         name="far_field",
-    )(ids, own_points, nodes, trans)
-
-
-def base_kernel(acc, leaf, basis, base):
-    def one(c, carry):
-        base[c] = acc[c] * KCOEF + dot(leaf[c], basis[c])
-        return carry
-
-    lax.fori_loop(0, acc.shape[0], one, 0)
-
-
-def base_sum(acc, leaf, basis):
-    return pl.pallas_call(
-        base_kernel,
-        out_shape=jax.ShapeDtypeStruct(acc.shape, F32),
-        in_specs=[VMEM] * 3,
-        out_specs=VMEM,
-        compiler_params=PARAMS,
-        cost_estimate=pl.CostEstimate(flops=2 << 30, bytes_accessed=4 << 20, transcendentals=0),
-        name="base_sum",
-    )(acc, leaf, basis)
+    )(ids, own_points, nodes, trans, acc, basis)
 
 
 def final_kernel(order, starts, base, returned, out, rows, sems):
@@ -340,7 +319,7 @@
             pltpu.VMEM((clusters, width, conductors), F32),
             pltpu.SemaphoreType.DMA((clusters,)),
         ],
-        compiler_params=PARAMS,
+        compiler_params=WIDE,
         name="finish",
     )(order, starts, base, returned)
 
@@ -413,6 +392,7 @@
     along = [same]
     for step in (1, 2, 3):
         along.append(lax.ppermute(same, "group", [(i, (i + step) % 4) for i in range(4)]))
+    along, acc = lax.optimization_barrier((along, acc))
     along = jnp.stack(along)
     other = lax.ppermute(along, "dev", [(i, i ^ 1) for i in range(32)])
     nodes = jnp.stack([along, other]).reshape(128, 40, width)
@@ -443,8 +423,7 @@
     )
     own_points = jnp.repeat(jnp.swapaxes(own_points, 1, 2), 32, axis=2)
     own_points = jnp.pad(own_points, ((0, 0), (0, 0), (0, 32)))
-    leaf = far_field(ids, own_points, nodes, trans_leaf)
-    base = base_sum(acc, leaf, cluster_basis)
+    base = far_field(ids, own_points, nodes, trans_leaf, acc, cluster_basis)
 
     spots = jnp.arange(peers, dtype=jnp.int32)
     rank = jnp.sum(

time: 140 us -> 126 us (0.900)
  the two profiles are of different devices: /device:TPU:1 before, /device:TPU:3 now
where the time goes in v5:
time: 126 us
  Pallas kernels  43.8 us (35%)
  starting transfers between devices  30 us (24%)
  waiting for transfers between devices  24.8 us (20%)
  other arithmetic  17.1 us (14%)
  local copies, waits for them, and re-layouts  8.96 us (7%)
    all_to_all x1, waiting for transfers between devices, shards(): lax.all_to_all(outgoing, 'dev', split_axis=0, concat_axis=0, tiled=True)  18.1 us
    all_to_all x1, starting transfers between devices, shards(): lax.all_to_all(back, 'dev', split_axis=0, concat_axis=0, tiled=True)  13.2 us
    pallas_call x1, Pallas kernels, far_field(): pl.pallas_call(far_kernel, out_shape=jax.ShapeDtypeStruct(acc.shape, F32)...  11 us
    pallas_call x1, Pallas kernels, remote_near(): pl.pallas_call(remote_kernel, out_shape=jax.ShapeDtypeStruct(acc.shape, F...  8.94 us
    all_to_all x1, starting transfers between devices, shards(): lax.all_to_all(outgoing, 'dev', split_axis=0, concat_axis=0, tiled=True)  8.13 us
    pallas_call x1, Pallas kernels, reply(): pl.pallas_call(reply_kernel, out_shape=jax.ShapeDtypeStruct((peers, rows...  7.86 us
    ppermute x3, waiting for transfers between devices, shards(): lax.ppermute(same, 'group', [(i, (i + step) % 4) for i in range(4)])  6.71 us
    pallas_call x1, Pallas kernels, prep(): pl.pallas_call(prep_kernel, out_shape=(jax.ShapeDtypeStruct((clusters, ro...  5.79 us
  transfers between devices with their start and end apart: 6, of which 2 were waited for; matrix products, arithmetic and copies ran while one was open for 15% of the time, Pallas kernels for 20%

profile of v5, /device:TPU:3, one launch (start us, length us, event | category | flops | bytes accessed | tf_op | source)
XLA Modules:
  0.0 125.5 jit_solution(7523108103909724214)
XLA Ops:
  0.0 0.8 reshape.49
  0.8 1.4 %fusion.6.axes = f32[3,17,256]{2,1,0:T(8,128)} fusion(bf16[1,1,96]{2,1,0:T(2,128)(2,1)S(1)} %reshape.49, bf16[3,16,256]{2,1,0:T(8,128)(2,1)} %bitcast.51), kind=kLoop, calls=%fused_computation.20 | loop fusion | flops 78336 | bytes 76992 | tf_op jit(solution)/shard_map/convert_element_type | solution.py:373
  2.1 1.3 %pad_add_fusion.2.ints = s32[48]{0:T(128)} fusion(s32[8]{0:T(128)} %bitcast.54, s32[8]{0:T(128)} %bitcast.55, s32[32]{0:T(128)} %bitcast.56), kind=kLoop, calls=%fused_computation.120 | loop fusion | flops 96 | bytes 384 | tf_op jit(solution)/shard_map/concatenate | solution.py:375
  3.4 5.8 %prep.1 = (bf16[16,168,256]{2,1,0:T(8,128)(2,1)}, bf16[16,256,16]{2,1,0:T(8,128)(2,1)}, bf16[32,168,256]{2,1,0:T(8,128)(2,1)}) custom-call(s32[48]{0:T(128)} %pad_add_fusion.2.ints, bf16[16,256,128]{2,1,0:T(8,128)(2,1)} %bitcast.47, f32[3,17,256]{2,1,0:T(8,128)} %fusion.6.axes, bf16[16,32,256]{2,1,0:T(8,128)(2,1)} %basis.3, bf16[16,32,32]{2,1,0:T(8,128)(2,1)} %trans.3, ...), custom_call_target="tpu_custom_call" | custom-call | tf_op jit(solution)/shard_map/prep/pallas_call | solution.py:92
  9.2 0.0 copy-start.10
  9.2 0.0 copy-start.11
  9.3 8.1 %all-to-all-start = ((bf16[32,168,256]{2,1,0:T(8,128)(2,1)}), bf16[32,168,256]{2,1,0:T(8,128)(2,1)}, u32[]{:S(2)}, u32[]{:S(2)}) async-start(bf16[32,168,256]{2,1,0:T(8,128)(2,1)} %get-tuple-element.14), calls=%async_computation | async-start | bytes 5505024 | tf_op jit(solution)/shard_map/all_to_all | solution.py:379
  18.1 0.2 convert_reduce_fusion.1
  18.3 0.6 convert_reduce_fusion.6
  18.9 0.1 convert_reduce_fusion.2
  19.1 0.2 select_reduce_fusion.1
  19.2 1.2 fusion.19
  20.4 0.7 pad_add_fusion.1.pairs
  21.2 0.6 convert_reduce_fusion.5
  21.8 0.1 convert_reduce_fusion
  21.9 0.2 select_reduce_fusion
  22.2 1.2 fusion.18
  23.4 1.3 %pad_add_fusion.pairs = s32[273]{0:T(512)} fusion(s32[272]{0:T(512)S(1)} %fusion.18, s32[1]{0:T(128)} %bitcast.9), kind=kLoop, calls=%fused_computation.54 | loop fusion | flops 273 | bytes 2184 | tf_op jit(solution)/shard_map/concatenate | solution.py:348
  24.7 0.6 convert_reduce_fusion.4.starts
  25.3 0.2 convert_reduce_fusion.3
  25.5 0.7 select_reduce_fusion.2.order
  26.2 4.7 %own_near.1.acc_in = f32[16,128,256]{2,1,0:T(8,128)S(1)} custom-call(s32[273]{0:T(512)S(1)} %pad_add_fusion.1.pairs, bf16[16,168,256]{2,1,0:T(8,128)(2,1)S(1)} %copy-done, bf16[16,256,16]{2,1,0:T(8,128)(2,1)S(1)} %copy-done.1), custom_call_target="tpu_custom_call" | custom-call | flops 6442450944 | bytes 4194304 | tf_op jit(solution)/shard_map/own_near/pallas_call | solution.py:140
  31.0 1.3 %copy-done.2 = f32[16,128,256]{2,1,0:T(8,128)} copy-done((f32[16,128,256]{2,1,0:T(8,128)}, f32[16,128,256]{2,1,0:T(8,128)S(1)}, u32[]{:S(2)}) %copy-start.2) | copy-done | bytes 2097176
  32.3 18.1 %all-to-all-done.incoming = bf16[32,168,256]{2,1,0:T(8,128)(2,1)} async-done(((bf16[32,168,256]{2,1,0:T(8,128)(2,1)}), bf16[32,168,256]{2,1,0:T(8,128)(2,1)}, u32[]{:S(2)}, u32[]{:S(2)}) %all-to-all-start) | async-done | bytes 2752544 | tf_op jit(solution)/shard_map/all_to_all | solution.py:379
  50.4 7.9 %reply.1 = bf16[32,128,256]{2,1,0:T(8,128)(2,1)} custom-call(s32[273]{0:T(512)} %pad_add_fusion.pairs, bf16[16,168,256]{2,1,0:T(8,128)(2,1)} %get-tuple-element.15.stage, bf16[16,256,16]{2,1,0:T(8,128)(2,1)} %get-tuple-element.16.fa, bf16[32,168,256]{2,1,0:T(8,128)(2,1)} %all-to-all-done.incoming), custom_call_target="tpu_custom_call" | custom-call | flops 6442450944 | bytes 8388608 | tf_op jit(solution)/shard_map/reply/pallas_call | solution.py:175
  58.3 13.2 %all-to-all-start.1 = ((bf16[32,128,256]{2,1,0:T(8,128)(2,1)}), bf16[32,128,256]{2,1,0:T(8,128)(2,1)S(1)}, u32[]{:S(2)}, u32[]{:S(2)}) async-start(bf16[32,128,256]{2,1,0:T(8,128)(2,1)} %reply.1), calls=%async_computation.1 | async-start | bytes 4194304 | tf_op jit(solution)/shard_map/all_to_all | solution.py:384
  71.4 1.1 slice.48
  72.6 3.6 %collective-permute-start.2 = (bf16[16,40,256]{2,1,0:T(8,128)(2,1)S(1)}, bf16[16,40,256]{2,1,0:T(8,128)(2,1)S(1)}, u32[]{:S(2)}, u32[]{:S(2)}) collective-permute-start(bf16[16,40,256]{2,1,0:T(8,128)(2,1)S(1)} %dynamic-slice_bitcast_fusion), channel_id=1, source_target_pairs={{0,96},{32,0},{64,32},{96,64},{1,97},{33,1},{65,33},{97,65},{2,98}... | collective-permute-start | bytes 983048 | tf_op jit(solution)/shard_map/ppermute | solution.py:394
  76.2 1.5 %collective-permute-start.1 = (bf16[16,40,256]{2,1,0:T(8,128)(2,1)S(1)}, bf16[16,40,256]{2,1,0:T(8,128)(2,1)S(1)}, u32[]{:S(2)}, u32[]{:S(2)}) collective-permute-start(bf16[16,40,256]{2,1,0:T(8,128)(2,1)S(1)} %dynamic-slice_bitcast_fusion), channel_id=1, source_target_pairs={{0,64},{32,96},{64,0},{96,32},{1,65},{33,97},{65,1},{97,33},{2,66}... | collective-permute-start | bytes 983048 | tf_op jit(solution)/shard_map/ppermute | solution.py:394
  77.7 0.7 constant_dynamic-slice_fusion.1
  78.4 0.1 fusion.32
  78.5 0.1 mul.78
  78.6 0.1 mul.82
  78.7 8.9 %remote_near.1.acc = f32[16,128,256]{2,1,0:T(8,128)} custom-call(s32[273]{0:T(512)} %pad_add_fusion.pairs, bf16[16,256,16]{2,1,0:T(8,128)(2,1)} %get-tuple-element.16.fa, bf16[32,168,256]{2,1,0:T(8,128)(2,1)} %all-to-all-done.incoming, f32[16,128,256]{2,1,0:T(8,128)} %copy-done.2), custom_call_target="tpu_custom_call" | custom-call | flops 6442450944 | bytes 8388608 | tf_op jit(solution)/shard_map/remote_near/pallas_call | solution.py:207
  87.6 6.7 %collective-permute-done = bf16[16,40,256]{2,1,0:T(8,128)(2,1)S(1)} collective-permute-done((bf16[16,40,256]{2,1,0:T(8,128)(2,1)S(1)}, bf16[16,40,256]{2,1,0:T(8,128)(2,1)S(1)}, u32[]{:S(2)}, u32[]{:S(2)}) %collective-permute-start) | collective-permute-done | bytes 327712 | tf_op jit(solution)/shard_map/ppermute | solution.py:394
  94.4 0.7 copy-done.7
  95.1 2.5 %fusion.31 = (bf16[1,4,16,40,256]{4,3,2,1,0:T(8,128)(2,1)S(1)}, bf16[4,16,40,256]{3,2,1,0:T(8,128)(2,1)}) fusion(bf16[1,16,40,256]{3,2,1,0:T(8,128)(2,1)} %bitcast.48, bf16[1,16,40,256]{3,2,1,0:T(8,128)(2,1)} %bitcast.49, bf16[1,16,40,256]{3,2,1,0:T(8,128)(2,1)} %bitcast.50, bf16[1,16,40,256]{3,2,1,0:T(8,128)(2,1)} %bitcast.46), kind=kLoop, calls=%fused_computation.127 | loop fusion | flops 1966080 | bytes 3932160 | tf_op jit(solution)/shard_map/stack | solution.py:398
  97.6 3.6 %collective-permute-start.3 = (bf16[4,16,40,256]{3,2,1,0:T(8,128)(2,1)}, bf16[4,16,40,256]{3,2,1,0:T(8,128)(2,1)}, u32[]{:S(2)}, u32[]{:S(2)}) collective-permute-start(bf16[4,16,40,256]{3,2,1,0:T(8,128)(2,1)} %get-tuple-element.30), channel_id=1, source_target_pairs={{0,1},{1,0},{2,3},{3,2},{4,5},{5,4},{6,7},{7,6},{8,9},{9,8},{10,11... | collective-permute-start | bytes 3932168 | tf_op jit(solution)/shard_map/ppermute | solution.py:397
  101.2 0.1 reshape.60
  101.4 0.1 copy.17
  101.5 0.8 broadcast_in_dim.47
  102.3 1.1 reshape.53
  103.4 0.6 pad.9.own_points
  104.0 0.7 pad_add_fusion.3.ids
  104.7 3.1 %pad_maximum_fusion = bf16[2,4,16,40,256]{4,3,2,1,0:T(8,128)(2,1)} fusion(bf16[1,4,16,40,256]{4,3,2,1,0:T(8,128)(2,1)} %bitcast.18, bf16[1,4,16,40,256]{4,3,2,1,0:T(8,128)(2,1)S(1)} %get-tuple-element.29), kind=kLoop, calls=%fused_computation | loop fusion | flops 1310720 | bytes 5242880 | tf_op jit(solution)/shard_map/stack | solution.py:398
  107.7 11.0 %far_field.1.base = f32[16,128,256]{2,1,0:T(8,128)} custom-call(s32[57]{0:T(128)} %pad_add_fusion.3.ids, f32[3,32,128]{2,1,0:T(8,128)} %pad.9.own_points, bf16[128,40,256]{2,1,0:T(8,128)(2,1)} %bitcast.45, bf16[16,32,32]{2,1,0:T(8,128)(2,1)} %trans.3, f32[16,128,256]{2,1,0:T(8,128)} %remote_near.1.acc, bf16[16,32,256]{2,1,0:T(8,128)(2,1)} %basis.3), custom_call_target="tpu_custom_call" | custom-call | flops 6442450944 | bytes 4194304 | tf_op jit(solution)/shard_map/far_field/pallas_call | solution.py:281
  118.7 1.4 %copy-done.3 = bf16[32,128,256]{2,1,0:T(8,128)(2,1)} copy-done((bf16[32,128,256]{2,1,0:T(8,128)(2,1)}, bf16[32,128,256]{2,1,0:T(8,128)(2,1)S(1)}, u32[]{:S(2)}) %copy-start.3) | copy-done | bytes 2097176
  120.1 5.5 %finish.1 = f32[16,256,128]{2,1,0:T(8,128)} custom-call(s32[32]{0:T(128)} %select_reduce_fusion.2.order, s32[17]{0:T(128)} %convert_reduce_fusion.4.starts, f32[16,128,256]{2,1,0:T(8,128)} %far_field.1.base, bf16[32,128,256]{2,1,0:T(8,128)(2,1)} %copy-done.3), custom_call_target="tpu_custom_call" | custom-call | tf_op jit(solution)/shard_map/finish/pallas_call | solution.py:313
  (40 shorter events, 0.2 us)
Async XLA Ops:
  9.2 8.9 %copy-start.8 = (s32[256]{0:T(256)S(1)}, s32[256]{0:T(256)}, u32[]{:S(2)}) copy-start(s32[256]{0:T(256)} %param.23) | copy-start | bytes 3076
  9.2 8.9 %copy-start.9 = (s32[256]{0:T(256)S(1)}, s32[256]{0:T(256)}, u32[]{:S(2)}) copy-start(s32[256]{0:T(256)} %param.22) | copy-start | bytes 3076
  9.2 9.7 %copy-start.10 = (bf16[1,3,32]{2,1,0:T(4,128)(2,1)S(1)}, bf16[1,3,32]{2,1,0:T(4,128)(2,1)}, u32[]{:S(2)}) copy-start(bf16[1,3,32]{2,1,0:T(4,128)(2,1)} %param.20) | copy-start | bytes 580
  9.2 15.4 %copy-start.11 = (s32[32,1]{0,1:T(1,128)S(1)}, s32[32,1]{0,1:T(1,128)}, u32[]{:S(2)}) copy-start(s32[32,1]{0,1:T(1,128)} %param.21) | copy-start | bytes 388
  9.3 16.9 %copy-start.12 = (s32[1,8]{1,0:T(1,128)S(1)}, s32[1,8]{1,0:T(1,128)}, u32[]{:S(2)}) copy-start(s32[1,8]{1,0:T(1,128)} %param.25) | copy-start | bytes 100
  9.3 17.0 %copy-start = (bf16[16,168,256]{2,1,0:T(8,128)(2,1)S(1)}, bf16[16,168,256]{2,1,0:T(8,128)(2,1)}, u32[]{:S(2)}) copy-start(bf16[16,168,256]{2,1,0:T(8,128)(2,1)} %get-tuple-element.15.stage) | copy-start | bytes 4128772
  9.3 17.0 %copy-start.1 = (bf16[16,256,16]{2,1,0:T(8,128)(2,1)S(1)}, bf16[16,256,16]{2,1,0:T(8,128)(2,1)}, u32[]{:S(2)}) copy-start(bf16[16,256,16]{2,1,0:T(8,128)(2,1)} %get-tuple-element.16.fa) | copy-start | bytes 393220
  9.3 41.1 %all-to-all-start = ((bf16[32,168,256]{2,1,0:T(8,128)(2,1)}), bf16[32,168,256]{2,1,0:T(8,128)(2,1)}, u32[]{:S(2)}, u32[]{:S(2)}) async-start(bf16[32,168,256]{2,1,0:T(8,128)(2,1)} %get-tuple-element.14), calls=%async_computation | async-start | bytes 5505024 | tf_op jit(solution)/shard_map/all_to_all | solution.py:379
  31.0 1.3 %copy-start.2 = (f32[16,128,256]{2,1,0:T(8,128)}, f32[16,128,256]{2,1,0:T(8,128)S(1)}, u32[]{:S(2)}) copy-start(f32[16,128,256]{2,1,0:T(8,128)S(1)} %own_near.1.acc_in) | copy-start | bytes 6291460
  58.3 60.4 %all-to-all-start.1 = ((bf16[32,128,256]{2,1,0:T(8,128)(2,1)}), bf16[32,128,256]{2,1,0:T(8,128)(2,1)S(1)}, u32[]{:S(2)}, u32[]{:S(2)}) async-start(bf16[32,128,256]{2,1,0:T(8,128)(2,1)} %reply.1), calls=%async_computation.1 | async-start | bytes 4194304 | tf_op jit(solution)/shard_map/all_to_all | solution.py:384
  72.6 15.0 %copy-start.4 = (bf16[16,40,256]{2,1,0:T(8,128)(2,1)}, bf16[16,40,256]{2,1,0:T(8,128)(2,1)S(1)}, u32[]{:S(2)}) copy-start(bf16[16,40,256]{2,1,0:T(8,128)(2,1)S(1)} %dynamic-slice_bitcast_fusion) | copy-start | bytes 983044
  72.6 15.0 %collective-permute-start.2 = (bf16[16,40,256]{2,1,0:T(8,128)(2,1)S(1)}, bf16[16,40,256]{2,1,0:T(8,128)(2,1)S(1)}, u32[]{:S(2)}, u32[]{:S(2)}) collective-permute-start(bf16[16,40,256]{2,1,0:T(8,128)(2,1)S(1)} %dynamic-slice_bitcast_fusion), channel_id=1, source_target_pairs={{0,96},{32,0},{64,32},{96,64},{1,97},{33,1},{65,33},{97,65},{2,98}... | collective-permute-start | bytes 983048 | tf_op jit(solution)/shard_map/ppermute | solution.py:394
  76.2 11.4 %collective-permute-start.1 = (bf16[16,40,256]{2,1,0:T(8,128)(2,1)S(1)}, bf16[16,40,256]{2,1,0:T(8,128)(2,1)S(1)}, u32[]{:S(2)}, u32[]{:S(2)}) collective-permute-start(bf16[16,40,256]{2,1,0:T(8,128)(2,1)S(1)} %dynamic-slice_bitcast_fusion), channel_id=1, source_target_pairs={{0,64},{32,96},{64,0},{96,32},{1,65},{33,97},{65,1},{97,33},{2,66}... | collective-permute-start | bytes 983048 | tf_op jit(solution)/shard_map/ppermute | solution.py:394
  77.7 16.7 %collective-permute-start = (bf16[16,40,256]{2,1,0:T(8,128)(2,1)S(1)}, bf16[16,40,256]{2,1,0:T(8,128)(2,1)S(1)}, u32[]{:S(2)}, u32[]{:S(2)}) collective-permute-start(bf16[16,40,256]{2,1,0:T(8,128)(2,1)S(1)} %dynamic-slice_bitcast_fusion), channel_id=1, source_target_pairs={{0,32},{32,64},{64,96},{96,0},{1,33},{33,65},{65,97},{97,1},{2,34}... | collective-permute-start | bytes 983048 | tf_op jit(solution)/shard_map/ppermute | solution.py:394
  87.6 6.7 %copy-start.5 = (bf16[16,40,256]{2,1,0:T(8,128)(2,1)}, bf16[16,40,256]{2,1,0:T(8,128)(2,1)S(1)}, u32[]{:S(2)}) copy-start(bf16[16,40,256]{2,1,0:T(8,128)(2,1)S(1)} %collective-permute-done.2) | copy-start | bytes 983044
  87.6 6.7 %copy-start.6 = (bf16[16,40,256]{2,1,0:T(8,128)(2,1)}, bf16[16,40,256]{2,1,0:T(8,128)(2,1)S(1)}, u32[]{:S(2)}) copy-start(bf16[16,40,256]{2,1,0:T(8,128)(2,1)S(1)} %collective-permute-done.1) | copy-start | bytes 983044
  94.3 0.7 copy-start.7
  97.6 7.1 %collective-permute-start.3 = (bf16[4,16,40,256]{3,2,1,0:T(8,128)(2,1)}, bf16[4,16,40,256]{3,2,1,0:T(8,128)(2,1)}, u32[]{:S(2)}, u32[]{:S(2)}) collective-permute-start(bf16[4,16,40,256]{3,2,1,0:T(8,128)(2,1)} %get-tuple-element.30), channel_id=1, source_target_pairs={{0,1},{1,0},{2,3},{3,2},{4,5},{5,4},{6,7},{7,6},{8,9},{9,8},{10,11... | collective-permute-start | bytes 3932168 | tf_op jit(solution)/shard_map/ppermute | solution.py:397
  118.7 1.4 %copy-start.3 = (bf16[32,128,256]{2,1,0:T(8,128)(2,1)}, bf16[32,128,256]{2,1,0:T(8,128)(2,1)S(1)}, u32[]{:S(2)}) copy-start(bf16[32,128,256]{2,1,0:T(8,128)(2,1)S(1)} %all-to-all-done.1.returned) | copy-start | bytes 6291460

commit v6 on v5

v6 whole, which is shorter than its diff:
```python
import functools

import jax
import jax.numpy as jnp
from jax import lax
from jax.experimental import pallas as pl
from jax.experimental.pallas import tpu as pltpu
from jax.sharding import PartitionSpec as P

KCOEF = 0.005
DELTA = 0.02
F32 = jnp.float32
BF16 = jnp.bfloat16
GROUP = 8
FEAT = 16
VMEM = pl.BlockSpec(memory_space=pltpu.VMEM)
SMEM = pl.BlockSpec(memory_space=pltpu.SMEM)
ANY = pl.BlockSpec(memory_space=pl.ANY)
MESH = pl.DeviceIdType.MESH
TAIL = 512
ROUTE = (
    (3, 2, 1), (0, 1, 1), (1, 2, 0), (2, 1, 0), (1, 2, 1), (3, 0, 0), (3, 3, 0), (0, 0, 1),
    (3, 1, 0), (3, 0, 1), (0, 2, 0), (1, 1, 1), (2, 2, 1), (3, 2, 0), (1, 3, 1), (1, 0, 0),
    (3, 3, 1), (2, 0, 1), (1, 3, 0), (2, 3, 0), (3, 1, 1), (2, 2, 0), (1, 0, 1), (0, 3, 0),
    (2, 0, 0), (0, 1, 0), (0, 2, 1), (2, 1, 1), (2, 3, 1), (0, 3, 1), (1, 1, 0),
)
MESH = pl.DeviceIdType.MESH
PARAMS = pltpu.CompilerParams(vmem_limit_bytes=14 << 20)
WIDE = pltpu.CompilerParams(vmem_limit_bytes=56 << 20)


def dot(left, right, dims=((1,), (0,))):
    return lax.dot_general(left, right, (dims, ((), ())), preferred_element_type=F32)


def halves(value):
    high = value.astype(BF16)
    return high, (value - high.astype(F32)).astype(BF16)


def thirds(value):
    high = value.astype(BF16)
    rest = value - high.astype(F32)
    mid = rest.astype(BF16)
    return high.astype(F32), mid.astype(F32), (rest - mid.astype(F32))


def pair_lists(first, second, count, lists, weights):
    lane = lax.broadcasted_iota(jnp.int32, first.shape, 1)
    own = second < 16
    a = jnp.where(own, jnp.minimum(first, second), first)
    b = jnp.where(own, jnp.maximum(first, second), second)
    b = jnp.where(lane < count, b, 64)

    def hot(rows, index):
        spot = lax.broadcasted_iota(jnp.int32, (rows, first.shape[1]), 0)
        return jnp.where(spot == index, 1.0, 0.0).astype(BF16)

    times = dot(hot(48, b), hot(16, a), ((1,), (1,)))
    row = lax.broadcasted_iota(jnp.int32, times.shape, 0)
    col = lax.broadcasted_iota(jnp.int32, times.shape, 1)
    held = jnp.where(times > 0, 1.0, 0.0)
    twice = jnp.where(row == col, times, 2.0 * times)
    key = (jnp.where(row < 16, row, row - 16) * 16 + col).astype(F32)
    up_r = lax.broadcasted_iota(jnp.int32, (16, 16), 0)
    up_c = lax.broadcasted_iota(jnp.int32, (16, 16), 1)
    within = dot(held.astype(BF16), jnp.where(up_r < up_c, 1.0, 0.0).astype(BF16))
    low_r = lax.broadcasted_iota(jnp.int32, (48, 48), 0)
    low_c = lax.broadcasted_iota(jnp.int32, (48, 48), 1)
    below = (low_c < low_r) & ((low_c >= 16) | (low_r < 16))
    above = jnp.sum(dot(jnp.where(below, 1.0, 0.0).astype(BF16), held.astype(BF16)), axis=1, keepdims=True)
    rank = jnp.where(held > 0, above + within + 1.0, -1.0)
    value = key + 1024.0 * twice
    slot = lax.broadcasted_iota(jnp.int32, (48, TAIL), 1).astype(F32)
    code = jnp.zeros((48, TAIL), F32)
    for i in range(16):
        code += jnp.where(rank[:, i : i + 1] == slot, value[:, i : i + 1], 0.0)
    for i, (lo, hi) in enumerate(((0, 16), (16, 48))):
        total = jnp.sum(jnp.sum(held[lo:hi], axis=1, keepdims=True), axis=0, keepdims=True)
        last = jnp.max(jnp.max((held * key)[lo:hi], axis=1, keepdims=True), axis=0, keepdims=True)
        mine = jnp.sum(code[lo:hi], axis=0, keepdims=True)
        mine = jnp.where(slot[:1] > total, last, mine)
        lists[i : i + 1] = jnp.where(slot[:1] == 0, total, mine).astype(jnp.int32)
    turned = dot(hot(16, a), hot(48, b), ((1,), (1,)))
    line = lax.broadcasted_iota(jnp.int32, (16, 128), 0)
    for i in range(16):
        part = jnp.broadcast_to(turned[:, i : i + 1], (16, 128))
        weights[i] = jnp.where(line == i, 0.5 * part, part)


def exchange_kernel(
    ints, pairs, charges, axes, basis, trans, pair, quad,
    stage, fa, incoming, nodes, lists, acc,
    rows_a, rows_b, outgoing, weights, kbuf, team_send, team_recv, node_send, node_recv, own_sem,
):
    clusters, _, rhs = charges.shape
    width = stage.shape[2]
    z, d = lax.axis_index("group"), lax.axis_index("dev")
    x, y, c = d // 8, lax.rem(d // 2, 4), lax.rem(d, 2)

    def member(x, y, c):
        return (x * 4 + y) * 2 + c

    def turn(i, k):
        return lax.rem(i + k, 4)

    team = [member(turn(x, i), turn(y, j), lax.rem(c + k, 2)) for i, j, k in ROUTE]
    barrier = pltpu.get_barrier_semaphore()
    for peer in team:
        pl.semaphore_signal(barrier, inc=1, device_id={"group": z, "dev": peer}, device_id_type=MESH)
    for k in (1, 2, 3):
        pl.semaphore_signal(barrier, inc=1, device_id={"group": turn(z, k), "dev": d}, device_id_type=MESH)

    total = jnp.zeros((trans.shape[1], rhs), F32)
    for i in range(clusters):
        leaf = dot(basis[i], charges[i]).astype(BF16)
        total += dot(trans[i], leaf)
    top = total.astype(BF16)
    mats = [mat[0].astype(F32) for mat in (pair, quad)]
    moves = jnp.concatenate([mat[8 * i : 8 * i + 8] for mat in mats for i in range(4)], axis=1)
    lane = lax.broadcasted_iota(jnp.int32, (1, width), 1)
    points = [axes[i, clusters : clusters + 1] for i in range(3)]
    info = points[0] + pltpu.roll(points[1], 32, 1) + pltpu.roll(points[2], 64, 1)
    for i in range(16):
        info = jnp.where(lane == rhs + i, ints[32 + i].astype(F32), info)
    line = lax.broadcasted_iota(jnp.int32, (8, width), 0)
    info = jnp.where(line == 0, jnp.broadcast_to(info, (8, width)), 0.0)
    me = ((c * 4 + z) * 4 + y) * 4 + x
    nodes[me, :16] = jnp.concatenate([top[:16], top[16:]], axis=1)
    nodes[me, 16:] = jnp.concatenate([moves, info], axis=0).astype(BF16)

    def node_copy(start, length, sem, peer):
        held = nodes.at[pl.ds(start, length)]
        return pltpu.make_async_remote_copy(
            src_ref=held,
            dst_ref=held,
            send_sem=node_send.at[sem],
            recv_sem=node_recv.at[sem],
            device_id=peer,
            device_id_type=MESH,
        )

    pl.semaphore_wait(barrier, 34)
    along_x = [node_copy(me, 1, k, {"group": z, "dev": member(turn(x, k + 1), y, c)}) for k in range(3)]
    for copy in along_x:
        copy.start()

    point = [axes[i, :clusters] for i in range(3)]
    norm = point[0] * point[0] + point[1] * point[1] + point[2] * point[2]
    one = jnp.ones_like(norm)
    rows_a[...] = jnp.zeros_like(rows_a)
    rows_b[...] = jnp.zeros_like(rows_b)
    for i, row in enumerate((*point, *thirds(norm + DELTA * DELTA), one, one, one)):
        rows_a[:, i, :] = row
    for i, row in enumerate((*(-2.0 * p for p in point), one, one, one, *thirds(norm))):
        rows_b[:, i, :] = row
    for i in range(clusters):
        stage[i, :rhs] = charges[i].T
        stage[i, rhs:] = rows_b[i].astype(BF16)

    for copy in along_x:
        copy.wait_recv()
    start = (c * 4 + z) * 16
    along_y = [
        node_copy(start + y * 4, 4, 3 + k, {"group": z, "dev": member(x, turn(y, k + 1), c)}) for k in range(3)
    ]
    for copy in along_y:
        copy.start()

    sent = []

    def send(i):
        outgoing[i] = stage[ints[team[i]]]
        copy = pltpu.make_async_remote_copy(
            src_ref=outgoing.at[i],
            dst_ref=incoming.at[d],
            send_sem=team_send.at[i],
            recv_sem=team_recv.at[i],
            device_id={"group": z, "dev": team[i]},
            device_id_type=MESH,
        )
        copy.start()
        sent.append(copy)

    for i in range(4):
        send(i)
    for i in range(clusters):
        fa[i] = rows_a[i].T.astype(BF16)
    pair_lists(pairs[:1], pairs[1:2], ints[48], lists, weights)
    for copy in along_y:
        copy.wait_recv()
    along_z = []
    for i in range(4, 31):
        send(i)
        if i % 2 == 0 and len(along_z) < 12:
            part, k = divmod(len(along_z), 3)
            peer = {"group": turn(z, k + 1), "dev": d}
            along_z.append(node_copy(start + part * 4, 4, 6 + len(along_z), peer))
            along_z[-1].start()
    outgoing[31] = stage[ints[d]]
    own = pltpu.make_async_copy(outgoing.at[31], incoming.at[d], own_sem)
    own.start()
    chip = {"group": z, "dev": member(x, y, 1 - c)}
    across = [node_copy(start, 16, 18, chip)]
    across[0].start()

    acc[...] = jnp.zeros_like(acc)

    def entries(i, t):
        low = t <= i
        return jnp.where(low, t, t - i - 1), jnp.where(low, i, 15 - i)

    def near(i, carry):
        for t in range(17):
            a, b = entries(i, t)
            s = dot(fa[a], stage[b, rhs:])
            k = lax.rsqrt(s.astype(BF16))
            line = weights[b, pl.ds(a, 1), :].astype(BF16)
            kbuf[t] = k * jnp.concatenate([line, line], axis=1)
        for t in range(17):
            a, b = entries(i, t)
            acc[a] += dot(stage[b, :rhs], kbuf[t], ((1,), (1,)))
            acc[b] += dot(stage[a, :rhs], kbuf[t])
        return carry

    lax.fori_loop(0, 8, near, 0)

    for k in range(3):
        for part in range(4):
            along_z[part * 3 + k].wait_recv()
        across.append(node_copy((c * 4 + turn(z, 3 - k)) * 16, 16, 19 + k, chip))
        across[-1].start()
    for copy in across:
        copy.wait_recv()
    for copy in sent:
        copy.wait_recv()
    own.wait()
    for copy in (*along_x, *along_y, *along_z, *across, *sent):
        copy.wait_send()


def exchange(ints, pairs, charges, axes, basis, trans, pair, quad):
    clusters, width, rhs = charges.shape
    rows = rhs + FEAT
    return pl.pallas_call(
        exchange_kernel,
        out_shape=(
            jax.ShapeDtypeStruct((clusters, rows, width), BF16),
            jax.ShapeDtypeStruct((clusters, width, FEAT), BF16),
            jax.ShapeDtypeStruct((32, rows, width), BF16),
            jax.ShapeDtypeStruct((128, 32, width), BF16),
            jax.ShapeDtypeStruct((2, TAIL), jnp.int32),
            jax.ShapeDtypeStruct((clusters, rhs, width), F32),
        ),
        in_specs=[SMEM] + [VMEM] * 7,
        out_specs=(VMEM, VMEM, ANY, VMEM, VMEM, VMEM),
        scratch_shapes=[pltpu.VMEM((clusters, FEAT, width), F32)] * 2
        + [
            pltpu.VMEM((32, rows, width), BF16),
            pltpu.VMEM((16, 16, 128), F32),
            pltpu.VMEM((17, width, width), BF16),
            pltpu.SemaphoreType.DMA((31,)),
            pltpu.SemaphoreType.DMA((31,)),
            pltpu.SemaphoreType.DMA((22,)),
            pltpu.SemaphoreType.DMA((22,)),
            pltpu.SemaphoreType.DMA,
        ],
        compiler_params=pltpu.CompilerParams(
            vmem_limit_bytes=56 << 20, collective_id=0, has_side_effects=True
        ),
        name="exchange",
    )(ints, pairs, charges, axes, basis, trans, pair, quad)


def unpack(code):
    return code & 15, (code >> 4) & 63, (code >> 10).astype(F32) * 0.5


def tile(code, fa, table):
    a, b, times = unpack(code)
    s = dot(fa[a], table[b, table.shape[1] - FEAT :])
    return lax.rsqrt(s.astype(BF16)) * times.astype(BF16)


def reply_kernel(pairs, stage, fa, incoming, back, kbuf):
    rhs, width = back.shape[1:]
    back[...] = jnp.zeros_like(back)
    for g in range(GROUP):
        kbuf[0, g] = tile(pairs[1, 1 + g], fa, incoming)

    def body(i, total):
        now = lax.rem(i, 2)
        for g in range(GROUP):
            j = 1 + i * GROUP + g
            a, b, _ = unpack(pairs[1, j])
            before = unpack(pairs[1, jnp.maximum(j - 1, 1)])[1]
            keep = jnp.where(before == b, 1.0, 0.0).astype(F32)
            total = total * keep + dot(stage[a, :rhs], kbuf[now, g])
            back[b] = total.astype(BF16)
            kbuf[1 - now, g] = tile(pairs[1, j + GROUP], fa, incoming)
        return total

    lax.fori_loop(0, pl.cdiv(pairs[1, 0], GROUP), body, jnp.zeros((rhs, width), F32))


def reply(pairs, stage, fa, incoming):
    peers, rows, width = incoming.shape
    return pl.pallas_call(
        reply_kernel,
        out_shape=jax.ShapeDtypeStruct((peers, rows - FEAT, width), BF16),
        in_specs=[SMEM] + [VMEM] * 3,
        out_specs=VMEM,
        scratch_shapes=[pltpu.VMEM((2, GROUP, width, width), BF16)],
        compiler_params=WIDE,
        cost_estimate=pl.CostEstimate(flops=6 << 30, bytes_accessed=8 << 20, transcendentals=0),
        name="reply",
    )(pairs, stage, fa, incoming)


def remote_kernel(pairs, fa, incoming, acc_in, acc, kbuf):
    rhs = acc.shape[1]
    acc[...] = acc_in[...]
    for g in range(GROUP):
        kbuf[0, g] = tile(pairs[1, 1 + g], fa, incoming)

    def body(i, carry):
        now = lax.rem(i, 2)
        for g in range(GROUP):
            j = 1 + i * GROUP + g
            a, b, _ = unpack(pairs[1, j])
            acc[a] += dot(incoming[b, :rhs], kbuf[now, g], ((1,), (1,)))
            kbuf[1 - now, g] = tile(pairs[1, j + GROUP], fa, incoming)
        return carry

    lax.fori_loop(0, pl.cdiv(pairs[1, 0], GROUP), body, 0)


def remote_near(pairs, fa, incoming, acc):
    width = acc.shape[2]
    return pl.pallas_call(
        remote_kernel,
        out_shape=jax.ShapeDtypeStruct(acc.shape, F32),
        in_specs=[SMEM] + [VMEM] * 3,
        out_specs=VMEM,
        scratch_shapes=[pltpu.VMEM((2, GROUP, width, width), BF16)],
        compiler_params=WIDE,
        cost_estimate=pl.CostEstimate(flops=6 << 30, bytes_accessed=8 << 20, transcendentals=0),
        name="remote_near",
    )(pairs, fa, incoming, acc)


def far_kernel(ids, own_points, nodes, trans, acc, basis, base):
    rank = 32

    def skel(n):
        rows = nodes[n, :16, :]
        return jnp.concatenate([rows[:, :128], rows[:, 128:]], axis=0)

    def transfer(n, which):
        rows = nodes[n, 16:, 128 * which : 128 * which + 128].astype(F32)
        return jnp.concatenate([rows[:8, 32 * i : 32 * i + 32] for i in range(4)], axis=0).astype(BF16)

    def points(n):
        return nodes[n, 16:, :128].astype(F32)[8:9]

    def kernel_tile(mine, theirs):
        gap = mine - theirs
        sq = gap * gap
        s = ((DELTA * DELTA + sq[:, :32]) + sq[:, 32:64]) + sq[:, 64:96]
        return halves(KCOEF * lax.rsqrt(s))

    def apply(tile, source):
        return dot(tile[0], source) + dot(tile[1], source)

    mine = [own_points[level] for level in range(3)]
    zero = jnp.zeros((rank, 128), F32)

    def one(f, total):
        n = ids[f]
        return total + apply(kernel_tile(mine[0], points(n)), skel(n))

    def two(f, total):
        n, m = ids[8 + f], ids[8 + f] + 64
        source = dot(transfer(n, 0), skel(n)) + dot(transfer(m, 0), skel(m))
        theirs = 0.5 * (points(n) + points(m))
        return total + apply(kernel_tile(mine[1], theirs), source.astype(BF16))

    def three(f, total):
        n = [ids[24 + f] + step for step in (0, 64, 4, 68)]
        terms = [dot(transfer(i, 1), skel(i)) for i in n]
        source = (terms[0] + terms[1]) + (terms[2] + terms[3])
        left = 0.5 * (points(n[0]) + points(n[1]))
        right = 0.5 * (points(n[2]) + points(n[3]))
        return total + apply(kernel_tile(mine[2], 0.5 * (left + right)), source.astype(BF16))

    far_one = lax.fori_loop(0, 8, one, zero, unroll=True)
    far_two = lax.fori_loop(0, 16, two, zero, unroll=4)
    far_three = lax.fori_loop(0, 32, three, zero, unroll=4)
    me = ids[56]

    def down_by(which, value):
        high, low = halves(value)
        mat = transfer(me, which)
        return dot(mat, high, ((0,), (0,))) + dot(mat, low, ((0,), (0,)))

    down = far_one + down_by(0, far_two) + down_by(1, far_three)
    high, low = halves(down.T)
    for c in range(trans.shape[0]):
        leaf = (dot(high, trans[c]) + dot(low, trans[c])).astype(BF16)
        base[c] = acc[c] * KCOEF + dot(leaf, basis[c])


def far_field(ids, own_points, nodes, trans, acc, basis):
    return pl.pallas_call(
        far_kernel,
        out_shape=jax.ShapeDtypeStruct(acc.shape, F32),
        in_specs=[SMEM] + [VMEM] * 5,
        out_specs=VMEM,
        compiler_params=WIDE,
        cost_estimate=pl.CostEstimate(flops=6 << 30, bytes_accessed=4 << 20, transcendentals=0),
        name="far_field",
    )(ids, own_points, nodes, trans, acc, basis)


def final_kernel(order, starts, base, returned, out, rows, sems):
    clusters = base.shape[0]

    def copy(c):
        return pltpu.make_async_copy(rows.at[c], out.at[c], sems.at[c])

    for c in range(clusters):

        def collect(i, total):
            return total + returned[order[i]].astype(F32)

        zero = jnp.zeros(base.shape[1:], F32)
        total = lax.fori_loop(starts[c], starts[c + 1], collect, zero)
        rows[c] = (base[c] + KCOEF * total).T
        copy(c).start()
    for c in range(clusters):
        copy(c).wait()


def finish(order, starts, base, returned):
    clusters, conductors, width = base.shape
    return pl.pallas_call(
        final_kernel,
        out_shape=jax.ShapeDtypeStruct((clusters, width, conductors), F32),
        in_specs=[SMEM] * 2 + [VMEM] * 2,
        out_specs=pl.BlockSpec(memory_space=pl.ANY),
        scratch_shapes=[
            pltpu.VMEM((clusters, width, conductors), F32),
            pltpu.SemaphoreType.DMA((clusters,)),
        ],
        compiler_params=WIDE,
        name="finish",
    )(order, starts, base, returned)


def shards(
    charges,
    panel_coords,
    cluster_basis,
    trans_leaf,
    trans_pair,
    trans_quad,
    skel_points,
    send_slots,
    pair_first,
    pair_second,
    pair_count,
    far_one,
    far_two,
    far_three,
):
    clusters, _, width = panel_coords.shape
    conductors = charges.shape[1]
    peers = lax.axis_size("dev")
    blocks = charges.reshape(clusters, width, conductors)
    points = jnp.pad(skel_points[0][:, None, :], ((0, 0), (0, 0), (0, width - skel_points.shape[2])))
    axes = jnp.concatenate([jnp.swapaxes(panel_coords, 0, 1), points], axis=1).astype(F32)
    ints = jnp.concatenate([send_slots[:, 0], far_two[0], far_three[0], pair_count])
    pairs = jnp.stack([pair_first, pair_second])
    stage, fa, incoming, nodes, lists, acc = exchange(
        ints, pairs, blocks, axes, cluster_basis, trans_leaf, trans_pair, trans_quad
    )
    back = reply(lists, stage, fa, incoming)
    returned = lax.all_to_all(back, "dev", split_axis=0, concat_axis=0, tiled=True)
    acc = remote_near(lists, fa, incoming, acc)

    z, d = lax.axis_index("group"), lax.axis_index("dev")
    x, y = d // 8, d // 2 % 4

    def place(owner):
        z, d = owner // peers, owner % peers
        return ((d % 2 * 4 + z) * 4 + d // 2 % 4) * 4 + d // 8

    quad = lax.dynamic_slice(
        nodes.reshape(2, 4, 4, 4, 32, width), (0, z, y // 2 * 2, x, 24, 0), (2, 1, 2, 1, 1, width)
    )
    quad = jnp.swapaxes(quad.reshape(2, 2, width), 0, 1).reshape(4, width)
    quad_lists = quad[:, 128:144].astype(jnp.int32)
    pair_list = lax.dynamic_slice_in_dim(quad_lists[:, :8], d % 4 // 2 * 2, 2, axis=0)
    ids = jnp.concatenate(
        [
            place(far_one[0]),
            place(2 * pair_list.reshape(-1)),
            place(4 * quad_lists[:, 8:].reshape(-1)),
            place(z * peers + d).reshape(1),
        ]
    )
    quad_points = quad[:, :96].astype(F32).reshape(4, 3, 32)
    pair_points = 0.5 * (quad_points[0::2] + quad_points[1::2])
    own_points = jnp.stack(
        [
            skel_points[0].astype(F32),
            lax.dynamic_index_in_dim(pair_points, d % 4 // 2, axis=0, keepdims=False),
            0.5 * (pair_points[0] + pair_points[1]),
        ]
    )
    own_points = jnp.repeat(jnp.swapaxes(own_points, 1, 2), 32, axis=2)
    own_points = jnp.pad(own_points, ((0, 0), (0, 0), (0, 32)))
    base = far_field(ids, own_points, nodes, trans_leaf, acc, cluster_basis)

    slots = send_slots[:, 0]
    spots = jnp.arange(peers, dtype=jnp.int32)
    rank = jnp.sum(
        (slots[None, :] < slots[:, None])
        | ((slots[None, :] == slots[:, None]) & (spots[None, :] < spots[:, None])),
        axis=1,
        dtype=jnp.int32,
    )
    order = jnp.sum(jnp.where(rank[None, :] == spots[:, None], spots[None, :], 0), axis=1)
    edges = jnp.arange(clusters + 1, dtype=jnp.int32)
    starts = jnp.sum(slots[None, :] < edges[:, None], axis=1, dtype=jnp.int32)
    out = finish(order, starts, base, returned)
    return out.reshape(clusters * width, conductors)


def solution(mesh):
    owners = ("group", "dev")
    rows, block, flat = P(owners, None), P(owners, None, None), P(owners)
    placed = (rows, *(block,) * 6, rows, *(flat,) * 3, *(rows,) * 3)
    return jax.shard_map(shards, mesh=mesh, in_specs=placed, out_specs=rows, check_vma=False)
```

time: 126 us -> 114 us (0.905)
  the two profiles are of different devices: /device:TPU:3 before, /device:TPU:43 now
where the time goes in v6:
time: 114 us
  Pallas kernels  97.5 us (86%)
  other arithmetic  6.36 us (6%)
  starting transfers between devices  5.09 us (4%)
  local copies, waits for them, and re-layouts  4.02 us (4%)
    pallas_call x1, Pallas kernels, exchange(): pl.pallas_call(exchange_kernel, out_shape=(jax.ShapeDtypeStruct((clusters...  48 us
    pallas_call x1, Pallas kernels, remote_near(): pl.pallas_call(remote_kernel, out_shape=jax.ShapeDtypeStruct(acc.shape, F...  17.8 us
    pallas_call x1, Pallas kernels, reply(): pl.pallas_call(reply_kernel, out_shape=jax.ShapeDtypeStruct((peers, rows...  15.5 us
    pallas_call x1, Pallas kernels, far_field(): pl.pallas_call(far_kernel, out_shape=jax.ShapeDtypeStruct(acc.shape, F32)...  10.7 us
    pallas_call x1, Pallas kernels, finish(): pl.pallas_call(final_kernel, out_shape=jax.ShapeDtypeStruct((clusters, wi...  5.48 us
    all_to_all x1, starting transfers between devices, shards(): lax.all_to_all(back, 'dev', split_axis=0, concat_axis=0, tiled=True)  5.09 us
  transfers between devices with their start and end apart: 1, of which 0 were waited for; matrix products, arithmetic and copies ran while one was open for 4% of the time, Pallas kernels for 25%

profile of v6, /device:TPU:43, one launch (start us, length us, event | category | flops | bytes accessed | tf_op | source)
XLA Modules:
  0.0 114.0 jit_solution(14086848780478506327)
XLA Ops:
  0.7 0.7 copy.24
  1.3 1.3 %pad_add_fusion.pairs = s32[2,256]{1,0:T(2,128)} fusion(s32[1,256]{1,0:T(1,128)} %bitcast.36, s32[1,256]{1,0:T(1,128)} %bitcast.37), kind=kLoop, calls=%fused_computation.22 | loop fusion | flops 512 | bytes 4096 | tf_op jit(solution)/shard_map/stack | solution.py:483
  2.6 1.4 %fusion.2.axes = f32[3,17,256]{2,1,0:T(8,128)} fusion(bf16[3,1,32]{2,1,0:T(2,128)(2,1)S(1)} %copy.24, bf16[3,16,256]{2,1,0:T(8,128)(2,1)} %bitcast.33), kind=kLoop, calls=%fused_computation.3 | loop fusion | flops 78336 | bytes 76992 | tf_op jit(solution)/shard_map/convert_element_type | solution.py:481
  4.0 1.3 %pad_add_fusion.1.ints = s32[49]{0:T(128)} fusion(s32[1]{0:T(128)S(6)} %copy.32, s32[8]{0:T(128)} %bitcast.38, s32[8]{0:T(128)} %bitcast.39, s32[32]{0:T(128)} %bitcast.40), kind=kLoop, calls=%fused_computation.84 | loop fusion | flops 147 | bytes 392 | tf_op jit(solution)/shard_map/concatenate | solution.py:482
  5.3 48.0 %exchange.1 = (bf16[16,144,256]{2,1,0:T(8,128)(2,1)}, bf16[16,256,16]{2,1,0:T(8,128)(2,1)}, bf16[32,144,256]{2,1,0:T(8,128)(2,1)}, bf16[128,32,256]{2,1,0:T(8,12...) custom-call(s32[49]{0:T(128)} %pad_add_fusion.1.ints, s32[2,256]{1,0:T(2,128)} %pad_add_fusion.pairs, ...), custom_call_target="tpu_custom_call" | custom-call | tf_op jit(solution)/shard_map/exchange/pallas_call | solution.py:245
  53.3 15.5 %reply.1 = bf16[32,128,256]{2,1,0:T(8,128)(2,1)} custom-call(s32[2,512]{1,0:T(2,128)} %get-tuple-element.12.pairs, bf16[16,144,256]{2,1,0:T(8,128)(2,1)} %get-tuple-element.16.stage, bf16[16,256,16]{2,1,0:T(8,128)(2,1)} %get-tuple-element.13.fa, bf16[32,144,256]{2,1,0:T(8,128)(2,1)} %get-tuple-element.14.incoming), custom_call_target="tpu_custom_call" | custom-call | flops 6442450944 | bytes 8388608 | tf_op jit(solution)/shard_map/reply/pallas_call | solution.py:308
  68.9 0.0 copy-start.1
  68.9 0.0 copy-start.3
  68.9 0.0 copy-start.2
  68.9 5.1 %all-to-all-start = ((bf16[32,128,256]{2,1,0:T(8,128)(2,1)}), bf16[32,128,256]{2,1,0:T(8,128)(2,1)S(1)}, u32[]{:S(2)}, u32[]{:S(2)}) async-start(bf16[32,128,256]{2,1,0:T(8,128)(2,1)} %reply.1), calls=%async_computation | async-start | bytes 4194304 | tf_op jit(solution)/shard_map/all_to_all | solution.py:488
  74.1 0.0 copy-done.1
  74.2 0.7 constant_dynamic-slice_fusion.1
  75.0 0.0 copy-done.3
  75.0 0.1 fusion.18
  75.1 0.1 mul.76
  75.2 0.1 mul.81
  75.3 0.1 reshape.45
  75.4 0.1 copy.27
  75.5 0.2 broadcast_in_dim.9
  75.7 0.1 reshape.42
  75.8 0.6 pad.9.own_points
  76.5 0.7 pad_add_fusion.2.ids
  77.1 0.0 copy-done.2
  77.1 0.7 convert_reduce_fusion.1.starts
  77.8 0.2 convert_reduce_fusion
  78.0 0.7 select_reduce_fusion.order
  78.7 17.8 %remote_near.1.acc = f32[16,128,256]{2,1,0:T(8,128)} custom-call(s32[2,512]{1,0:T(2,128)} %get-tuple-element.12.pairs, bf16[16,256,16]{2,1,0:T(8,128)(2,1)} %get-tuple-element.13.fa, bf16[32,144,256]{2,1,0:T(8,128)(2,1)} %get-tuple-element.14.incoming, f32[16,128,256]{2,1,0:T(8,128)} %get-tuple-element.15.acc_in), custom_call_target="tpu_custom_call" | custom-call | flops 6442450944 | bytes 8388608 | tf_op jit(solution)/shard_map/remote_near/pallas_call | solution.py:340
  96.4 10.7 %far_field.1.base = f32[16,128,256]{2,1,0:T(8,128)} custom-call(s32[57]{0:T(128)} %pad_add_fusion.2.ids, f32[3,32,128]{2,1,0:T(8,128)} %pad.9.own_points, bf16[128,32,256]{2,1,0:T(8,128)(2,1)} %get-tuple-element.11.nodes, bf16[16,32,32]{2,1,0:T(8,128)(2,1)} %trans.3, f32[16,128,256]{2,1,0:T(8,128)} %remote_near.1.acc, bf16[16,32,256]{2,1,0:T(8,128)(2,1)} %basis.3), custom_call_target="tpu_custom_call" | custom-call | flops 6442450944 | bytes 4194304 | tf_op jit(solution)/shard_map/far_field/pallas_call | solution.py:414
  107.2 0.0 all-to-all-done.returned
  107.2 0.0 copy-start
  107.2 1.3 %copy-done = bf16[32,128,256]{2,1,0:T(8,128)(2,1)} copy-done((bf16[32,128,256]{2,1,0:T(8,128)(2,1)}, bf16[32,128,256]{2,1,0:T(8,128)(2,1)S(1)}, u32[]{:S(2)}) %copy-start) | copy-done | bytes 2097176
  108.5 5.5 %finish.1 = f32[16,256,128]{2,1,0:T(8,128)} custom-call(s32[32]{0:T(128)} %select_reduce_fusion.order, s32[17]{0:T(128)} %convert_reduce_fusion.1.starts, f32[16,128,256]{2,1,0:T(8,128)} %far_field.1.base, bf16[32,128,256]{2,1,0:T(8,128)(2,1)} %copy-done), custom_call_target="tpu_custom_call" | custom-call | tf_op jit(solution)/shard_map/finish/pallas_call | solution.py:446
  (12 shorter events, 0.1 us)
Async XLA Ops:
  68.9 5.3 %copy-start.1 = (bf16[1,3,32]{2,1,0:T(4,128)(2,1)S(1)}, bf16[1,3,32]{2,1,0:T(4,128)(2,1)}, u32[]{:S(2)}) copy-start(bf16[1,3,32]{2,1,0:T(4,128)(2,1)} %param.20) | copy-start | bytes 580
  68.9 6.1 %copy-start.3 = (s32[1,8]{1,0:T(1,128)S(1)}, s32[1,8]{1,0:T(1,128)}, u32[]{:S(2)}) copy-start(s32[1,8]{1,0:T(1,128)} %param.25) | copy-start | bytes 100
  68.9 8.3 %copy-start.2 = (s32[32,1]{0,1:T(1,128)S(1)}, s32[32,1]{0,1:T(1,128)}, u32[]{:S(2)}) copy-start(s32[32,1]{0,1:T(1,128)} %param.21) | copy-start | bytes 388
  68.9 38.3 %all-to-all-start = ((bf16[32,128,256]{2,1,0:T(8,128)(2,1)}), bf16[32,128,256]{2,1,0:T(8,128)(2,1)S(1)}, u32[]{:S(2)}, u32[]{:S(2)}) async-start(bf16[32,128,256]{2,1,0:T(8,128)(2,1)} %reply.1), calls=%async_computation | async-start | bytes 4194304 | tf_op jit(solution)/shard_map/all_to_all | solution.py:488
  107.2 1.3 %copy-start = (bf16[32,128,256]{2,1,0:T(8,128)(2,1)}, bf16[32,128,256]{2,1,0:T(8,128)(2,1)S(1)}, u32[]{:S(2)}) copy-start(bf16[32,128,256]{2,1,0:T(8,128)(2,1)S(1)} %all-to-all-done.returned) | copy-start | bytes 6291460

commit v7 on v6

--- a/solution.py
+++ b/solution.py
@@ -18,6 +18,8 @@
 ANY = pl.BlockSpec(memory_space=pl.ANY)
 MESH = pl.DeviceIdType.MESH
 TAIL = 512
+SPLIT = (0, 10)
+STEPS = tuple((i, j) for i in range(4) for j in range(4) if i or j)
 ROUTE = (
     (3, 2, 1), (0, 1, 1), (1, 2, 0), (2, 1, 0), (1, 2, 1), (3, 0, 0), (3, 3, 0), (0, 0, 1),
     (3, 1, 0), (3, 0, 1), (0, 2, 0), (1, 1, 1), (2, 2, 1), (3, 2, 0), (1, 3, 1), (1, 0, 0),
@@ -25,7 +27,6 @@
     (2, 0, 0), (0, 1, 0), (0, 2, 1), (2, 1, 1), (2, 3, 1), (0, 3, 1), (1, 1, 0),
 )
 MESH = pl.DeviceIdType.MESH
-PARAMS = pltpu.CompilerParams(vmem_limit_bytes=14 << 20)
 WIDE = pltpu.CompilerParams(vmem_limit_bytes=56 << 20)
 
 
@@ -111,40 +112,6 @@
     for k in (1, 2, 3):
         pl.semaphore_signal(barrier, inc=1, device_id={"group": turn(z, k), "dev": d}, device_id_type=MESH)
 
-    total = jnp.zeros((trans.shape[1], rhs), F32)
-    for i in range(clusters):
-        leaf = dot(basis[i], charges[i]).astype(BF16)
-        total += dot(trans[i], leaf)
-    top = total.astype(BF16)
-    mats = [mat[0].astype(F32) for mat in (pair, quad)]
-    moves = jnp.concatenate([mat[8 * i : 8 * i + 8] for mat in mats for i in range(4)], axis=1)
-    lane = lax.broadcasted_iota(jnp.int32, (1, width), 1)
-    points = [axes[i, clusters : clusters + 1] for i in range(3)]
-    info = points[0] + pltpu.roll(points[1], 32, 1) + pltpu.roll(points[2], 64, 1)
-    for i in range(16):
-        info = jnp.where(lane == rhs + i, ints[32 + i].astype(F32), info)
-    line = lax.broadcasted_iota(jnp.int32, (8, width), 0)
-    info = jnp.where(line == 0, jnp.broadcast_to(info, (8, width)), 0.0)
-    me = ((c * 4 + z) * 4 + y) * 4 + x
-    nodes[me, :16] = jnp.concatenate([top[:16], top[16:]], axis=1)
-    nodes[me, 16:] = jnp.concatenate([moves, info], axis=0).astype(BF16)
-
-    def node_copy(start, length, sem, peer):
-        held = nodes.at[pl.ds(start, length)]
-        return pltpu.make_async_remote_copy(
-            src_ref=held,
-            dst_ref=held,
-            send_sem=node_send.at[sem],
-            recv_sem=node_recv.at[sem],
-            device_id=peer,
-            device_id_type=MESH,
-        )
-
-    pl.semaphore_wait(barrier, 34)
-    along_x = [node_copy(me, 1, k, {"group": z, "dev": member(turn(x, k + 1), y, c)}) for k in range(3)]
-    for copy in along_x:
-        copy.start()
-
     point = [axes[i, :clusters] for i in range(3)]
     norm = point[0] * point[0] + point[1] * point[1] + point[2] * point[2]
     one = jnp.ones_like(norm)
@@ -158,19 +125,11 @@
         stage[i, :rhs] = charges[i].T
         stage[i, rhs:] = rows_b[i].astype(BF16)
 
-    for copy in along_x:
-        copy.wait_recv()
-    start = (c * 4 + z) * 16
-    along_y = [
-        node_copy(start + y * 4, 4, 3 + k, {"group": z, "dev": member(x, turn(y, k + 1), c)}) for k in range(3)
-    ]
-    for copy in along_y:
-        copy.start()
-
+    pl.semaphore_wait(barrier, 34)
     sent = []
 
     def send(i):
-        outgoing[i] = stage[ints[team[i]]]
+        outgoing[i] = stage[ints[2, team[i]]]
         copy = pltpu.make_async_remote_copy(
             src_ref=outgoing.at[i],
             dst_ref=incoming.at[d],
@@ -182,26 +141,65 @@
         copy.start()
         sent.append(copy)
 
-    for i in range(4):
+    for i in range(SPLIT[0]):
+        send(i)
+    total = jnp.zeros((trans.shape[1], rhs), F32)
+    for i in range(clusters):
+        leaf = dot(basis[i], charges[i]).astype(BF16)
+        total += dot(trans[i], leaf)
+    top = total.astype(BF16)
+    mats = [mat[0].astype(F32) for mat in (pair, quad)]
+    moves = jnp.concatenate([mat[8 * i : 8 * i + 8] for mat in mats for i in range(4)], axis=1)
+    lane = lax.broadcasted_iota(jnp.int32, (1, width), 1)
+    points = [axes[i, clusters : clusters + 1] for i in range(3)]
+    info = points[0] + pltpu.roll(points[1], 32, 1) + pltpu.roll(points[2], 64, 1)
+    for i in range(16):
+        info = jnp.where(lane == rhs + i, ints[2, 32 + i].astype(F32), info)
+    line = lax.broadcasted_iota(jnp.int32, (8, width), 0)
+    info = jnp.where(line == 0, jnp.broadcast_to(info, (8, width)), 0.0)
+    me = ((c * 4 + z) * 4 + y) * 4 + x
+    nodes[me, :16] = jnp.concatenate([top[:16], top[16:]], axis=1)
+    nodes[me, 16:] = jnp.concatenate([moves, info], axis=0).astype(BF16)
+
+    def node_copy(start, length, sem, peer):
+        held = nodes.at[pl.ds(start, length)]
+        return pltpu.make_async_remote_copy(
+            src_ref=held,
+            dst_ref=held,
+            send_sem=node_send.at[sem],
+            recv_sem=node_recv.at[sem],
+            device_id=peer,
+            device_id_type=MESH,
+        )
+
+    plane = [
+        node_copy(me, 1, i, {"group": z, "dev": member(turn(x, dx), turn(y, dy), c)})
+        for i, (dx, dy) in enumerate(STEPS)
+    ]
+    for copy in plane:
+        copy.start()
+
+    for i in range(SPLIT[0], SPLIT[1]):
         send(i)
     for i in range(clusters):
         fa[i] = rows_a[i].T.astype(BF16)
-    pair_lists(pairs[:1], pairs[1:2], ints[48], lists, weights)
-    for copy in along_y:
+    pair_lists(pairs[:1], pairs[1:2], ints[2, 48], lists, weights)
+    for copy in plane:
         copy.wait_recv()
+    start = (c * 4 + z) * 16
     along_z = []
-    for i in range(4, 31):
+    for i in range(SPLIT[1], 31):
         send(i)
-        if i % 2 == 0 and len(along_z) < 12:
+        while len(along_z) * (31 - SPLIT[1]) < 12 * (i + 1 - SPLIT[1]):
             part, k = divmod(len(along_z), 3)
             peer = {"group": turn(z, k + 1), "dev": d}
-            along_z.append(node_copy(start + part * 4, 4, 6 + len(along_z), peer))
+            along_z.append(node_copy(start + part * 4, 4, 15 + len(along_z), peer))
             along_z[-1].start()
-    outgoing[31] = stage[ints[d]]
+    outgoing[31] = stage[ints[2, d]]
     own = pltpu.make_async_copy(outgoing.at[31], incoming.at[d], own_sem)
     own.start()
     chip = {"group": z, "dev": member(x, y, 1 - c)}
-    across = [node_copy(start, 16, 18, chip)]
+    across = [node_copy(start, 16, 27, chip)]
     across[0].start()
 
     acc[...] = jnp.zeros_like(acc)
@@ -228,14 +226,14 @@
     for k in range(3):
         for part in range(4):
             along_z[part * 3 + k].wait_recv()
-        across.append(node_copy((c * 4 + turn(z, 3 - k)) * 16, 16, 19 + k, chip))
+        across.append(node_copy((c * 4 + turn(z, 3 - k)) * 16, 16, 28 + k, chip))
         across[-1].start()
     for copy in across:
         copy.wait_recv()
     for copy in sent:
         copy.wait_recv()
     own.wait()
-    for copy in (*along_x, *along_y, *along_z, *across, *sent):
+    for copy in (*plane, *along_z, *across, *sent):
         copy.wait_send()
 
 
@@ -261,8 +259,8 @@
             pltpu.VMEM((17, width, width), BF16),
             pltpu.SemaphoreType.DMA((31,)),
             pltpu.SemaphoreType.DMA((31,)),
-            pltpu.SemaphoreType.DMA((22,)),
-            pltpu.SemaphoreType.DMA((22,)),
+            pltpu.SemaphoreType.DMA((31,)),
+            pltpu.SemaphoreType.DMA((31,)),
             pltpu.SemaphoreType.DMA,
         ],
         compiler_params=pltpu.CompilerParams(
@@ -282,74 +280,141 @@
     return lax.rsqrt(s.astype(BF16)) * times.astype(BF16)
 
 
-def reply_kernel(pairs, stage, fa, incoming, back, kbuf):
-    rhs, width = back.shape[1:]
+def fetch(blocks, held, sems):
+    def copy(b):
+        return pltpu.make_async_copy(blocks.at[b], held.at[b], sems.at[b])
+
+    def begin(b, carry):
+        copy(b).start()
+        return carry
+
+    def end(b, carry):
+        copy(b).wait()
+        return carry
+
+    lax.fori_loop(0, held.shape[0], begin, 0)
+
+    def reach(done, b):
+        upto = jnp.maximum(done, b + 1)
+        lax.fori_loop(done, upto, end, 0)
+        return upto
+
+    return reach
+
+
+def reply_kernel(pairs, stage_in, fa_in, incoming_in, back_out, stage, fa, incoming, back, kbuf, sems, ins, outs):
+    peers, rhs, width = back.shape
+    first = [
+        pltpu.make_async_copy(fa_in, fa, sems.at[0]),
+        pltpu.make_async_copy(stage_in, stage, sems.at[1]),
+    ]
+    for copy in first:
+        copy.start()
+    reach = fetch(incoming_in, incoming, ins)
     back[...] = jnp.zeros_like(back)
+    for copy in first:
+        copy.wait()
+
+    def entry(j):
+        return unpack(pairs[1, 1 + j])[1]
+
+    def leave(b):
+        return pltpu.make_async_copy(back.at[b], back_out.at[b], outs.at[b])
+
+    def begin(b, carry):
+        leave(b).start()
+        return carry
+
+    def end(b, carry):
+        leave(b).wait()
+        return carry
+
+    done = reach(0, entry(GROUP - 1))
     for g in range(GROUP):
         kbuf[0, g] = tile(pairs[1, 1 + g], fa, incoming)
 
-    def body(i, total):
+    def body(i, carry):
+        total, done, sent = carry
         now = lax.rem(i, 2)
+        done = reach(done, entry(i * GROUP + 2 * GROUP - 1))
         for g in range(GROUP):
-            j = 1 + i * GROUP + g
-            a, b, _ = unpack(pairs[1, j])
-            before = unpack(pairs[1, jnp.maximum(j - 1, 1)])[1]
-            keep = jnp.where(before == b, 1.0, 0.0).astype(F32)
+            j = i * GROUP + g
+            a, b, _ = unpack(pairs[1, 1 + j])
+            keep = jnp.where(entry(jnp.maximum(j - 1, 0)) == b, 1.0, 0.0).astype(F32)
             total = total * keep + dot(stage[a, :rhs], kbuf[now, g])
             back[b] = total.astype(BF16)
-            kbuf[1 - now, g] = tile(pairs[1, j + GROUP], fa, incoming)
-        return total
-
-    lax.fori_loop(0, pl.cdiv(pairs[1, 0], GROUP), body, jnp.zeros((rhs, width), F32))
+            kbuf[1 - now, g] = tile(pairs[1, 1 + j + GROUP], fa, incoming)
+        last = entry(i * GROUP + GROUP - 1)
+        lax.fori_loop(sent, last, begin, 0)
+        return total, done, jnp.maximum(sent, last)
+
+    zero = jnp.zeros((rhs, width), F32)
+    _, done, sent = lax.fori_loop(0, pl.cdiv(pairs[1, 0], GROUP), body, (zero, done, 0))
+    lax.fori_loop(sent, peers, begin, 0)
+    reach(done, peers - 1)
+    lax.fori_loop(0, peers, end, 0)
 
 
 def reply(pairs, stage, fa, incoming):
     peers, rows, width = incoming.shape
+    out = jax.ShapeDtypeStruct((peers, rows - FEAT, width), BF16)
     return pl.pallas_call(
         reply_kernel,
-        out_shape=jax.ShapeDtypeStruct((peers, rows - FEAT, width), BF16),
-        in_specs=[SMEM] + [VMEM] * 3,
-        out_specs=VMEM,
-        scratch_shapes=[pltpu.VMEM((2, GROUP, width, width), BF16)],
+        out_shape=out,
+        in_specs=[SMEM] + [ANY] * 3,
+        out_specs=ANY,
+        scratch_shapes=[
+            pltpu.VMEM(stage.shape, BF16),
+            pltpu.VMEM(fa.shape, BF16),
+            pltpu.VMEM(incoming.shape, BF16),
+            pltpu.VMEM(out.shape, BF16),
+            pltpu.VMEM((2, GROUP, width, width), BF16),
+            pltpu.SemaphoreType.DMA((2,)),
+            pltpu.SemaphoreType.DMA((peers,)),
+            pltpu.SemaphoreType.DMA((peers,)),
+        ],
         compiler_params=WIDE,
         cost_estimate=pl.CostEstimate(flops=6 << 30, bytes_accessed=8 << 20, transcendentals=0),
         name="reply",
     )(pairs, stage, fa, incoming)
 
 
-def remote_kernel(pairs, fa, incoming, acc_in, acc, kbuf):
+def rest_kernel(
+    pairs, ids, own_points, trans, basis, fa_in, incoming_in, nodes_in, acc_in, base_out,
+    fa, incoming, nodes, acc, kbuf, sems, ins, outs,
+):
+    loads = [
+        pltpu.make_async_copy(src, dst, sems.at[i])
+        for i, (src, dst) in enumerate(((fa_in, fa), (acc_in, acc), (nodes_in, nodes)))
+    ]
+    loads[0].start()
+    reach = fetch(incoming_in, incoming, ins)
+    loads[1].start()
+    loads[2].start()
+    loads[0].wait()
     rhs = acc.shape[1]
-    acc[...] = acc_in[...]
+
+    def entry(j):
+        return unpack(pairs[1, 1 + j])[1]
+
+    done = reach(0, entry(GROUP - 1))
     for g in range(GROUP):
         kbuf[0, g] = tile(pairs[1, 1 + g], fa, incoming)
-
-    def body(i, carry):
+    loads[1].wait()
+
+    def body(i, done):
         now = lax.rem(i, 2)
+        done = reach(done, entry(i * GROUP + 2 * GROUP - 1))
         for g in range(GROUP):
             j = 1 + i * GROUP + g
             a, b, _ = unpack(pairs[1, j])
             acc[a] += dot(incoming[b, :rhs], kbuf[now, g], ((1,), (1,)))
             kbuf[1 - now, g] = tile(pairs[1, j + GROUP], fa, incoming)
-        return carry
-
-    lax.fori_loop(0, pl.cdiv(pairs[1, 0], GROUP), body, 0)
-
-
-def remote_near(pairs, fa, incoming, acc):
-    width = acc.shape[2]
-    return pl.pallas_call(
-        remote_kernel,
-        out_shape=jax.ShapeDtypeStruct(acc.shape, F32),
-        in_specs=[SMEM] + [VMEM] * 3,
-        out_specs=VMEM,
-        scratch_shapes=[pltpu.VMEM((2, GROUP, width, width), BF16)],
-        compiler_params=WIDE,
-        cost_estimate=pl.CostEstimate(flops=6 << 30, bytes_accessed=8 << 20, transcendentals=0),
-        name="remote_near",
-    )(pairs, fa, incoming, acc)
-
-
-def far_kernel(ids, own_points, nodes, trans, acc, basis, base):
+        return done
+
+    done = lax.fori_loop(0, pl.cdiv(pairs[1, 0], GROUP), body, done)
+    reach(done, incoming.shape[0] - 1)
+    loads[2].wait()
     rank = 32
 
     def skel(n):
@@ -405,56 +470,83 @@
 
     down = far_one + down_by(0, far_two) + down_by(1, far_three)
     high, low = halves(down.T)
+
+    def leave(c):
+        return pltpu.make_async_copy(acc.at[c], base_out.at[c], outs.at[c])
+
     for c in range(trans.shape[0]):
         leaf = (dot(high, trans[c]) + dot(low, trans[c])).astype(BF16)
-        base[c] = acc[c] * KCOEF + dot(leaf, basis[c])
-
-
-def far_field(ids, own_points, nodes, trans, acc, basis):
+        acc[c] = acc[c] * KCOEF + dot(leaf, basis[c])
+        leave(c).start()
+    for c in range(trans.shape[0]):
+        leave(c).wait()
+
+
+def rest(pairs, ids, own_points, trans, basis, fa, incoming, nodes, acc):
+    width = acc.shape[2]
     return pl.pallas_call(
-        far_kernel,
+        rest_kernel,
         out_shape=jax.ShapeDtypeStruct(acc.shape, F32),
-        in_specs=[SMEM] + [VMEM] * 5,
-        out_specs=VMEM,
+        in_specs=[SMEM] * 2 + [VMEM] * 3 + [ANY] * 4,
+        out_specs=ANY,
+        scratch_shapes=[
+            pltpu.VMEM(fa.shape, BF16),
+            pltpu.VMEM(incoming.shape, BF16),
+            pltpu.VMEM(nodes.shape, BF16),
+            pltpu.VMEM(acc.shape, F32),
+            pltpu.VMEM((2, GROUP, width, width), BF16),
+            pltpu.SemaphoreType.DMA((3,)),
+            pltpu.SemaphoreType.DMA(incoming.shape[:1]),
+            pltpu.SemaphoreType.DMA(acc.shape[:1]),
+        ],
         compiler_params=WIDE,
-        cost_estimate=pl.CostEstimate(flops=6 << 30, bytes_accessed=4 << 20, transcendentals=0),
-        name="far_field",
-    )(ids, own_points, nodes, trans, acc, basis)
-
-
-def final_kernel(order, starts, base, returned, out, rows, sems):
+        cost_estimate=pl.CostEstimate(flops=12 << 30, bytes_accessed=8 << 20, transcendentals=0),
+        name="rest",
+    )(pairs, ids, own_points, trans, basis, fa, incoming, nodes, acc)
+
+
+def final_kernel(ints, base, returned, out, sums, held, rows, base_sem, ins, outs):
     clusters = base.shape[0]
-
-    def copy(c):
-        return pltpu.make_async_copy(rows.at[c], out.at[c], sems.at[c])
+    load = pltpu.make_async_copy(base, sums, base_sem)
+    load.start()
+    reach = fetch(returned, held, ins)
+    load.wait()
+
+    def collect(h, done):
+        done = reach(done, h)
+        sums[ints[2, h]] += KCOEF * held[h].astype(F32)
+        return done
+
+    lax.fori_loop(0, held.shape[0], collect, 0)
+
+    def leave(c):
+        return pltpu.make_async_copy(rows.at[c], out.at[c], outs.at[c])
 
     for c in range(clusters):
-
-        def collect(i, total):
-            return total + returned[order[i]].astype(F32)
-
-        zero = jnp.zeros(base.shape[1:], F32)
-        total = lax.fori_loop(starts[c], starts[c + 1], collect, zero)
-        rows[c] = (base[c] + KCOEF * total).T
-        copy(c).start()
+        rows[c] = sums[c].T
+        leave(c).start()
     for c in range(clusters):
-        copy(c).wait()
-
-
-def finish(order, starts, base, returned):
-    clusters, conductors, width = base.shape
+        leave(c).wait()
+
+
+def finish(ints, base, returned):
+    clusters, rhs, width = base.shape
     return pl.pallas_call(
         final_kernel,
-        out_shape=jax.ShapeDtypeStruct((clusters, width, conductors), F32),
-        in_specs=[SMEM] * 2 + [VMEM] * 2,
-        out_specs=pl.BlockSpec(memory_space=pl.ANY),
+        out_shape=jax.ShapeDtypeStruct((clusters, width, rhs), F32),
+        in_specs=[SMEM] + [ANY] * 2,
+        out_specs=ANY,
         scratch_shapes=[
-            pltpu.VMEM((clusters, width, conductors), F32),
+            pltpu.VMEM(base.shape, F32),
+            pltpu.VMEM(returned.shape, BF16),
+            pltpu.VMEM((clusters, width, rhs), F32),
+            pltpu.SemaphoreType.DMA,
+            pltpu.SemaphoreType.DMA(returned.shape[:1]),
             pltpu.SemaphoreType.DMA((clusters,)),
         ],
         compiler_params=WIDE,
         name="finish",
-    )(order, starts, base, returned)
+    )(ints, base, returned)
 
 
 def shards(
@@ -480,13 +572,12 @@
     points = jnp.pad(skel_points[0][:, None, :], ((0, 0), (0, 0), (0, width - skel_points.shape[2])))
     axes = jnp.concatenate([jnp.swapaxes(panel_coords, 0, 1), points], axis=1).astype(F32)
     ints = jnp.concatenate([send_slots[:, 0], far_two[0], far_three[0], pair_count])
-    pairs = jnp.stack([pair_first, pair_second])
+    ints = jnp.stack([pair_first, pair_second, jnp.pad(ints, (0, 256 - ints.shape[0]))])
     stage, fa, incoming, nodes, lists, acc = exchange(
-        ints, pairs, blocks, axes, cluster_basis, trans_leaf, trans_pair, trans_quad
+        ints, ints, blocks, axes, cluster_basis, trans_leaf, trans_pair, trans_quad
     )
     back = reply(lists, stage, fa, incoming)
     returned = lax.all_to_all(back, "dev", split_axis=0, concat_axis=0, tiled=True)
-    acc = remote_near(lists, fa, incoming, acc)
 
     z, d = lax.axis_index("group"), lax.axis_index("dev")
     x, y = d // 8, d // 2 % 4
@@ -520,20 +611,8 @@
     )
     own_points = jnp.repeat(jnp.swapaxes(own_points, 1, 2), 32, axis=2)
     own_points = jnp.pad(own_points, ((0, 0), (0, 0), (0, 32)))
-    base = far_field(ids, own_points, nodes, trans_leaf, acc, cluster_basis)
-
-    slots = send_slots[:, 0]
-    spots = jnp.arange(peers, dtype=jnp.int32)
-    rank = jnp.sum(
-        (slots[None, :] < slots[:, None])
-        | ((slots[None, :] == slots[:, None]) & (spots[None, :] < spots[:, None])),
-        axis=1,
-        dtype=jnp.int32,
-    )
-    order = jnp.sum(jnp.where(rank[None, :] == spots[:, None], spots[None, :], 0), axis=1)
-    edges = jnp.arange(clusters + 1, dtype=jnp.int32)
-    starts = jnp.sum(slots[None, :] < edges[:, None], axis=1, dtype=jnp.int32)
-    out = finish(order, starts, base, returned)
+    base = rest(lists, ids, own_points, trans_leaf, cluster_basis, fa, incoming, nodes, acc)
+    out = finish(ints, base, returned)
     return out.reshape(clusters * width, conductors)
 
 

time: 114 us -> 106 us (0.930)
  the two profiles are of different devices: /device:TPU:43 before, /device:TPU:1 now
where the time goes in v7:
time: 106 us; the launch traced here: 105 us
  Pallas kernels  78.1 us (74%)
  starting transfers between devices  11.2 us (11%)
  waiting for transfers between devices  6.4 us (6%)
  other arithmetic  4.31 us (4%)
  local copies, waits for them, and re-layouts  4.07 us (4%)
    pallas_call x1, Pallas kernels, exchange(): pl.pallas_call(exchange_kernel, out_shape=(jax.ShapeDtypeStruct((clusters...  44.4 us
    pallas_call x1, Pallas kernels, rest(): pl.pallas_call(rest_kernel, out_shape=jax.ShapeDtypeStruct(acc.shape, F32...  18.7 us
    all_to_all x1, starting transfers between devices, shards(): lax.all_to_all(back, 'dev', split_axis=0, concat_axis=0, tiled=True)  11.2 us
    pallas_call x1, Pallas kernels, reply(): pl.pallas_call(reply_kernel, out_shape=out, in_specs=[SMEM] + [ANY] * 3,...  9.86 us
    all_to_all x1, waiting for transfers between devices, shards(): lax.all_to_all(back, 'dev', split_axis=0, concat_axis=0, tiled=True)  6.4 us
    pallas_call x1, Pallas kernels, finish(): pl.pallas_call(final_kernel, out_shape=jax.ShapeDtypeStruct((clusters, wi...  5.04 us
  transfers between devices with their start and end apart: 1, of which 1 were waited for; matrix products, arithmetic and copies ran while one was open for 3% of the time, Pallas kernels for 18%

profile of v7, /device:TPU:1, one launch (start us, length us, event | category | flops | bytes accessed | tf_op | source)
XLA Modules:
  0.0 105.0 jit_solution(2061086573536691601)
XLA Ops:
  0.7 0.7 copy.20
  1.3 0.8 pad_add_fusion.1
  2.1 1.4 %fusion.2.axes = f32[3,17,256]{2,1,0:T(8,128)} fusion(bf16[3,1,32]{2,1,0:T(2,128)(2,1)S(1)} %copy.20, bf16[3,16,256]{2,1,0:T(8,128)(2,1)} %bitcast.34), kind=kLoop, calls=%fused_computation.3 | loop fusion | flops 78336 | bytes 76992 | tf_op jit(solution)/shard_map/convert_element_type | solution.py:573
  3.5 1.3 %pad_add_fusion.ints.pairs = s32[3,256]{1,0:T(4,128)} fusion(s32[1,256]{1,0:T(1,128)S(1)} %bitcast.37, s32[1,256]{1,0:T(1,128)} %bitcast.38, s32[1,256]{1,0:T(1,128)} %bitcast.39), kind=kLoop, calls=%fused_computation.5 | loop fusion | flops 1536 | bytes 6144 | tf_op jit(solution)/shard_map/stack | solution.py:575
  4.8 44.4 %exchange.1 = (bf16[16,144,256]{2,1,0:T(8,128)(2,1)}, bf16[16,256,16]{2,1,0:T(8,128)(2,1)}, bf16[32,144,256]{2,1,0:T(8,128)(2,1)}, bf16[128,32,256]{2,1,0:T(8,12...) custom-call(s32[3,256]{1,0:T(4,128)} %pad_add_fusion.ints.pairs, s32[3,256]{1,0:T(4,128)} %pad_add_fusion.ints.pairs, ...), custom_call_target="tpu_custom_call" | custom-call | tf_op jit(solution)/shard_map/exchange/pallas_call | solution.py:243
  49.2 9.9 %reply.1 = bf16[32,128,256]{2,1,0:T(8,128)(2,1)} custom-call(s32[2,512]{1,0:T(2,128)} %get-tuple-element.11.pairs, bf16[16,144,256]{2,1,0:T(8,128)(2,1)} %get-tuple-element.16.stage_in, bf16[16,256,16]{2,1,0:T(8,128)(2,1)} %get-tuple-element.13.fa_in, bf16[32,144,256]{2,1,0:T(8,128)(2,1)} %get-tuple-element.14.incoming_in), custom_call_target="tpu_custom_call" | custom-call | flops 6442450944 | bytes 8388608 | tf_op jit(solution)/shard_map/reply/pallas_call | solution.py:361
  59.1 0.0 copy-start.1
  59.1 0.0 copy-start.2
  59.1 11.2 %all-to-all-start = ((bf16[32,128,256]{2,1,0:T(8,128)(2,1)}), bf16[32,128,256]{2,1,0:T(8,128)(2,1)S(1)}, u32[]{:S(2)}, u32[]{:S(2)}) async-start(bf16[32,128,256]{2,1,0:T(8,128)(2,1)} %reply.1), calls=%async_computation | async-start | bytes 4194304 | tf_op jit(solution)/shard_map/all_to_all | solution.py:580
  70.4 0.0 copy-done.1
  70.4 0.7 constant_dynamic-slice_fusion.1
  71.2 0.1 fusion.16
  71.3 0.1 reshape.43
  71.5 0.1 mul.76
  71.6 0.1 mul.81
  71.7 0.1 copy.23
  71.8 0.2 broadcast_in_dim.3
  71.9 0.1 reshape.40
  72.1 0.6 pad.14.own_points
  72.7 0.0 copy-done.2
  72.8 0.7 pad_add_fusion.2.ids
  73.4 18.7 %rest.1.base = f32[16,128,256]{2,1,0:T(8,128)} custom-call(s32[2,512]{1,0:T(2,128)} %get-tuple-element.11.pairs, s32[57]{0:T(128)} %pad_add_fusion.2.ids, f32[3,32,128]{2,1,0:T(8,128)} %pad.14.own_points, bf16[16,32,32]{2,1,0:T(8,128)(2,1)} %trans.3, bf16[16,32,256]{2,1,0:T(8,128)(2,1)} %basis.3, bf16[16,256,16]{2,1,0:T(8,128)(2,1)} %get-tuple-element.13.fa_in, ...), custom_call_target="tpu_custom_call" | custom-call | flops 12884901888 | bytes 8388608 | tf_op jit(solution)/shard_map/rest/pallas_call | solution.py:487
  92.2 6.4 %all-to-all-done.returned = bf16[32,128,256]{2,1,0:T(8,128)(2,1)S(1)} async-done(((bf16[32,128,256]{2,1,0:T(8,128)(2,1)}), bf16[32,128,256]{2,1,0:T(8,128)(2,1)S(1)}, u32[]{:S(2)}, u32[]{:S(2)}) %all-to-all-start) | async-done | bytes 2097184 | tf_op jit(solution)/shard_map/all_to_all | solution.py:580
  98.6 0.0 copy-start
  98.6 1.3 %copy-done = bf16[32,128,256]{2,1,0:T(8,128)(2,1)} copy-done((bf16[32,128,256]{2,1,0:T(8,128)(2,1)}, bf16[32,128,256]{2,1,0:T(8,128)(2,1)S(1)}, u32[]{:S(2)}) %copy-start) | copy-done | bytes 2097176
  99.9 5.0 %finish.1 = f32[16,256,128]{2,1,0:T(8,128)} custom-call(s32[3,256]{1,0:T(4,128)} %pad_add_fusion.ints.pairs, f32[16,128,256]{2,1,0:T(8,128)} %rest.1.base, bf16[32,128,256]{2,1,0:T(8,128)(2,1)} %copy-done), custom_call_target="tpu_custom_call" | custom-call | tf_op jit(solution)/shard_map/finish/pallas_call | solution.py:534
  (13 shorter events, 0.2 us)
Async XLA Ops:
  59.1 11.3 %copy-start.1 = (bf16[1,3,32]{2,1,0:T(4,128)(2,1)S(1)}, bf16[1,3,32]{2,1,0:T(4,128)(2,1)}, u32[]{:S(2)}) copy-start(bf16[1,3,32]{2,1,0:T(4,128)(2,1)} %param.20) | copy-start | bytes 580
  59.1 13.6 %copy-start.2 = (s32[1,8]{1,0:T(1,128)S(1)}, s32[1,8]{1,0:T(1,128)}, u32[]{:S(2)}) copy-start(s32[1,8]{1,0:T(1,128)} %param.25) | copy-start | bytes 100
  59.1 39.5 %all-to-all-start = ((bf16[32,128,256]{2,1,0:T(8,128)(2,1)}), bf16[32,128,256]{2,1,0:T(8,128)(2,1)S(1)}, u32[]{:S(2)}, u32[]{:S(2)}) async-start(bf16[32,128,256]{2,1,0:T(8,128)(2,1)} %reply.1), calls=%async_computation | async-start | bytes 4194304 | tf_op jit(solution)/shard_map/all_to_all | solution.py:580
  98.6 1.3 %copy-start = (bf16[32,128,256]{2,1,0:T(8,128)(2,1)}, bf16[32,128,256]{2,1,0:T(8,128)(2,1)S(1)}, u32[]{:S(2)}) copy-start(bf16[32,128,256]{2,1,0:T(8,128)(2,1)S(1)} %all-to-all-done.returned) | copy-start | bytes 6291460

commit v8 on v7

--- a/solution.py
+++ b/solution.py
@@ -27,6 +27,7 @@
     (2, 0, 0), (0, 1, 0), (0, 2, 1), (2, 1, 1), (2, 3, 1), (0, 3, 1), (1, 1, 0),
 )
 MESH = pl.DeviceIdType.MESH
+NARROW = pltpu.CompilerParams(vmem_limit_bytes=12 << 20)
 WIDE = pltpu.CompilerParams(vmem_limit_bytes=56 << 20)
 
 
@@ -83,6 +84,23 @@
         mine = jnp.where(slot[:1] > total, last, mine)
         lists[i : i + 1] = jnp.where(slot[:1] == 0, total, mine).astype(jnp.int32)
     turned = dot(hot(16, a), hot(48, b), ((1,), (1,)))
+    times = turned[:, 16:]
+    row = lax.broadcasted_iota(jnp.int32, times.shape, 0)
+    col = lax.broadcasted_iota(jnp.int32, times.shape, 1)
+    held = jnp.where(times > 0, 1.0, 0.0)
+    side_r = lax.broadcasted_iota(jnp.int32, (32, 32), 0)
+    side_c = lax.broadcasted_iota(jnp.int32, (32, 32), 1)
+    within = dot(held.astype(BF16), jnp.where(side_r < side_c, 1.0, 0.0).astype(BF16))
+    above = dot(jnp.where(up_c < up_r, 1.0, 0.0).astype(BF16), held.astype(BF16))
+    rank = jnp.where(held > 0, jnp.sum(above, axis=1, keepdims=True) + within + 1.0, -1.0)
+    value = (col * 16 + row).astype(F32) + 2048.0 * times
+    code = jnp.zeros((16, TAIL), F32)
+    for i in range(32):
+        code += jnp.where(rank[:, i : i + 1] == slot[:16], value[:, i : i + 1], 0.0)
+    total = jnp.sum(jnp.sum(held, axis=1, keepdims=True), axis=0, keepdims=True)
+    last = jnp.max(jnp.max(held * row.astype(F32), axis=1, keepdims=True), axis=0, keepdims=True)
+    mine = jnp.where(slot[:1] > total, last, jnp.sum(code, axis=0, keepdims=True))
+    lists[2:3] = jnp.where(slot[:1] == 0, total, mine).astype(jnp.int32)
     line = lax.broadcasted_iota(jnp.int32, (16, 128), 0)
     for i in range(16):
         part = jnp.broadcast_to(turned[:, i : i + 1], (16, 128))
@@ -90,7 +108,7 @@
 
 
 def exchange_kernel(
-    ints, pairs, charges, axes, basis, trans, pair, quad,
+    ints, first, second, charges, axes, basis, trans, pair, quad,
     stage, fa, incoming, nodes, lists, acc,
     rows_a, rows_b, outgoing, weights, kbuf, team_send, team_recv, node_send, node_recv, own_sem,
 ):
@@ -129,7 +147,7 @@
     sent = []
 
     def send(i):
-        outgoing[i] = stage[ints[2, team[i]]]
+        outgoing[i] = stage[ints[team[i]]]
         copy = pltpu.make_async_remote_copy(
             src_ref=outgoing.at[i],
             dst_ref=incoming.at[d],
@@ -154,7 +172,7 @@
     points = [axes[i, clusters : clusters + 1] for i in range(3)]
     info = points[0] + pltpu.roll(points[1], 32, 1) + pltpu.roll(points[2], 64, 1)
     for i in range(16):
-        info = jnp.where(lane == rhs + i, ints[2, 32 + i].astype(F32), info)
+        info = jnp.where(lane == rhs + i, ints[32 + i].astype(F32), info)
     line = lax.broadcasted_iota(jnp.int32, (8, width), 0)
     info = jnp.where(line == 0, jnp.broadcast_to(info, (8, width)), 0.0)
     me = ((c * 4 + z) * 4 + y) * 4 + x
@@ -183,7 +201,7 @@
         send(i)
     for i in range(clusters):
         fa[i] = rows_a[i].T.astype(BF16)
-    pair_lists(pairs[:1], pairs[1:2], ints[2, 48], lists, weights)
+    pair_lists(*(jnp.concatenate([p[:1], p[1:]], axis=1) for p in (first, second)), ints[48], lists, weights)
     for copy in plane:
         copy.wait_recv()
     start = (c * 4 + z) * 16
@@ -195,7 +213,7 @@
             peer = {"group": turn(z, k + 1), "dev": d}
             along_z.append(node_copy(start + part * 4, 4, 15 + len(along_z), peer))
             along_z[-1].start()
-    outgoing[31] = stage[ints[2, d]]
+    outgoing[31] = stage[ints[d]]
     own = pltpu.make_async_copy(outgoing.at[31], incoming.at[d], own_sem)
     own.start()
     chip = {"group": z, "dev": member(x, y, 1 - c)}
@@ -237,7 +255,7 @@
         copy.wait_send()
 
 
-def exchange(ints, pairs, charges, axes, basis, trans, pair, quad):
+def exchange(ints, first, second, charges, axes, basis, trans, pair, quad):
     clusters, width, rhs = charges.shape
     rows = rhs + FEAT
     return pl.pallas_call(
@@ -247,10 +265,10 @@
             jax.ShapeDtypeStruct((clusters, width, FEAT), BF16),
             jax.ShapeDtypeStruct((32, rows, width), BF16),
             jax.ShapeDtypeStruct((128, 32, width), BF16),
-            jax.ShapeDtypeStruct((2, TAIL), jnp.int32),
+            jax.ShapeDtypeStruct((3, TAIL), jnp.int32),
             jax.ShapeDtypeStruct((clusters, rhs, width), F32),
         ),
-        in_specs=[SMEM] + [VMEM] * 7,
+        in_specs=[SMEM] + [VMEM] * 8,
         out_specs=(VMEM, VMEM, ANY, VMEM, VMEM, VMEM),
         scratch_shapes=[pltpu.VMEM((clusters, FEAT, width), F32)] * 2
         + [
@@ -267,7 +285,7 @@
             vmem_limit_bytes=56 << 20, collective_id=0, has_side_effects=True
         ),
         name="exchange",
-    )(ints, pairs, charges, axes, basis, trans, pair, quad)
+    )(ints, first, second, charges, axes, basis, trans, pair, quad)
 
 
 def unpack(code):
@@ -381,40 +399,38 @@
 
 def rest_kernel(
     pairs, ids, own_points, trans, basis, fa_in, incoming_in, nodes_in, acc_in, base_out,
-    fa, incoming, nodes, acc, kbuf, sems, ins, outs,
+    fa, incoming, nodes, own, acc, kbuf, sems, outs,
 ):
     loads = [
         pltpu.make_async_copy(src, dst, sems.at[i])
-        for i, (src, dst) in enumerate(((fa_in, fa), (acc_in, acc), (nodes_in, nodes)))
+        for i, (src, dst) in enumerate(
+            ((fa_in, fa), (incoming_in, incoming), (acc_in, own), (acc_in, acc), (nodes_in, nodes))
+        )
     ]
-    loads[0].start()
-    reach = fetch(incoming_in, incoming, ins)
-    loads[1].start()
-    loads[2].start()
+    for load in loads:
+        load.start()
     loads[0].wait()
-    rhs = acc.shape[1]
-
-    def entry(j):
-        return unpack(pairs[1, 1 + j])[1]
-
-    done = reach(0, entry(GROUP - 1))
+    loads[1].wait()
+    rhs, width = acc.shape[1:]
     for g in range(GROUP):
-        kbuf[0, g] = tile(pairs[1, 1 + g], fa, incoming)
-    loads[1].wait()
-
-    def body(i, done):
+        kbuf[0, g] = tile(pairs[2, 1 + g], fa, incoming)
+    loads[2].wait()
+    loads[3].wait()
+
+    def body(i, total):
         now = lax.rem(i, 2)
-        done = reach(done, entry(i * GROUP + 2 * GROUP - 1))
         for g in range(GROUP):
             j = 1 + i * GROUP + g
-            a, b, _ = unpack(pairs[1, j])
-            acc[a] += dot(incoming[b, :rhs], kbuf[now, g], ((1,), (1,)))
-            kbuf[1 - now, g] = tile(pairs[1, j + GROUP], fa, incoming)
-        return done
-
-    done = lax.fori_loop(0, pl.cdiv(pairs[1, 0], GROUP), body, done)
-    reach(done, incoming.shape[0] - 1)
-    loads[2].wait()
+            a, b, _ = unpack(pairs[2, j])
+            before = unpack(pairs[2, jnp.maximum(j - 1, 1)])[0]
+            keep = jnp.where(before == a, 1.0, 0.0).astype(F32)
+            total = total * keep + dot(incoming[b, :rhs], kbuf[now, g], ((1,), (1,)))
+            acc[a] = own[a] + total
+            kbuf[1 - now, g] = tile(pairs[2, j + GROUP], fa, incoming)
+        return total
+
+    lax.fori_loop(0, pl.cdiv(pairs[2, 0], GROUP), body, jnp.zeros((rhs, width), F32))
+    loads[4].wait()
     rank = 32
 
     def skel(n):
@@ -459,8 +475,8 @@
         return total + apply(kernel_tile(mine[2], 0.5 * (left + right)), source.astype(BF16))
 
     far_one = lax.fori_loop(0, 8, one, zero, unroll=True)
-    far_two = lax.fori_loop(0, 16, two, zero, unroll=4)
-    far_three = lax.fori_loop(0, 32, three, zero, unroll=4)
+    far_two = lax.fori_loop(0, 16, two, zero, unroll=8)
+    far_three = lax.fori_loop(0, 32, three, zero, unroll=8)
     me = ids[56]
 
     def down_by(which, value):
@@ -494,9 +510,9 @@
             pltpu.VMEM(incoming.shape, BF16),
             pltpu.VMEM(nodes.shape, BF16),
             pltpu.VMEM(acc.shape, F32),
+            pltpu.VMEM(acc.shape, F32),
             pltpu.VMEM((2, GROUP, width, width), BF16),
-            pltpu.SemaphoreType.DMA((3,)),
-            pltpu.SemaphoreType.DMA(incoming.shape[:1]),
+            pltpu.SemaphoreType.DMA((5,)),
             pltpu.SemaphoreType.DMA(acc.shape[:1]),
         ],
         compiler_params=WIDE,
@@ -505,19 +521,17 @@
     )(pairs, ids, own_points, trans, basis, fa, incoming, nodes, acc)
 
 
-def final_kernel(ints, base, returned, out, sums, held, rows, base_sem, ins, outs):
+def final_kernel(ints, base, returned, out, sums, rows, base_sem, outs):
     clusters = base.shape[0]
     load = pltpu.make_async_copy(base, sums, base_sem)
     load.start()
-    reach = fetch(returned, held, ins)
     load.wait()
 
-    def collect(h, done):
-        done = reach(done, h)
-        sums[ints[2, h]] += KCOEF * held[h].astype(F32)
-        return done
-
-    lax.fori_loop(0, held.shape[0], collect, 0)
+    def collect(h, carry):
+        sums[ints[h]] += KCOEF * returned[h].astype(F32)
+        return carry
+
+    lax.fori_loop(0, returned.shape[0], collect, 0)
 
     def leave(c):
         return pltpu.make_async_copy(rows.at[c], out.at[c], outs.at[c])
@@ -534,17 +548,15 @@
     return pl.pallas_call(
         final_kernel,
         out_shape=jax.ShapeDtypeStruct((clusters, width, rhs), F32),
-        in_specs=[SMEM] + [ANY] * 2,
+        in_specs=[SMEM, ANY, VMEM],
         out_specs=ANY,
         scratch_shapes=[
             pltpu.VMEM(base.shape, F32),
-            pltpu.VMEM(returned.shape, BF16),
             pltpu.VMEM((clusters, width, rhs), F32),
             pltpu.SemaphoreType.DMA,
-            pltpu.SemaphoreType.DMA(returned.shape[:1]),
             pltpu.SemaphoreType.DMA((clusters,)),
         ],
-        compiler_params=WIDE,
+        compiler_params=NARROW,
         name="finish",
     )(ints, base, returned)
 
@@ -572,9 +584,9 @@
     points = jnp.pad(skel_points[0][:, None, :], ((0, 0), (0, 0), (0, width - skel_points.shape[2])))
     axes = jnp.concatenate([jnp.swapaxes(panel_coords, 0, 1), points], axis=1).astype(F32)
     ints = jnp.concatenate([send_slots[:, 0], far_two[0], far_three[0], pair_count])
-    ints = jnp.stack([pair_first, pair_second, jnp.pad(ints, (0, 256 - ints.shape[0]))])
     stage, fa, incoming, nodes, lists, acc = exchange(
-        ints, ints, blocks, axes, cluster_basis, trans_leaf, trans_pair, trans_quad
+        ints, pair_first.reshape(2, 128), pair_second.reshape(2, 128), blocks, axes,
+        cluster_basis, trans_leaf, trans_pair, trans_quad,
     )
     back = reply(lists, stage, fa, incoming)
     returned = lax.all_to_all(back, "dev", split_axis=0, concat_axis=0, tiled=True)

time: 106 us -> 103 us (0.972)
  starting transfers between devices: 11.2 us -> 8.99 us
  Pallas kernels: 78.1 us -> 77 us
    pallas_call x1, Pallas kernels: 5.04 us -> 2.82 us  [finish(): pl.pallas_call(final_kernel, out_shape=jax.ShapeDtypeStruct((clusters, wi...]
    all_to_all x1, starting transfers between devices: 11.2 us -> 8.99 us  [shards(): lax.all_to_all(back, 'dev', split_axis=0, concat_axis=0, tiled=True)]
    another operation x1 -> x0, other arithmetic: 1.29 us -> none  [shards(): jnp.stack([pair_first, pair_second, jnp.pad(ints, (0, 256 - ints.shape[0]...]
    pallas_call x1, Pallas kernels: 9.86 us -> 11.1 us  [reply(): pl.pallas_call(reply_kernel, out_shape=out, in_specs=[SMEM] + [ANY] * 3,...]
where the time goes in v8:
time: 103 us; the launch traced here: 101 us
  Pallas kernels  77 us (75%)
  starting transfers between devices  8.99 us (9%)
  waiting for transfers between devices  6.58 us (6%)
  local copies, waits for them, and re-layouts  4.3 us (4%)
  other arithmetic  3.58 us (3%)
    pallas_call x1, Pallas kernels, exchange(): pl.pallas_call(exchange_kernel, out_shape=(jax.ShapeDtypeStruct((clusters...  44.4 us
    pallas_call x1, Pallas kernels, rest(): pl.pallas_call(rest_kernel, out_shape=jax.ShapeDtypeStruct(acc.shape, F32...  18.6 us
    pallas_call x1, Pallas kernels, reply(): pl.pallas_call(reply_kernel, out_shape=out, in_specs=[SMEM] + [ANY] * 3,...  11.1 us
    all_to_all x1, starting transfers between devices, shards(): lax.all_to_all(back, 'dev', split_axis=0, concat_axis=0, tiled=True)  8.99 us
    all_to_all x1, waiting for transfers between devices, shards(): lax.all_to_all(back, 'dev', split_axis=0, concat_axis=0, tiled=True)  6.58 us
    pallas_call x1, Pallas kernels, finish(): pl.pallas_call(final_kernel, out_shape=jax.ShapeDtypeStruct((clusters, wi...  2.82 us
  transfers between devices with their start and end apart: 1, of which 1 were waited for; matrix products, arithmetic and copies ran while one was open for 3% of the time, Pallas kernels for 18%

profile of v8, /device:TPU:1, one launch (start us, length us, event | category | flops | bytes accessed | tf_op | source)
XLA Modules:
  0.0 101.4 jit_solution(2526082858390102468)
XLA Ops:
  0.7 0.7 copy.20
  1.3 1.4 %fusion.2.axes = f32[3,17,256]{2,1,0:T(8,128)} fusion(bf16[3,1,32]{2,1,0:T(2,128)(2,1)S(1)} %copy.20, bf16[3,16,256]{2,1,0:T(8,128)(2,1)} %bitcast.33), kind=kLoop, calls=%fused_computation.3 | loop fusion | flops 78336 | bytes 76992 | tf_op jit(solution)/shard_map/convert_element_type | solution.py:585
  2.7 1.3 %pad_add_fusion.ints = s32[49]{0:T(128)} fusion(s32[1]{0:T(128)S(6)} %copy.28, s32[8]{0:T(128)} %bitcast.38, s32[8]{0:T(128)} %bitcast.39, s32[32]{0:T(128)} %bitcast.40), kind=kLoop, calls=%fused_computation.75 | loop fusion | flops 147 | bytes 392 | tf_op jit(solution)/shard_map/concatenate | solution.py:586
  4.1 44.4 %exchange.1 = (bf16[16,144,256]{2,1,0:T(8,128)(2,1)}, bf16[16,256,16]{2,1,0:T(8,128)(2,1)}, bf16[32,144,256]{2,1,0:T(8,128)(2,1)}, bf16[128,32,256]{2,1,0:T(8,12...) custom-call(s32[49]{0:T(128)} %pad_add_fusion.ints, s32[2,128]{1,0:T(2,128)} %bitcast.36, s32[2,128]{1,0:T(2,128)} %bitcast.37, ...), custom_call_target="tpu_custom_call" | custom-call | tf_op jit(solution)/shard_map/exchange/pallas_call | solution.py:261
  48.5 11.1 %reply.1 = bf16[32,128,256]{2,1,0:T(8,128)(2,1)} custom-call(s32[3,512]{1,0:T(4,128)} %get-tuple-element.11.pairs, bf16[16,144,256]{2,1,0:T(8,128)(2,1)} %get-tuple-element.16.stage_in, bf16[16,256,16]{2,1,0:T(8,128)(2,1)} %get-tuple-element.13.fa_in, bf16[32,144,256]{2,1,0:T(8,128)(2,1)} %get-tuple-element.14.incoming_in), custom_call_target="tpu_custom_call" | custom-call | flops 6442450944 | bytes 8388608 | tf_op jit(solution)/shard_map/reply/pallas_call | solution.py:379
  59.7 0.0 copy-start.2
  59.7 0.0 copy-start.3
  59.7 9.0 %all-to-all-start = ((bf16[32,128,256]{2,1,0:T(8,128)(2,1)}), bf16[32,128,256]{2,1,0:T(8,128)(2,1)S(1)}, u32[]{:S(2)}, u32[]{:S(2)}) async-start(bf16[32,128,256]{2,1,0:T(8,128)(2,1)} %reply.1), calls=%async_computation | async-start | bytes 4194304 | tf_op jit(solution)/shard_map/all_to_all | solution.py:592
  68.8 0.0 copy-done.2
  68.8 0.7 constant_dynamic-slice_fusion.1
  69.6 0.1 fusion.16
  69.7 0.1 reshape.51
  69.9 0.1 mul.76
  70.0 0.1 mul.81
  70.0 0.1 copy.23
  70.1 0.2 broadcast_in_dim.3
  70.3 0.1 reshape.48
  70.4 0.6 pad.9.own_points
  71.1 0.0 copy-done.3
  71.2 0.7 pad_add_fusion.1.ids
  71.8 0.0 copy-start.1
  71.8 18.6 %rest.1.base = f32[16,128,256]{2,1,0:T(8,128)} custom-call(s32[3,512]{1,0:T(4,128)} %get-tuple-element.11.pairs, s32[57]{0:T(128)} %pad_add_fusion.1.ids, f32[3,32,128]{2,1,0:T(8,128)} %pad.9.own_points, bf16[16,32,32]{2,1,0:T(8,128)(2,1)} %trans.3, bf16[16,32,256]{2,1,0:T(8,128)(2,1)} %basis.3, bf16[16,256,16]{2,1,0:T(8,128)(2,1)} %get-tuple-element.13.fa_in, ...), custom_call_target="tpu_custom_call" | custom-call | flops 12884901888 | bytes 8388608 | tf_op jit(solution)/shard_map/rest/pallas_call | solution.py:503
  90.4 6.6 %all-to-all-done.returned = bf16[32,128,256]{2,1,0:T(8,128)(2,1)S(1)} async-done(((bf16[32,128,256]{2,1,0:T(8,128)(2,1)}), bf16[32,128,256]{2,1,0:T(8,128)(2,1)S(1)}, u32[]{:S(2)}, u32[]{:S(2)}) %all-to-all-start) | async-done | bytes 2097184 | tf_op jit(solution)/shard_map/all_to_all | solution.py:592
  97.0 0.0 copy-done.1
  97.0 0.0 copy-start
  97.0 1.6 %copy-done = f32[16,128,256]{2,1,0:T(8,128)S(1)} copy-done((f32[16,128,256]{2,1,0:T(8,128)S(1)}, f32[16,128,256]{2,1,0:T(8,128)}, u32[]{:S(2)}) %copy-start) | copy-done | bytes 2097176
  98.6 2.8 %finish.1 = f32[16,256,128]{2,1,0:T(8,128)} custom-call(s32[49]{0:T(128)S(1)} %copy-done.1, f32[16,128,256]{2,1,0:T(8,128)S(1)} %copy-done, bf16[32,128,256]{2,1,0:T(8,128)(2,1)S(1)} %all-to-all-done.returned), custom_call_target="tpu_custom_call" | custom-call | tf_op jit(solution)/shard_map/finish/pallas_call | solution.py:548
  (12 shorter events, 0.2 us)
Async XLA Ops:
  59.7 9.1 %copy-start.2 = (bf16[1,3,32]{2,1,0:T(4,128)(2,1)S(1)}, bf16[1,3,32]{2,1,0:T(4,128)(2,1)}, u32[]{:S(2)}) copy-start(bf16[1,3,32]{2,1,0:T(4,128)(2,1)} %param.20) | copy-start | bytes 580
  59.7 11.4 %copy-start.3 = (s32[1,8]{1,0:T(1,128)S(1)}, s32[1,8]{1,0:T(1,128)}, u32[]{:S(2)}) copy-start(s32[1,8]{1,0:T(1,128)} %param.25) | copy-start | bytes 100
  59.7 37.3 %all-to-all-start = ((bf16[32,128,256]{2,1,0:T(8,128)(2,1)}), bf16[32,128,256]{2,1,0:T(8,128)(2,1)S(1)}, u32[]{:S(2)}, u32[]{:S(2)}) async-start(bf16[32,128,256]{2,1,0:T(8,128)(2,1)} %reply.1), calls=%async_computation | async-start | bytes 4194304 | tf_op jit(solution)/shard_map/all_to_all | solution.py:592
  71.8 25.2 %copy-start.1 = (s32[49]{0:T(128)S(1)}, s32[49]{0:T(128)}, u32[]{:S(2)}) copy-start(s32[49]{0:T(128)} %pad_add_fusion.ints) | copy-start | bytes 592
  97.0 1.6 %copy-start = (f32[16,128,256]{2,1,0:T(8,128)S(1)}, f32[16,128,256]{2,1,0:T(8,128)}, u32[]{:S(2)}) copy-start(f32[16,128,256]{2,1,0:T(8,128)} %rest.1.base) | copy-start | bytes 6291460

commit v9 on v8

--- a/solution.py
+++ b/solution.py
@@ -27,7 +27,7 @@
     (2, 0, 0), (0, 1, 0), (0, 2, 1), (2, 1, 1), (2, 3, 1), (0, 3, 1), (1, 1, 0),
 )
 MESH = pl.DeviceIdType.MESH
-NARROW = pltpu.CompilerParams(vmem_limit_bytes=12 << 20)
+FINAL = pltpu.CompilerParams(vmem_limit_bytes=57 << 20)
 WIDE = pltpu.CompilerParams(vmem_limit_bytes=56 << 20)
 
 
@@ -108,7 +108,7 @@
 
 
 def exchange_kernel(
-    ints, first, second, charges, axes, basis, trans, pair, quad,
+    slots, pair_far, quad_far, count, first, second, points, charges, axes, basis, trans, pair, quad,
     stage, fa, incoming, nodes, lists, acc,
     rows_a, rows_b, outgoing, weights, kbuf, team_send, team_recv, node_send, node_recv, own_sem,
 ):
@@ -130,7 +130,7 @@
     for k in (1, 2, 3):
         pl.semaphore_signal(barrier, inc=1, device_id={"group": turn(z, k), "dev": d}, device_id_type=MESH)
 
-    point = [axes[i, :clusters] for i in range(3)]
+    point = [axes[i] for i in range(3)]
     norm = point[0] * point[0] + point[1] * point[1] + point[2] * point[2]
     one = jnp.ones_like(norm)
     rows_a[...] = jnp.zeros_like(rows_a)
@@ -147,7 +147,7 @@
     sent = []
 
     def send(i):
-        outgoing[i] = stage[ints[team[i]]]
+        outgoing[i] = stage[slots[team[i]]]
         copy = pltpu.make_async_remote_copy(
             src_ref=outgoing.at[i],
             dst_ref=incoming.at[d],
@@ -169,10 +169,10 @@
     mats = [mat[0].astype(F32) for mat in (pair, quad)]
     moves = jnp.concatenate([mat[8 * i : 8 * i + 8] for mat in mats for i in range(4)], axis=1)
     lane = lax.broadcasted_iota(jnp.int32, (1, width), 1)
-    points = [axes[i, clusters : clusters + 1] for i in range(3)]
-    info = points[0] + pltpu.roll(points[1], 32, 1) + pltpu.roll(points[2], 64, 1)
-    for i in range(16):
-        info = jnp.where(lane == rhs + i, ints[32 + i].astype(F32), info)
+    info = jnp.concatenate([points[i : i + 1] for i in range(3)] + [jnp.zeros((1, width - 96), F32)], axis=1)
+    for i in range(8):
+        info = jnp.where(lane == rhs + i, pair_far[i].astype(F32), info)
+        info = jnp.where(lane == rhs + 8 + i, quad_far[i].astype(F32), info)
     line = lax.broadcasted_iota(jnp.int32, (8, width), 0)
     info = jnp.where(line == 0, jnp.broadcast_to(info, (8, width)), 0.0)
     me = ((c * 4 + z) * 4 + y) * 4 + x
@@ -201,7 +201,7 @@
         send(i)
     for i in range(clusters):
         fa[i] = rows_a[i].T.astype(BF16)
-    pair_lists(*(jnp.concatenate([p[:1], p[1:]], axis=1) for p in (first, second)), ints[48], lists, weights)
+    pair_lists(*(jnp.concatenate([p[:1], p[1:]], axis=1) for p in (first, second)), count[0], lists, weights)
     for copy in plane:
         copy.wait_recv()
     start = (c * 4 + z) * 16
@@ -213,7 +213,7 @@
             peer = {"group": turn(z, k + 1), "dev": d}
             along_z.append(node_copy(start + part * 4, 4, 15 + len(along_z), peer))
             along_z[-1].start()
-    outgoing[31] = stage[ints[d]]
+    outgoing[31] = stage[slots[d]]
     own = pltpu.make_async_copy(outgoing.at[31], incoming.at[d], own_sem)
     own.start()
     chip = {"group": z, "dev": member(x, y, 1 - c)}
@@ -255,7 +255,7 @@
         copy.wait_send()
 
 
-def exchange(ints, first, second, charges, axes, basis, trans, pair, quad):
+def exchange(slots, pair_far, quad_far, count, first, second, points, charges, axes, basis, trans, pair, quad):
     clusters, width, rhs = charges.shape
     rows = rhs + FEAT
     return pl.pallas_call(
@@ -268,7 +268,7 @@
             jax.ShapeDtypeStruct((3, TAIL), jnp.int32),
             jax.ShapeDtypeStruct((clusters, rhs, width), F32),
         ),
-        in_specs=[SMEM] + [VMEM] * 8,
+        in_specs=[SMEM] * 4 + [VMEM] * 9,
         out_specs=(VMEM, VMEM, ANY, VMEM, VMEM, VMEM),
         scratch_shapes=[pltpu.VMEM((clusters, FEAT, width), F32)] * 2
         + [
@@ -285,7 +285,7 @@
             vmem_limit_bytes=56 << 20, collective_id=0, has_side_effects=True
         ),
         name="exchange",
-    )(ints, first, second, charges, axes, basis, trans, pair, quad)
+    )(slots, pair_far, quad_far, count, first, second, points, charges, axes, basis, trans, pair, quad)
 
 
 def unpack(code):
@@ -502,7 +502,7 @@
     width = acc.shape[2]
     return pl.pallas_call(
         rest_kernel,
-        out_shape=jax.ShapeDtypeStruct(acc.shape, F32),
+        out_shape=jax.ShapeDtypeStruct((4 * acc.shape[0], *acc.shape[1:]), F32),
         in_specs=[SMEM] * 2 + [VMEM] * 3 + [ANY] * 4,
         out_specs=ANY,
         scratch_shapes=[
@@ -521,42 +521,44 @@
     )(pairs, ids, own_points, trans, basis, fa, incoming, nodes, acc)
 
 
-def final_kernel(ints, base, returned, out, sums, rows, base_sem, outs):
+def final_kernel(ints, base_in, returned, out, base, sums, rows, base_sem, outs):
     clusters = base.shape[0]
-    load = pltpu.make_async_copy(base, sums, base_sem)
+    load = pltpu.make_async_copy(base_in.at[pl.ds(0, clusters)], base, base_sem)
     load.start()
+    sums[...] = jnp.zeros_like(sums)
+
+    def collect(h, carry):
+        sums[ints[h]] += returned[h].astype(F32)
+        return carry
+
+    lax.fori_loop(0, returned.shape[0], collect, 0)
     load.wait()
-
-    def collect(h, carry):
-        sums[ints[h]] += KCOEF * returned[h].astype(F32)
-        return carry
-
-    lax.fori_loop(0, returned.shape[0], collect, 0)
 
     def leave(c):
         return pltpu.make_async_copy(rows.at[c], out.at[c], outs.at[c])
 
     for c in range(clusters):
-        rows[c] = sums[c].T
+        rows[c] = (base[c] + KCOEF * sums[c]).T
         leave(c).start()
     for c in range(clusters):
         leave(c).wait()
 
 
 def finish(ints, base, returned):
-    clusters, rhs, width = base.shape
+    clusters, rhs, width = base.shape[0] // 4, *base.shape[1:]
     return pl.pallas_call(
         final_kernel,
         out_shape=jax.ShapeDtypeStruct((clusters, width, rhs), F32),
         in_specs=[SMEM, ANY, VMEM],
         out_specs=ANY,
         scratch_shapes=[
-            pltpu.VMEM(base.shape, F32),
+            pltpu.VMEM((clusters, rhs, width), F32),
+            pltpu.VMEM((clusters, rhs, width), F32),
             pltpu.VMEM((clusters, width, rhs), F32),
             pltpu.SemaphoreType.DMA,
             pltpu.SemaphoreType.DMA((clusters,)),
         ],
-        compiler_params=NARROW,
+        compiler_params=FINAL,
         name="finish",
     )(ints, base, returned)
 
@@ -581,12 +583,11 @@
     conductors = charges.shape[1]
     peers = lax.axis_size("dev")
     blocks = charges.reshape(clusters, width, conductors)
-    points = jnp.pad(skel_points[0][:, None, :], ((0, 0), (0, 0), (0, width - skel_points.shape[2])))
-    axes = jnp.concatenate([jnp.swapaxes(panel_coords, 0, 1), points], axis=1).astype(F32)
-    ints = jnp.concatenate([send_slots[:, 0], far_two[0], far_three[0], pair_count])
+    axes = jnp.swapaxes(panel_coords, 0, 1).astype(F32)
+    slots = send_slots.reshape(-1)
     stage, fa, incoming, nodes, lists, acc = exchange(
-        ints, pair_first.reshape(2, 128), pair_second.reshape(2, 128), blocks, axes,
-        cluster_basis, trans_leaf, trans_pair, trans_quad,
+        slots, far_two.reshape(-1), far_three.reshape(-1), pair_count, pair_first.reshape(2, 128),
+        pair_second.reshape(2, 128), skel_points[0].astype(F32), blocks, axes, cluster_basis, trans_leaf, trans_pair, trans_quad,
     )
     back = reply(lists, stage, fa, incoming)
     returned = lax.all_to_all(back, "dev", split_axis=0, concat_axis=0, tiled=True)
@@ -624,7 +625,7 @@
     own_points = jnp.repeat(jnp.swapaxes(own_points, 1, 2), 32, axis=2)
     own_points = jnp.pad(own_points, ((0, 0), (0, 0), (0, 32)))
     base = rest(lists, ids, own_points, trans_leaf, cluster_basis, fa, incoming, nodes, acc)
-    out = finish(ints, base, returned)
+    out = finish(slots, base, returned)
     return out.reshape(clusters * width, conductors)
 
 

time: 103 us -> 104 us (level)
  starting transfers between devices: 8.99 us -> 12.4 us
  Pallas kernels: 77 us -> 73.9 us
  waiting for transfers between devices: 6.58 us -> 9.44 us
    all_to_all x1, starting transfers between devices: 8.99 us -> 12.4 us  [shards(): lax.all_to_all(back, 'dev', split_axis=0, concat_axis=0, tiled=True)]
    all_to_all x1, waiting for transfers between devices: 6.58 us -> 9.44 us  [shards(): lax.all_to_all(back, 'dev', split_axis=0, concat_axis=0, tiled=True)]
    pallas_call x1, Pallas kernels: 18.6 us -> 15.8 us  [rest(): pl.pallas_call(rest_kernel, out_shape=jax.ShapeDtypeStruct((4 * acc.shape...]
    pallas_call x1, Pallas kernels: 11.1 us -> 8.76 us  [reply(): pl.pallas_call(reply_kernel, out_shape=out, in_specs=[SMEM] + [ANY] * 3,...]
    pallas_call x1, Pallas kernels: 2.82 us -> 4.74 us  [finish(): pl.pallas_call(final_kernel, out_shape=jax.ShapeDtypeStruct((clusters, wi...]
    concatenate x1 -> x0, other arithmetic: 1.34 us -> none  [shards(): jnp.concatenate([send_slots[:, 0], far_two[0], far_three[0], pair_count])]
    convert_element_type x1, other arithmetic: 0.01 us -> 1.22 us  [shards(): skel_points[0].astype(F32)]
  transfers between devices with their start and end apart: 1 -> 1, of which waited for: 1 -> 1; matrix products, arithmetic and copies ran while one was open for 3% -> 3% of each run, Pallas kernels for 18% -> 15%
where the time goes in v9:
time: 104 us; the launch traced here: 103 us
  Pallas kernels  73.9 us (71%)
  starting transfers between devices  12.4 us (12%)
  waiting for transfers between devices  9.44 us (9%)
  other arithmetic  3.42 us (3%)
  local copies, waits for them, and re-layouts  3.38 us (3%)
    pallas_call x1, Pallas kernels, exchange(): pl.pallas_call(exchange_kernel, out_shape=(jax.ShapeDtypeStruct((clusters...  44.6 us
    pallas_call x1, Pallas kernels, rest(): pl.pallas_call(rest_kernel, out_shape=jax.ShapeDtypeStruct((4 * acc.shape...  15.8 us
    all_to_all x1, starting transfers between devices, shards(): lax.all_to_all(back, 'dev', split_axis=0, concat_axis=0, tiled=True)  12.4 us
    all_to_all x1, waiting for transfers between devices, shards(): lax.all_to_all(back, 'dev', split_axis=0, concat_axis=0, tiled=True)  9.44 us
    pallas_call x1, Pallas kernels, reply(): pl.pallas_call(reply_kernel, out_shape=out, in_specs=[SMEM] + [ANY] * 3,...  8.76 us
    pallas_call x1, Pallas kernels, finish(): pl.pallas_call(final_kernel, out_shape=jax.ShapeDtypeStruct((clusters, wi...  4.74 us
  transfers between devices with their start and end apart: 1, of which 1 were waited for; matrix products, arithmetic and copies ran while one was open for 3% of the time, Pallas kernels for 15%

profile of v9, /device:TPU:1, one launch (start us, length us, event | category | flops | bytes accessed | tf_op | source)
XLA Modules:
  0.0 103.4 jit_solution(9621435829141527560)
XLA Ops:
  0.0 1.2 %fusion.14 = (f32[1,3,32]{2,1,0:T(4,128)S(1)}, f32[3,32]{1,0:T(4,128)}) fusion(bf16[1,3,32]{2,1,0:T(4,128)(2,1)} %param.20), kind=kLoop, calls=%fused_computation.79 | loop fusion | flops 96 | bytes 960 | tf_op jit(solution)/shard_map/convert_element_type | solution.py:590
  1.2 1.4 %convert_bitcast_fusion.axes = f32[3,16,256]{2,1,0:T(8,128)} fusion(bf16[16,3,256]{2,0,1:T(8,128)(2,1)} %param.15), kind=kLoop, calls=%fused_computation | loop fusion | flops 12288 | bytes 73728 | tf_op jit(solution)/shard_map/convert_element_type | solution.py:586
  3.2 44.6 %exchange.1 = (bf16[16,144,256]{2,1,0:T(8,128)(2,1)}, bf16[16,256,16]{2,1,0:T(8,128)(2,1)}, bf16[32,144,256]{2,1,0:T(8,128)(2,1)}, bf16[128,32,256]{2,1,0:T(8,12...) custom-call(s32[32]{0:T(128)} %bitcast.36, s32[8]{0:T(128)} %bitcast.40, s32[8]{0:T(128)} %bitcast.41, ...), custom_call_target="tpu_custom_call" | custom-call | tf_op jit(solution)/shard_map/exchange/pallas_call | solution.py:261
  47.9 8.8 %reply.1 = bf16[32,128,256]{2,1,0:T(8,128)(2,1)} custom-call(s32[3,512]{1,0:T(4,128)} %get-tuple-element.11.pairs, bf16[16,144,256]{2,1,0:T(8,128)(2,1)} %get-tuple-element.16.stage_in, bf16[16,256,16]{2,1,0:T(8,128)(2,1)} %get-tuple-element.13.fa_in, bf16[32,144,256]{2,1,0:T(8,128)(2,1)} %get-tuple-element.14.incoming_in), custom_call_target="tpu_custom_call" | custom-call | flops 6442450944 | bytes 8388608 | tf_op jit(solution)/shard_map/reply/pallas_call | solution.py:379
  56.6 0.0 copy-start.1
  56.6 12.4 %all-to-all-start = ((bf16[32,128,256]{2,1,0:T(8,128)(2,1)}), bf16[32,128,256]{2,1,0:T(8,128)(2,1)S(1)}, u32[]{:S(2)}, u32[]{:S(2)}) async-start(bf16[32,128,256]{2,1,0:T(8,128)(2,1)} %reply.1), calls=%async_computation | async-start | bytes 4194304 | tf_op jit(solution)/shard_map/all_to_all | solution.py:593
  69.1 0.7 constant_dynamic-slice_fusion.1
  69.9 0.1 reshape.66
  70.0 0.1 fusion.13
  70.2 0.1 copy.20
  70.3 0.2 broadcast_in_dim.3
  70.5 0.1 reshape.62
  70.6 0.1 mul.76
  70.7 0.1 mul.81
  70.8 0.6 pad.4.own_points
  71.4 0.0 copy-done.1
  71.5 0.6 pad_add_fusion.ids
  72.1 15.8 %rest.1.base_in = f32[64,128,256]{2,1,0:T(8,128)} custom-call(s32[3,512]{1,0:T(4,128)} %get-tuple-element.11.pairs, s32[57]{0:T(128)} %pad_add_fusion.ids, f32[3,32,128]{2,1,0:T(8,128)} %pad.4.own_points, bf16[16,32,32]{2,1,0:T(8,128)(2,1)} %trans.3, bf16[16,32,256]{2,1,0:T(8,128)(2,1)} %basis.3, bf16[16,256,16]{2,1,0:T(8,128)(2,1)} %get-tuple-element.13.fa_in, ...), custom_call_target="tpu_custom_call" | custom-call | flops 12884901888 | bytes 8388608 | tf_op jit(solution)/shard_map/rest/pallas_call | solution.py:503
  87.9 9.4 %all-to-all-done.returned = bf16[32,128,256]{2,1,0:T(8,128)(2,1)S(1)} async-done(((bf16[32,128,256]{2,1,0:T(8,128)(2,1)}), bf16[32,128,256]{2,1,0:T(8,128)(2,1)S(1)}, u32[]{:S(2)}, u32[]{:S(2)}) %all-to-all-start) | async-done | bytes 2097184 | tf_op jit(solution)/shard_map/all_to_all | solution.py:593
  97.3 0.0 copy-start
  97.3 1.4 %copy-done = bf16[32,128,256]{2,1,0:T(8,128)(2,1)} copy-done((bf16[32,128,256]{2,1,0:T(8,128)(2,1)}, bf16[32,128,256]{2,1,0:T(8,128)(2,1)S(1)}, u32[]{:S(2)}) %copy-start) | copy-done | bytes 2097176
  98.7 4.7 %finish.1 = f32[16,256,128]{2,1,0:T(8,128)} custom-call(s32[32]{0:T(128)} %bitcast.37, f32[64,128,256]{2,1,0:T(8,128)} %rest.1.base_in, bf16[32,128,256]{2,1,0:T(8,128)(2,1)} %copy-done), custom_call_target="tpu_custom_call" | custom-call | tf_op jit(solution)/shard_map/finish/pallas_call | solution.py:549
  (11 shorter events, 0.1 us)
Async XLA Ops:
  56.6 14.8 %copy-start.1 = (s32[1,8]{1,0:T(1,128)S(1)}, s32[1,8]{1,0:T(1,128)}, u32[]{:S(2)}) copy-start(s32[1,8]{1,0:T(1,128)} %param.25) | copy-start | bytes 100
  56.6 40.7 %all-to-all-start = ((bf16[32,128,256]{2,1,0:T(8,128)(2,1)}), bf16[32,128,256]{2,1,0:T(8,128)(2,1)S(1)}, u32[]{:S(2)}, u32[]{:S(2)}) async-start(bf16[32,128,256]{2,1,0:T(8,128)(2,1)} %reply.1), calls=%async_computation | async-start | bytes 4194304 | tf_op jit(solution)/shard_map/all_to_all | solution.py:593
  97.3 1.4 %copy-start = (bf16[32,128,256]{2,1,0:T(8,128)(2,1)}, bf16[32,128,256]{2,1,0:T(8,128)(2,1)S(1)}, u32[]{:S(2)}) copy-start(bf16[32,128,256]{2,1,0:T(8,128)(2,1)S(1)} %all-to-all-done.returned) | copy-start | bytes 6291460

commit v10 on v9

--- a/solution.py
+++ b/solution.py
@@ -27,7 +27,7 @@
     (2, 0, 0), (0, 1, 0), (0, 2, 1), (2, 1, 1), (2, 3, 1), (0, 3, 1), (1, 1, 0),
 )
 MESH = pl.DeviceIdType.MESH
-FINAL = pltpu.CompilerParams(vmem_limit_bytes=57 << 20)
+FINAL = pltpu.CompilerParams(vmem_limit_bytes=12 << 20)
 WIDE = pltpu.CompilerParams(vmem_limit_bytes=56 << 20)
 
 
@@ -502,7 +502,7 @@
     width = acc.shape[2]
     return pl.pallas_call(
         rest_kernel,
-        out_shape=jax.ShapeDtypeStruct((4 * acc.shape[0], *acc.shape[1:]), F32),
+        out_shape=jax.ShapeDtypeStruct(acc.shape, F32),
         in_specs=[SMEM] * 2 + [VMEM] * 3 + [ANY] * 4,
         out_specs=ANY,
         scratch_shapes=[
@@ -521,10 +521,8 @@
     )(pairs, ids, own_points, trans, basis, fa, incoming, nodes, acc)
 
 
-def final_kernel(ints, base_in, returned, out, base, sums, rows, base_sem, outs):
+def final_kernel(ints, base, returned, out, sums, rows, outs):
     clusters = base.shape[0]
-    load = pltpu.make_async_copy(base_in.at[pl.ds(0, clusters)], base, base_sem)
-    load.start()
     sums[...] = jnp.zeros_like(sums)
 
     def collect(h, carry):
@@ -532,7 +530,6 @@
         return carry
 
     lax.fori_loop(0, returned.shape[0], collect, 0)
-    load.wait()
 
     def leave(c):
         return pltpu.make_async_copy(rows.at[c], out.at[c], outs.at[c])
@@ -545,17 +542,15 @@
 
 
 def finish(ints, base, returned):
-    clusters, rhs, width = base.shape[0] // 4, *base.shape[1:]
+    clusters, rhs, width = base.shape
     return pl.pallas_call(
         final_kernel,
         out_shape=jax.ShapeDtypeStruct((clusters, width, rhs), F32),
-        in_specs=[SMEM, ANY, VMEM],
+        in_specs=[SMEM, VMEM, VMEM],
         out_specs=ANY,
         scratch_shapes=[
             pltpu.VMEM((clusters, rhs, width), F32),
-            pltpu.VMEM((clusters, rhs, width), F32),
             pltpu.VMEM((clusters, width, rhs), F32),
-            pltpu.SemaphoreType.DMA,
             pltpu.SemaphoreType.DMA((clusters,)),
         ],
         compiler_params=FINAL,

time: 104 us -> 103 us (level); the launches traced: 103 us -> 101 us
  Pallas kernels: 73.9 us -> 86.1 us
  waiting for transfers between devices: 9.44 us -> 1.59 us
  starting transfers between devices: 12.4 us -> 5.16 us
    all_to_all x1, waiting for transfers between devices: 9.44 us -> 1.59 us  [shards(): lax.all_to_all(back, 'dev', split_axis=0, concat_axis=0, tiled=True)]
    pallas_call x1, Pallas kernels: 15.8 us -> 23.6 us  [rest(): pl.pallas_call(rest_kernel, out_shape=jax.ShapeDtypeStruct(acc.shape, F32...]
    all_to_all x1, starting transfers between devices: 12.4 us -> 5.16 us  [shards(): lax.all_to_all(back, 'dev', split_axis=0, concat_axis=0, tiled=True)]
    pallas_call x1, Pallas kernels: 8.76 us -> 15.4 us  [reply(): pl.pallas_call(reply_kernel, out_shape=out, in_specs=[SMEM] + [ANY] * 3,...]
    pallas_call x1, Pallas kernels: 4.74 us -> 2.69 us  [finish(): pl.pallas_call(final_kernel, out_shape=jax.ShapeDtypeStruct((clusters, wi...]
  transfers between devices with their start and end apart: 1 -> 1, of which waited for: 1 -> 1; matrix products, arithmetic and copies ran while one was open for 3% -> 3% of each run, Pallas kernels for 15% -> 23%
where the time goes in v10:
time: 103 us; the launch traced here: 101 us
  Pallas kernels  86.1 us (84%)
  starting transfers between devices  5.16 us (5%)
  local copies, waits for them, and re-layouts  3.61 us (4%)
  other arithmetic  3.5 us (3%)
  waiting for transfers between devices  1.59 us (2%)
    pallas_call x1, Pallas kernels, exchange(): pl.pallas_call(exchange_kernel, out_shape=(jax.ShapeDtypeStruct((clusters...  44.4 us
    pallas_call x1, Pallas kernels, rest(): pl.pallas_call(rest_kernel, out_shape=jax.ShapeDtypeStruct(acc.shape, F32...  23.6 us
    pallas_call x1, Pallas kernels, reply(): pl.pallas_call(reply_kernel, out_shape=out, in_specs=[SMEM] + [ANY] * 3,...  15.4 us
    all_to_all x1, starting transfers between devices, shards(): lax.all_to_all(back, 'dev', split_axis=0, concat_axis=0, tiled=True)  5.16 us
    pallas_call x1, Pallas kernels, finish(): pl.pallas_call(final_kernel, out_shape=jax.ShapeDtypeStruct((clusters, wi...  2.69 us
  transfers between devices with their start and end apart: 1, of which 1 were waited for; matrix products, arithmetic and copies ran while one was open for 3% of the time, Pallas kernels for 23%

profile of v10, /device:TPU:1, one launch (start us, length us, event | category | flops | bytes accessed | tf_op | source)
XLA Modules:
  0.0 100.9 jit_solution(11802116113175433471)
XLA Ops:
  0.7 1.3 %fusion.14 = (f32[1,3,32]{2,1,0:T(4,128)S(1)}, f32[3,32]{1,0:T(4,128)}) fusion(bf16[1,3,32]{2,1,0:T(4,128)(2,1)} %param.20), kind=kLoop, calls=%fused_computation.79 | loop fusion | flops 96 | bytes 960 | tf_op jit(solution)/shard_map/convert_element_type | solution.py:585
  1.9 1.4 %convert_bitcast_fusion.axes = f32[3,16,256]{2,1,0:T(8,128)} fusion(bf16[16,3,256]{2,0,1:T(8,128)(2,1)} %param.15), kind=kLoop, calls=%fused_computation | loop fusion | flops 12288 | bytes 73728 | tf_op jit(solution)/shard_map/convert_element_type | solution.py:581
  3.3 44.4 %exchange.1 = (bf16[16,144,256]{2,1,0:T(8,128)(2,1)}, bf16[16,256,16]{2,1,0:T(8,128)(2,1)}, bf16[32,144,256]{2,1,0:T(8,128)(2,1)}, bf16[128,32,256]{2,1,0:T(8,12...) custom-call(s32[32]{0:T(128)} %bitcast.34, s32[8]{0:T(128)} %bitcast.40, s32[8]{0:T(128)} %bitcast.41, ...), custom_call_target="tpu_custom_call" | custom-call | tf_op jit(solution)/shard_map/exchange/pallas_call | solution.py:261
  47.7 15.4 %reply.1 = bf16[32,128,256]{2,1,0:T(8,128)(2,1)} custom-call(s32[3,512]{1,0:T(4,128)} %get-tuple-element.11.pairs, bf16[16,144,256]{2,1,0:T(8,128)(2,1)} %get-tuple-element.16.stage_in, bf16[16,256,16]{2,1,0:T(8,128)(2,1)} %get-tuple-element.13.fa_in, bf16[32,144,256]{2,1,0:T(8,128)(2,1)} %get-tuple-element.14.incoming_in), custom_call_target="tpu_custom_call" | custom-call | flops 6442450944 | bytes 8388608 | tf_op jit(solution)/shard_map/reply/pallas_call | solution.py:379
  63.1 0.0 copy-start.2
  63.1 5.2 %all-to-all-start = ((bf16[32,128,256]{2,1,0:T(8,128)(2,1)}), bf16[32,128,256]{2,1,0:T(8,128)(2,1)S(1)}, u32[]{:S(2)}, u32[]{:S(2)}) async-start(bf16[32,128,256]{2,1,0:T(8,128)(2,1)} %reply.1), calls=%async_computation | async-start | bytes 4194304 | tf_op jit(solution)/shard_map/all_to_all | solution.py:588
  68.4 0.7 constant_dynamic-slice_fusion.1
  69.2 0.1 fusion.13
  69.3 0.1 reshape.66
  69.5 0.1 mul.76
  69.5 0.1 mul.81
  69.6 0.1 copy.20
  69.7 0.2 broadcast_in_dim.3
  69.9 0.1 reshape.62
  70.0 0.6 pad.4.own_points
  70.7 0.0 copy-done.2
  70.7 0.7 pad_add_fusion.ids
  71.4 0.0 copy-start.1
  71.4 23.6 %rest.1.base = f32[16,128,256]{2,1,0:T(8,128)} custom-call(s32[3,512]{1,0:T(4,128)} %get-tuple-element.11.pairs, s32[57]{0:T(128)} %pad_add_fusion.ids, f32[3,32,128]{2,1,0:T(8,128)} %pad.4.own_points, bf16[16,32,32]{2,1,0:T(8,128)(2,1)} %trans.3, bf16[16,32,256]{2,1,0:T(8,128)(2,1)} %basis.3, bf16[16,256,16]{2,1,0:T(8,128)(2,1)} %get-tuple-element.13.fa_in, ...), custom_call_target="tpu_custom_call" | custom-call | flops 12884901888 | bytes 8388608 | tf_op jit(solution)/shard_map/rest/pallas_call | solution.py:503
  95.0 1.6 %all-to-all-done.returned = bf16[32,128,256]{2,1,0:T(8,128)(2,1)S(1)} async-done(((bf16[32,128,256]{2,1,0:T(8,128)(2,1)}), bf16[32,128,256]{2,1,0:T(8,128)(2,1)S(1)}, u32[]{:S(2)}, u32[]{:S(2)}) %all-to-all-start) | async-done | bytes 2097184 | tf_op jit(solution)/shard_map/all_to_all | solution.py:588
  96.6 0.0 copy-done.1
  96.6 0.0 copy-start
  96.6 1.6 %copy-done = f32[16,128,256]{2,1,0:T(8,128)S(1)} copy-done((f32[16,128,256]{2,1,0:T(8,128)S(1)}, f32[16,128,256]{2,1,0:T(8,128)}, u32[]{:S(2)}) %copy-start) | copy-done | bytes 2097176
  98.2 2.7 %finish.1 = f32[16,256,128]{2,1,0:T(8,128)} custom-call(s32[32]{0:T(128)S(1)} %bitcast.35, f32[16,128,256]{2,1,0:T(8,128)S(1)} %copy-done, bf16[32,128,256]{2,1,0:T(8,128)(2,1)S(1)} %all-to-all-done.returned), custom_call_target="tpu_custom_call" | custom-call | tf_op jit(solution)/shard_map/finish/pallas_call | solution.py:546
  (11 shorter events, 0.2 us)
Async XLA Ops:
  63.1 7.5 %copy-start.2 = (s32[1,8]{1,0:T(1,128)S(1)}, s32[1,8]{1,0:T(1,128)}, u32[]{:S(2)}) copy-start(s32[1,8]{1,0:T(1,128)} %param.25) | copy-start | bytes 100
  63.1 33.5 %all-to-all-start = ((bf16[32,128,256]{2,1,0:T(8,128)(2,1)}), bf16[32,128,256]{2,1,0:T(8,128)(2,1)S(1)}, u32[]{:S(2)}, u32[]{:S(2)}) async-start(bf16[32,128,256]{2,1,0:T(8,128)(2,1)} %reply.1), calls=%async_computation | async-start | bytes 4194304 | tf_op jit(solution)/shard_map/all_to_all | solution.py:588
  71.4 25.2 %copy-start.1 = (s32[32,1]{0,1:T(1,128)S(1)}, s32[32,1]{0,1:T(1,128)}, u32[]{:S(2)}) copy-start(s32[32,1]{0,1:T(1,128)} %param.21) | copy-start | bytes 388
  96.6 1.6 %copy-start = (f32[16,128,256]{2,1,0:T(8,128)S(1)}, f32[16,128,256]{2,1,0:T(8,128)}, u32[]{:S(2)}) copy-start(f32[16,128,256]{2,1,0:T(8,128)} %rest.1.base) | copy-start | bytes 6291460
